TPU v7x, 512 devices: a whole 4x4x16 slice. The times are simulated.
512 devices in a mesh: ex: 32 (over z, core), hid: 16 (over y, x).
Axes of the slice: x: 4, y: 4, z: 16, core: 2. Of those that a mesh axis runs over, the one named last changes fastest.
Arguments:
- tokens: bfloat16 [8192, 2048], P(('ex', 'hid')), may hold values from -6 to 6
- cotangent: bfloat16 [8192, 2048], P(('ex', 'hid')), may hold values from -6 to 6
- gates: float32 [8192, 4], P(('ex', 'hid')), may hold values from 0.1 to 1
- routes: int32 [8192, 4], P(('ex', 'hid')), may hold values from 0 to 63, all different within a row; in each aligned block of 16 rows (0 to 15, 16 to 31, ...) at most 2 rows name the same one
- w_gate: bfloat16 [512, 176, 2048], P(('ex', 'hid')), may hold values from -0.125 to 0.125
- w_up: bfloat16 [512, 176, 2048], P(('ex', 'hid')), may hold values from -0.125 to 0.125
- w_down: bfloat16 [512, 176, 2048], P(('ex', 'hid')), may hold values from -0.15625 to 0.15625
Outputs:
- grad_tokens: bfloat16 [8192, 2048], P(('ex', 'hid'))
Inputs may be any that keep to these rules, and one draw needn't show every extreme that they name: `routes`: among the 16 tokens of one device (aligned blocks of rows) no expert is named more than 2 times, a bound that some block reaches; a token's 4 experts differ.
All inputs are finite; a program needn't handle non-finite values.
Results may differ from a plain program's by a relative error of at most 0.007.
Values may be sent and summed in bfloat16 or wider, within the bound.
No kernel may reach another device: no remote copies, remote signals or barrier semaphores. Data moves between devices by JAX's collectives and lax.ppermute only.
A program may use at most 64 MiB of HBM per device.

v0:
```python
import jax
import jax.numpy as jnp
from jax import lax
from jax.sharding import PartitionSpec as P

EXP_DEV = 2


def hidden_grad(inputs, cotan, wgate, wup, wdown):
    dims = (((1,), (1,)), ((), ()))
    gate = lax.dot_general(inputs, wgate, dims, preferred_element_type=jnp.float32)
    upper = lax.dot_general(inputs, wup, dims, preferred_element_type=jnp.float32)
    hidden = lax.dot_general(cotan, wdown, dims, preferred_element_type=jnp.float32)
    sig = jax.nn.sigmoid(gate)
    d_up = (hidden * gate * sig).astype(jnp.bfloat16)
    d_gate = (hidden * upper * sig * (1.0 + gate * (1.0 - sig))).astype(jnp.bfloat16)
    first = jnp.dot(d_gate, wgate, preferred_element_type=jnp.float32)
    second = jnp.dot(d_up, wup, preferred_element_type=jnp.float32)
    return first + second


def per_device(tokens, cotangent, gates, routes, w_gate, w_up, w_down):
    n_ex = lax.axis_size("ex")
    n_hid = lax.axis_size("hid")
    tok_dev, width = tokens.shape
    top = routes.shape[1]
    experts_all = EXP_DEV * n_ex
    blocks = n_hid // EXP_DEV
    slot_cap = max(2, (2 * tok_dev * top + experts_all - 1) // experts_all)
    flat = routes.reshape(-1)
    count = flat.shape[0]
    order = jnp.arange(count, dtype=jnp.int32)
    same = flat[:, None] == flat[None, :]
    earlier = order[None, :] < order[:, None]
    slot = jnp.sum(jnp.where(same & earlier, 1, 0), axis=1).astype(jnp.int32)
    owner_ex = flat // EXP_DEV
    local = flat % EXP_DEV
    rows_x = jnp.repeat(tokens, top, axis=0)
    rows_dy = jnp.repeat(cotangent, top, axis=0).astype(jnp.float32)
    scaled = (gates.reshape(-1)[:, None] * rows_dy).astype(jnp.bfloat16)
    stacked = jnp.stack([rows_x, scaled], axis=1)
    buffer = (
        jnp.zeros((EXP_DEV, 2, n_ex, slot_cap, width), jnp.bfloat16)
        .at[local, :, owner_ex, slot]
        .set(stacked)
    )
    arrived = lax.all_to_all(buffer, "ex", split_axis=2, concat_axis=2, tiled=True)
    tail = arrived.shape[1:]
    received = lax.all_to_all(
        jnp.broadcast_to(arrived[:, None], (EXP_DEV, blocks) + tail).reshape((n_hid,) + tail),
        "hid",
        split_axis=0,
        concat_axis=0,
        tiled=True,
    )
    rows = n_hid * n_ex * slot_cap
    inputs = received[:, 0].reshape(rows, width)
    cotan = received[:, 1].reshape(rows, width)
    partial_value = hidden_grad(inputs, cotan, w_gate[0], w_up[0], w_down[0]).astype(jnp.bfloat16)
    partial_value = partial_value.reshape(n_hid, n_ex, slot_cap, width)
    moved = lax.all_to_all(partial_value, "ex", split_axis=1, concat_axis=1, tiled=True)
    landed = lax.all_to_all(moved, "hid", split_axis=0, concat_axis=0, tiled=True)
    back = jnp.sum(
        landed.astype(jnp.float32).reshape(EXP_DEV, blocks, n_ex, slot_cap, width), axis=1
    ).astype(jnp.bfloat16)
    index = (local * n_ex + owner_ex) * slot_cap + slot
    picked = back.reshape(-1, width)[index].reshape(tok_dev, top, width).astype(jnp.float32)
    return jnp.sum(picked, axis=1).astype(jnp.bfloat16)


def solution(mesh):
    in_specs = (
        P(("ex", "hid"), None),
        P(("ex", "hid"), None),
        P(("ex", "hid"), None),
        P(("ex", "hid"), None),
        P(("ex", "hid"), None, None),
        P(("ex", "hid"), None, None),
        P(("ex", "hid"), None, None),
    )
    out_specs = P(("ex", "hid"), None)
    return jax.shard_map(
        per_device, mesh=mesh, in_specs=in_specs, out_specs=out_specs, check_vma=False
    )
```

profile of v0, /device:TPU:1, one launch (start us, length us, event | category | flops | bytes accessed | tf_op | source)
XLA Modules:
  0.0 526.2 jit_solution(9818134712290660868)
XLA Ops:
  0.0 0.8 copy.34
  1.2 0.9 broadcast_in_dim.33
  3.2 0.9 broadcast_in_dim.32
  5.0 1.0 broadcast_in_dim.16
  6.0 3.7 scatter_fusion
  9.7 1.0 copy.38
  10.7 72.3 %all_to_all.20 = bf16[2,2,32,2,2048]{4,1,3,0,2:T(2,128)(2,1)S(1)} all-to-all(bf16[2,2,32,2,2048]{4,1,3,0,2:T(2,128)(2,1)S(1)} %copy.38), channel_id=1, replica_groups=mesh['ex'=32,'hid'=16] {'ex'}, dimensions={2} | all-to-all | bytes 2097152 | tf_op jit(solution)/shard_map/all_to_all | solution.py:47
  83.8 5.8 %broadcast_in_dim.34 = bf16[2,8,2,32,2,2048]{5,4,3,2,1,0:T(2,128)(2,1)S(1)} broadcast(bf16[2,2,32,2,2048]{4,3,2,1,0:T(2,128)(2,1)S(1)} %copy.39), dimensions={0,2,3,4,5} | broadcast | bytes 9437184 | tf_op jit(solution)/shard_map/broadcast_in_dim | solution.py:50
  89.6 101.4 %all_to_all.21 = bf16[16,2,32,2,2048]{4,3,2,1,0:T(2,128)(2,1)S(1)} all-to-all(bf16[16,2,32,2,2048]{4,3,2,1,0:T(2,128)(2,1)S(1)} %bitcast.31), channel_id=1, replica_groups=mesh['ex'=32,'hid'=16] {'hid'}, dimensions={0} | all-to-all | bytes 16777216 | tf_op jit(solution)/shard_map/all_to_all | solution.py:49
  191.0 7.2 %fusion.24 = (bf16[16,1,32,2,2048]{4,3,2,1,0:T(2,128)(2,1)}, bf16[16,1,32,2,2048]{4,3,2,1,0:T(2,128)(2,1)}) fusion(bf16[16,2,32,2,2048]{4,3,2,1,0:T(2,128)(2,1)S(1)} %all_to_all.21), kind=kLoop, calls=%fused_computation.49 | loop fusion | bytes 16777216 | tf_op jit(solution)/shard_map/slice | solution.py:57
  198.2 7.2 %reshape_squeeze.7 = bf16[1024,2048]{1,0:T(8,128)(2,1)} reshape(bf16[16,1,32,2,2048]{4,3,2,1,0:T(2,128)(2,1)} %get-tuple-element.8) | data formatting | bytes 8388608 | tf_op jit(solution)/shard_map/reshape;squeeze | solution.py:57
  205.4 7.3 %reshape_squeeze.6 = bf16[1024,2048]{1,0:T(8,128)(2,1)} reshape(bf16[16,1,32,2,2048]{4,3,2,1,0:T(2,128)(2,1)} %get-tuple-element.9) | data formatting | bytes 8388608 | tf_op jit(solution)/shard_map/reshape;squeeze | solution.py:58
  212.7 3.9 fusion.5
  216.6 1.5 fusion.10
  218.2 8.2 %fusion.3 = f32[1024,2048]{1,0:T(8,128)} fusion(f32[1024,176]{0,1:T(8,128)S(1)} %fusion.10, bf16[1024,2048]{1,0:T(8,128)(2,1)} %reshape_squeeze.7, bf16[1,176,2048]{2,1,0:T(8,128)(2,1)S(1)} %copy-done.2, bf16[1,176,2048]{2,1,0:T(8,128)(2,1)S(1)} %copy-done, f32[1024,176]{0,1:T(8,128)S(1)} %fusion.5), kind=kOutput, calls=%fused_computation.8 | convolution fusion | flops 1478197248 | bytes 15466496 | tf_op jit(solution)/shard_map/dot_general | solution.py:17
  226.4 6.7 %add_convert_fusion = bf16[1024,2048]{1,0:T(8,128)(2,1)} fusion(f32[1024,2048]{1,0:T(8,128)} %fusion.3, bf16[1,176,2048]{2,1,0:T(8,128)(2,1)S(1)} %copy-done, f32[1024,176]{0,1:T(8,128)S(1)} %fusion.10, f32[1024,176]{0,1:T(8,128)S(1)} %fusion.5), kind=kOutput, calls=%fused_computation.2 | convolution fusion | flops 743473152 | bytes 14745600 | tf_op jit(solution)/shard_map/dot_general | solution.py:18
  233.0 7.6 %reshape.247 = bf16[16,32,2,2048]{3,2,1,0:T(2,128)(2,1)} reshape(bf16[1024,2048]{1,0:T(8,128)(2,1)} %add_convert_fusion) | data formatting | bytes 8388608 | tf_op jit(solution)/shard_map/reshape | solution.py:60
  240.7 6.7 %copy.40 = bf16[16,32,2,2048]{3,2,0,1:T(2,128)(2,1)S(1)} copy(bf16[16,32,2,2048]{3,2,1,0:T(2,128)(2,1)} %reshape.247) | data formatting | bytes 8388608 | tf_op jit(solution)/shard_map/reshape | solution.py:60
  247.4 195.9 %all_to_all.22 = bf16[16,32,2,2048]{3,2,0,1:T(2,128)(2,1)} all-to-all(bf16[16,32,2,2048]{3,2,0,1:T(2,128)(2,1)S(1)} %copy.40), channel_id=1, replica_groups=mesh['ex'=32,'hid'=16] {'ex'}, dimensions={1} | all-to-all | bytes 8388608 | tf_op jit(solution)/shard_map/all_to_all | solution.py:61
  443.3 8.0 %copy.41 = bf16[16,32,2,2048]{3,2,1,0:T(2,128)(2,1)} copy(bf16[16,32,2,2048]{3,2,0,1:T(2,128)(2,1)} %all_to_all.22) | data formatting | bytes 8388608 | tf_op jit(solution)/shard_map/all_to_all | solution.py:61
  451.3 4.5 all-to-all-start.3
  455.8 62.0 %all-to-all-done.3 = bf16[16,32,2,2048]{3,2,1,0:T(2,128)(2,1)} async-done(((bf16[16,32,2,2048]{3,2,1,0:T(2,128)(2,1)}), bf16[16,32,2,2048]{3,2,1,0:T(2,128)(2,1)}, u32[]{:S(2)}, u32[]{:S(2)}) %all-to-all-start.3) | async-done | bytes 4194336 | tf_op jit(solution)/shard_map/all_to_all | solution.py:62
  517.8 6.3 %bitcast_reduce_fusion = bf16[2,32,2,2048]{3,2,1,0:T(2,128)(2,1)S(1)} fusion(bf16[16,32,2,2048]{3,2,1,0:T(2,128)(2,1)} %all-to-all-done.3), kind=kLoop, calls=%fused_computation.3 | loop fusion | flops 1835008 | bytes 4718592 | tf_op jit(solution)/shard_map/reduce_sum | solution.py:63
  525.2 0.9 reduce_sum.35
  (25 shorter events, 4.0 us)
Async XLA Ops:
  0.0 218.2 %copy-start = (bf16[1,176,2048]{2,1,0:T(8,128)(2,1)S(1)}, bf16[1,176,2048]{2,1,0:T(8,128)(2,1)}, u32[]{:S(2)}) copy-start(bf16[1,176,2048]{2,1,0:T(8,128)(2,1)} %param.12) | copy-start | bytes 2162692
  205.4 7.3 %copy-start.2 = (bf16[1,176,2048]{2,1,0:T(8,128)(2,1)S(1)}, bf16[1,176,2048]{2,1,0:T(8,128)(2,1)}, u32[]{:S(2)}) copy-start(bf16[1,176,2048]{2,1,0:T(8,128)(2,1)} %param.11) | copy-start | bytes 2162692
  212.7 3.9 copy-start.1
  212.7 3.9 copy-start.3
  451.3 66.6 %all-to-all-start.3 = ((bf16[16,32,2,2048]{3,2,1,0:T(2,128)(2,1)}), bf16[16,32,2,2048]{3,2,1,0:T(2,128)(2,1)}, u32[]{:S(2)}, u32[]{:S(2)}) async-start(bf16[16,32,2,2048]{3,2,1,0:T(2,128)(2,1)} %copy.41), calls=%async_computation.3 | async-start | bytes 8388608 | tf_op jit(solution)/shard_map/all_to_all | solution.py:62
where the time goes:
time: 527 us; the launch traced here: 526 us
  blocking collectives  370 us (70%)
  waiting for transfers between devices  62 us (12%)
  local copies, waits for them, and re-layouts  61.9 us (12%)
  matrix products  20.3 us (4%)
  other arithmetic  7.64 us (1%)
    all_to_all x1, blocking collectives, per_device(): lax.all_to_all(partial_value, 'ex', split_axis=1, concat_axis=1, tiled=True)  196 us
    all_to_all x1, blocking collectives, per_device(): lax.all_to_all(jnp.broadcast_to(arrived[:, None], (EXP_DEV, blocks) + tai...  101 us
    all_to_all x1, blocking collectives, per_device(): lax.all_to_all(buffer, 'ex', split_axis=2, concat_axis=2, tiled=True)  72.3 us
    all_to_all x1, waiting for transfers between devices, per_device(): lax.all_to_all(moved, 'hid', split_axis=0, concat_axis=0, tiled=True)  62 us
    reshape x2, local copies, waits for them, and re-layouts, per_device(): partial_value = partial_value.reshape(n_hid, n_ex, slot_cap, width)  14.3 us
  transfers between devices with their start and end apart: 1, of which 1 were waited for; matrix products, arithmetic and copies ran while one was open for 0% of the time, Pallas kernels for 0%

commit v1 on v0

v1 whole, which is shorter than its diff:
```python
import functools

import jax
import jax.numpy as jnp
from jax import lax
from jax.experimental import pallas as pl
from jax.experimental.pallas import tpu as pltpu
from jax.sharding import PartitionSpec as P

BF = jnp.bfloat16
F32 = jnp.float32
COLS = 4


def _iota(shape, axis):
    return lax.broadcasted_iota(jnp.int32, shape, axis)


def _select(cond):
    return jnp.where(cond, 1.0, 0.0).astype(F32)


def _named(routes, expert):
    tok, top = routes.shape
    each = [_select(routes[:, k : k + 1] == expert) for k in range(top)]
    named = functools.reduce(lambda a, b: a + b, each)
    earlier = _select(_iota((tok, tok), 1) < _iota((tok, tok), 0)).astype(BF)
    slot = jnp.dot(earlier, named.astype(BF), preferred_element_type=F32)
    return each, named, slot


def pack_kernel(tok_ref, cot_ref, gate_ref, route_ref, out_ref):
    g = lax.axis_index("hid") // 8
    tok, width = tok_ref.shape
    top = route_ref.shape[1]
    rows = out_ref.shape[0]
    r = _iota((tok, rows), 1)
    expert = 2 * (r // 8) + jnp.bitwise_xor((r // 4) % 2, g)
    each, named, slot = _named(route_ref[...], expert)
    hit = _select(slot == (r % 2).astype(F32))
    is_x = _select((r // 2) % 2 == 0)
    cot = cot_ref[...].astype(F32)
    parts = [tok_ref[...]]
    picks = [(named * hit * is_x).astype(BF)]
    for k in range(top):
        parts.append((gate_ref[:, k : k + 1] * cot).astype(BF))
        picks.append((each[k] * hit * (1.0 - is_x)).astype(BF))
    data = jnp.concatenate(parts, axis=0)
    pick = jnp.concatenate(picks, axis=0)
    out_ref[...] = lax.dot_general(
        pick, data, (((0,), (0,)), ((), ())), preferred_element_type=F32
    ).astype(BF)


def unpack_kernel(in_ref, own_ref, other_ref):
    rows = own_ref.shape[0]
    half = rows // 2
    q = _iota((rows, in_ref.shape[0]), 0)
    r = _iota((rows, in_ref.shape[0]), 1)
    want = ((q % half) // 2) * 8 + (q // half) * 2 + q % 2
    data = in_ref[...]
    for o, ref in enumerate((own_ref, other_ref)):
        pick = _select(r == want + 4 * o).astype(BF)
        ref[...] = jnp.dot(pick, data, preferred_element_type=F32).astype(BF)


def grad_kernel(*refs):
    n = 4
    rows_in, w_in, outs = refs[:n], refs[n : 2 * n], refs[2 * n : 3 * n]
    x, y, wg, wu, wd, gate, upper, hidden, sem_r, sem_w = refs[3 * n :]
    half = rows_in[0].shape[0] // 2
    unit = w_in[0].shape[0] // 3
    width = x.shape[1]
    step = width // COLS
    row_copies = []
    for i in range(n):
        for m, dst in enumerate((x, y)):
            cp = pltpu.make_async_copy(
                rows_in[i].at[pl.ds(m * half, half)], dst.at[pl.ds(i * half, half)], sem_r.at[2 * i + m]
            )
            cp.start()
            row_copies.append(cp)
    w_copies = []
    for c in range(COLS):
        mine = []
        for m, dst in enumerate((wg, wu, wd)):
            for i in range(n):
                cp = pltpu.make_async_copy(
                    w_in[i].at[pl.ds(m * unit, unit), pl.ds(c * step, step)],
                    dst.at[pl.ds(i * unit, unit), pl.ds(c * step, step)],
                    sem_w.at[(c * 3 + m) * n + i],
                )
                cp.start()
                mine.append(cp)
        w_copies.append(mine)
    for cp in row_copies:
        cp.wait()
    dims = (((1,), (1,)), ((), ()))
    for c in range(COLS):
        for cp in w_copies[c]:
            cp.wait()
        at = slice(c * step, (c + 1) * step)
        for acc, left, right in ((gate, x, wg), (upper, x, wu), (hidden, y, wd)):
            part = lax.dot_general(left[:, at], right[:, at], dims, preferred_element_type=F32)
            if c == 0:
                acc[...] = part
            else:
                acc[...] += part
    gv, uv, hv = gate[...], upper[...], hidden[...]
    sig = jax.nn.sigmoid(gv)
    d_up = (hv * gv * sig).astype(BF)
    d_gate = (hv * uv * sig * (1.0 + gv * (1.0 - sig))).astype(BF)
    for c in range(COLS):
        at = slice(c * step, (c + 1) * step)
        res = jnp.dot(d_gate, wg[:, at], preferred_element_type=F32) + jnp.dot(
            d_up, wu[:, at], preferred_element_type=F32
        )
        for i in range(n):
            outs[i][:, at] = res[i * half : (i + 1) * half].astype(BF)


def merge_kernel(a_ref, b_ref, c_ref, d_ref, out_ref):
    rows = a_ref.shape[0]
    width = out_ref.shape[1]
    own = (a_ref[...].astype(F32) + b_ref[...].astype(F32)).astype(BF)
    other = (c_ref[...].astype(F32) + d_ref[...].astype(F32)).astype(BF)
    data = jnp.concatenate([own[:, :width], own[:, width:], other[:, :width], other[:, width:]], axis=0)
    r = _iota((out_ref.shape[0], 4 * rows), 0)
    q = _iota((out_ref.shape[0], 4 * rows), 1)
    want = ((r // 2) % 2) * 2 * rows + ((r // 4) % 2) * rows + (r // 8) * 2 + r % 2
    out_ref[...] = jnp.dot(
        _select(q == want).astype(BF), data, preferred_element_type=F32
    ).astype(BF)


def final_kernel(in_ref, route_ref, out_ref):
    g = lax.axis_index("hid") // 8
    tok = out_ref.shape[0]
    rows, width = in_ref.shape
    r = _iota((tok, rows), 1)
    expert = 2 * (r // 8) + jnp.bitwise_xor((r // 2) % 2, g)
    _, named, slot = _named(route_ref[...], expert)
    pick = named * _select(slot == (r % 2).astype(F32))
    data = in_ref[...]
    for h in range(2):
        mine = (pick * _select((r // 4) % 2 == h)).astype(BF)
        out_ref[:, h * width : (h + 1) * width] = jnp.dot(
            mine, data, preferred_element_type=F32
        ).astype(BF)


def _shape(*dims):
    return jax.ShapeDtypeStruct(dims, BF)


def _call(kernel, out_shape, name, cost, **kw):
    return pl.pallas_call(
        kernel,
        out_shape=out_shape,
        name=name,
        cost_estimate=pl.CostEstimate(flops=cost[0], bytes_accessed=cost[1], transcendentals=0),
        **kw,
    )


def per_device(tokens, cotangent, gates, routes, w_gate, w_up, w_down):
    n_ex = lax.axis_size("ex")
    n_hid = lax.axis_size("hid")
    side = 4
    tok, width = tokens.shape
    unit = w_gate.shape[1]
    row_of = lambda h, dy, dx: ((h // side) ^ dy) * side + (h % side + dx) % side
    perm = lambda dy, dx: [(h, row_of(h, dy, dx)) for h in range(n_hid)]
    move = lambda v, dy, dx: lax.ppermute(v, "hid", perm(dy, dx))

    weights = jnp.concatenate([w_gate[0], w_up[0], w_down[0]], axis=0)
    w_all = [weights] + [move(weights, 0, d) for d in (1, -1, 2)]

    small = (1 << 26, 1 << 21)
    packed = _call(pack_kernel, _shape(8 * n_ex, width), "pack", small)(tokens, cotangent, gates, routes)
    arrived = lax.all_to_all(packed, "ex", split_axis=0, concat_axis=0, tiled=True)
    own, other = _call(
        unpack_kernel, (_shape(4 * n_ex, width), _shape(4 * n_ex, width)), "unpack", small
    )(arrived)
    rows_all = [own, move(own, 1, 0), move(other, 2, 0), move(other, 3, 0)]

    hid = 4 * unit
    rows = 2 * n_ex
    parts = _call(
        grad_kernel,
        tuple(_shape(rows, width) for _ in range(4)),
        "grad",
        (10 * 4 * rows * hid * width, 6 * hid * width),
        in_specs=[pl.BlockSpec(memory_space=pl.ANY)] * 8,
        scratch_shapes=[
            pltpu.VMEM((4 * rows, width), BF),
            pltpu.VMEM((4 * rows, width), BF),
            pltpu.VMEM((hid, width), BF),
            pltpu.VMEM((hid, width), BF),
            pltpu.VMEM((hid, width), BF),
            pltpu.VMEM((4 * rows, hid), F32),
            pltpu.VMEM((4 * rows, hid), F32),
            pltpu.VMEM((4 * rows, hid), F32),
            pltpu.SemaphoreType.DMA((8,)),
            pltpu.SemaphoreType.DMA((12 * COLS,)),
        ],
        compiler_params=pltpu.CompilerParams(vmem_limit_bytes=40 * 1024 * 1024),
    )(*rows_all, *w_all)
    back = [parts[0]] + [move(parts[d], d, 0) for d in (1, 2, 3)]
    merged = _call(merge_kernel, _shape(8 * n_ex, width // 2), "merge", small)(*back)
    landed = lax.all_to_all(merged, "ex", split_axis=0, concat_axis=0, tiled=True)
    return _call(final_kernel, _shape(tok, width), "final", small)(landed, routes)


def solution(mesh):
    split = P(("ex", "hid"), None)
    deep = P(("ex", "hid"), None, None)
    return jax.shard_map(
        per_device,
        mesh=mesh,
        in_specs=(split, split, split, split, deep, deep, deep),
        out_specs=split,
        check_vma=False,
    )
```

time: 527 us -> 207 us (0.39)
  blocking collectives: 370 us -> 46 us
  local copies, waits for them, and re-layouts: 61.9 us -> 6.09 us
  starting transfers between devices: 4.53 us -> 46 us
  waiting for transfers between devices: 62 us -> 89.5 us
  matrix products: 20.3 us -> 0 us
  Pallas kernels: 0 us -> 17 us
  other arithmetic: 7.64 us -> 1.69 us
    all_to_all x3 -> x1, blocking collectives: 370 us -> 46 us  [per_device(): lax.all_to_all(merged, 'ex', split_axis=0, concat_axis=0, tiled=True)]
    ppermute x0 -> x9, waiting for transfers between devices: none -> 45.4 us  [per_device(): move = lambda v, dy, dx: lax.ppermute(v, 'hid', perm(dy, dx))]
    ppermute x0 -> x9, starting transfers between devices: none -> 29.2 us  [per_device(): move = lambda v, dy, dx: lax.ppermute(v, 'hid', perm(dy, dx))]
    dot_general x4 -> x0, matrix products: 20.3 us -> none  [the longest x1 8.19 us: hidden_grad(): first = jnp.dot(d_gate, wgate, preferred_element_type=jnp.float32)]
    all_to_all x1, waiting for transfers between devices: 62 us -> 44.1 us  [per_device(): lax.all_to_all(packed, 'ex', split_axis=0, concat_axis=0, tiled=True)]
    pallas_call x0 -> x5, Pallas kernels: none -> 17 us  [the longest x1 7.44 us: per_device(): _call(grad_kernel, tuple((_shape(rows, width) for _ in range(4))), 'grad'...]
    another operation x4 -> x0, local copies, waits for them, and re-layouts: 15.1 us -> none  [the longest x1 7.27 us: per_device(): cotan = received[:, 1].reshape(rows, width)]
    reshape x4 -> x0, local copies, waits for them, and re-layouts: 14.5 us -> none  [the longest x2 14.3 us: per_device(): partial_value = partial_value.reshape(n_hid, n_ex, slot_cap, width)]
  transfers between devices with their start and end apart: 1 -> 10, of which waited for: 1 -> 5; matrix products, arithmetic and copies ran while one was open for 0% -> 1% of each run, Pallas kernels for 0% -> 1%
where the time goes in v1:
time: 207 us; the launch traced here: 206 us
  waiting for transfers between devices  89.5 us (43%)
  starting transfers between devices  46 us (22%)
  blocking collectives  46 us (22%)
  Pallas kernels  17 us (8%)
  local copies, waits for them, and re-layouts  6.09 us (3%)
    all_to_all x1, blocking collectives, per_device(): lax.all_to_all(merged, 'ex', split_axis=0, concat_axis=0, tiled=True)  46 us
    ppermute x9, waiting for transfers between devices, per_device(): move = lambda v, dy, dx: lax.ppermute(v, 'hid', perm(dy, dx))  45.4 us
    all_to_all x1, waiting for transfers between devices, per_device(): lax.all_to_all(packed, 'ex', split_axis=0, concat_axis=0, tiled=True)  44.1 us
    ppermute x9, starting transfers between devices, per_device(): move = lambda v, dy, dx: lax.ppermute(v, 'hid', perm(dy, dx))  29.2 us
    all_to_all x1, starting transfers between devices, per_device(): lax.all_to_all(packed, 'ex', split_axis=0, concat_axis=0, tiled=True)  16.8 us
    pallas_call x1, Pallas kernels, per_device(): _call(grad_kernel, tuple((_shape(rows, width) for _ in range(4))), 'grad'...  7.44 us
    unnamed x14, local copies, waits for them, and re-layouts  6.09 us
  transfers between devices with their start and end apart: 10, of which 5 were waited for; matrix products, arithmetic and copies ran while one was open for 1% of the time, Pallas kernels for 1%

profile of v1, /device:TPU:1, one launch (start us, length us, event | category | flops | bytes accessed | tf_op | source)
XLA Modules:
  0.0 206.5 jit_solution(8854907044649907408)
XLA Ops:
  0.0 1.3 copy.9.route_ref
  1.3 1.4 copy.8.gate_ref
  2.7 2.5 %pack.1 = bf16[256,2048]{1,0:T(8,128)(2,1)} custom-call(bf16[16,2048]{1,0:T(8,128)(2,1)} %tok_ref.1, bf16[16,2048]{1,0:T(8,128)(2,1)} %cot_ref.1, f32[16,4]{1,0:T(8,128)} %copy.8.gate_ref, s32[16,4]{1,0:T(8,128)} %copy.9.route_ref), custom_call_target="tpu_custom_call" | custom-call | flops 67108864 | bytes 2097152 | tf_op jit(solution)/shard_map/pack/pallas_call | solution.py:180
  5.2 16.8 %all-to-all-start = ((bf16[32,8,2048]{2,1,0:T(8,128)(2,1)}), bf16[32,8,2048]{2,1,0:T(8,128)(2,1)S(1)}, u32[]{:S(2)}, u32[]{:S(2)}) async-start(bf16[32,8,2048]{2,1,0:T(8,128)(2,1)} %bitcast.8), calls=%async_computation | async-start | bytes 2097152 | tf_op jit(solution)/shard_map/all_to_all | solution.py:181
  22.0 1.7 pad_maximum_fusion.refs_4_
  23.6 4.6 %collective-permute-start.5 = (bf16[528,2048]{1,0:T(8,128)(2,1)S(1)}, bf16[528,2048]{1,0:T(8,128)(2,1)}, u32[]{:S(2)}, u32[]{:S(2)}) collective-permute-start(bf16[528,2048]{1,0:T(8,128)(2,1)S(1)} %pad_maximum_fusion.refs_4_), channel_id=1, source_target_pairs={{0,2},{1,3},{2,0},{3,1},{4,6},{5,7},{6,4},{7,5},{8,10},{9,11},{10,... | collective-permute-start | bytes 6488072 | tf_op jit(solution)/shard_map/ppermute | solution.py:174
  28.3 2.8 %collective-permute-start.4 = (bf16[528,2048]{1,0:T(8,128)(2,1)S(1)}, bf16[528,2048]{1,0:T(8,128)(2,1)}, u32[]{:S(2)}, u32[]{:S(2)}) collective-permute-start(bf16[528,2048]{1,0:T(8,128)(2,1)S(1)} %pad_maximum_fusion.refs_4_), channel_id=1, source_target_pairs={{0,3},{1,0},{2,1},{3,2},{4,7},{5,4},{6,5},{7,6},{8,11},{9,8},{10,9... | collective-permute-start | bytes 6488072 | tf_op jit(solution)/shard_map/ppermute | solution.py:174
  31.1 2.5 %collective-permute-start.3 = (bf16[528,2048]{1,0:T(8,128)(2,1)S(1)}, bf16[528,2048]{1,0:T(8,128)(2,1)}, u32[]{:S(2)}, u32[]{:S(2)}) collective-permute-start(bf16[528,2048]{1,0:T(8,128)(2,1)S(1)} %pad_maximum_fusion.refs_4_), channel_id=1, source_target_pairs={{0,1},{1,2},{2,3},{3,0},{4,5},{5,6},{6,7},{7,4},{8,9},{9,10},{10,1... | collective-permute-start | bytes 6488072 | tf_op jit(solution)/shard_map/ppermute | solution.py:174
  33.6 44.1 %all-to-all-done = bf16[32,8,2048]{2,1,0:T(8,128)(2,1)S(1)} async-done(((bf16[32,8,2048]{2,1,0:T(8,128)(2,1)}), bf16[32,8,2048]{2,1,0:T(8,128)(2,1)S(1)}, u32[]{:S(2)}, u32[]{:S(2)}) %all-to-all-start) | async-done | bytes 1048608 | tf_op jit(solution)/shard_map/all_to_all | solution.py:181
  78.6 2.6 %unpack.1 = (bf16[128,2048]{1,0:T(8,128)(2,1)}, bf16[128,2048]{1,0:T(8,128)(2,1)}) custom-call(bf16[256,2048]{1,0:T(8,128)(2,1)} %bitcast.7), custom_call_target="tpu_custom_call" | custom-call | flops 67108864 | bytes 2097152 | tf_op jit(solution)/shard_map/unpack/pallas_call | solution.py:182
  81.3 3.2 %collective-permute-start = (bf16[128,2048]{1,0:T(8,128)(2,1)}, bf16[128,2048]{1,0:T(8,128)(2,1)S(1)}, u32[]{:S(2)}, u32[]{:S(2)}) collective-permute-start(bf16[128,2048]{1,0:T(8,128)(2,1)} %get-tuple-element.11.refs_0_), channel_id=1, source_target_pairs={{0,4},{1,5},{2,6},{3,7},{4,0},{5,1},{6,2},{7,3},{8,12},{9,13},{10,... | collective-permute-start | bytes 1572872 | tf_op jit(solution)/shard_map/ppermute | solution.py:174
  84.5 3.8 %collective-permute-start.2 = (bf16[128,2048]{1,0:T(8,128)(2,1)}, bf16[128,2048]{1,0:T(8,128)(2,1)S(1)}, u32[]{:S(2)}, u32[]{:S(2)}) collective-permute-start(bf16[128,2048]{1,0:T(8,128)(2,1)} %get-tuple-element.12), channel_id=1, source_target_pairs={{0,12},{1,13},{2,14},{3,15},{4,8},{5,9},{6,10},{7,11},{8,4},{9,5},... | collective-permute-start | bytes 1572872 | tf_op jit(solution)/shard_map/ppermute | solution.py:174
  88.3 2.6 %collective-permute-start.1 = (bf16[128,2048]{1,0:T(8,128)(2,1)}, bf16[128,2048]{1,0:T(8,128)(2,1)S(1)}, u32[]{:S(2)}, u32[]{:S(2)}) collective-permute-start(bf16[128,2048]{1,0:T(8,128)(2,1)} %get-tuple-element.12), channel_id=1, source_target_pairs={{0,8},{1,9},{2,10},{3,11},{4,12},{5,13},{6,14},{7,15},{8,0},{9,1},... | collective-permute-start | bytes 1572872 | tf_op jit(solution)/shard_map/ppermute | solution.py:174
  90.9 31.1 %collective-permute-done.4.refs_6_ = bf16[528,2048]{1,0:T(8,128)(2,1)} collective-permute-done((bf16[528,2048]{1,0:T(8,128)(2,1)S(1)}, bf16[528,2048]{1,0:T(8,128)(2,1)}, u32[]{:S(2)}, u32[]{:S(2)}) %collective-permute-start.4) | collective-permute-done | bytes 2162720 | tf_op jit(solution)/shard_map/ppermute | solution.py:174
  122.5 1.0 copy-done.1
  123.5 7.4 %grad.1 = (bf16[64,2048]{1,0:T(8,128)(2,1)S(1)}, bf16[64,2048]{1,0:T(8,128)(2,1)S(1)}, bf16[64,2048]{1,0:T(8,128)(2,1)S(1)}, bf16[64,2048]{1,0:T(8,128)(2,1)S(1)}) custom-call(bf16[128,2048]{1,0:T(8,128)(2,1)S(1)} %copy-done.1, bf16[128,2048]{1,0:T(8,128)(2,1)S(1)} %collective-permute-done.refs_1_, bf16[128,2048]{1,0:T(8,128)(2,1)S(1)} %collective-permute-done.1.refs_2_, ...), custom_call_target="tpu_custom_call" | custom-call | flops 3690987520 | bytes 8650752 | tf_op jit(solution)/shard_map/grad/pallas_call | solution.py:189
  131.7 3.2 %collective-permute-start.6 = (bf16[64,2048]{1,0:T(8,128)(2,1)S(1)}, bf16[64,2048]{1,0:T(8,128)(2,1)S(1)}, u32[]{:S(2)}, u32[]{:S(2)}) collective-permute-start(bf16[64,2048]{1,0:T(8,128)(2,1)S(1)} %get-tuple-element.14), channel_id=1, source_target_pairs={{0,4},{1,5},{2,6},{3,7},{4,0},{5,1},{6,2},{7,3},{8,12},{9,13},{10,... | collective-permute-start | bytes 786440 | tf_op jit(solution)/shard_map/ppermute | solution.py:174
  134.8 4.5 %collective-permute-start.7 = (bf16[64,2048]{1,0:T(8,128)(2,1)S(1)}, bf16[64,2048]{1,0:T(8,128)(2,1)S(1)}, u32[]{:S(2)}, u32[]{:S(2)}) collective-permute-start(bf16[64,2048]{1,0:T(8,128)(2,1)S(1)} %get-tuple-element.15), channel_id=1, source_target_pairs={{0,8},{1,9},{2,10},{3,11},{4,12},{5,13},{6,14},{7,15},{8,0},{9,1},... | collective-permute-start | bytes 786440 | tf_op jit(solution)/shard_map/ppermute | solution.py:174
  139.4 1.9 collective-permute-start.8
  141.3 7.5 %collective-permute-done.7.c_ref = bf16[64,2048]{1,0:T(8,128)(2,1)S(1)} collective-permute-done((bf16[64,2048]{1,0:T(8,128)(2,1)S(1)}, bf16[64,2048]{1,0:T(8,128)(2,1)S(1)}, u32[]{:S(2)}, u32[]{:S(2)}) %collective-permute-start.7) | collective-permute-done | bytes 262176 | tf_op jit(solution)/shard_map/ppermute | solution.py:174
  148.9 6.4 %collective-permute-done.8.d_ref = bf16[64,2048]{1,0:T(8,128)(2,1)S(1)} collective-permute-done((bf16[64,2048]{1,0:T(8,128)(2,1)S(1)}, bf16[64,2048]{1,0:T(8,128)(2,1)S(1)}, u32[]{:S(2)}, u32[]{:S(2)}) %collective-permute-start.8) | collective-permute-done | bytes 262176 | tf_op jit(solution)/shard_map/ppermute | solution.py:174
  155.9 2.4 %merge.1 = bf16[256,1024]{1,0:T(8,128)(2,1)} custom-call(bf16[64,2048]{1,0:T(8,128)(2,1)} %copy-done, bf16[64,2048]{1,0:T(8,128)(2,1)} %copy-done.3, bf16[64,2048]{1,0:T(8,128)(2,1)} %copy-done.4, bf16[64,2048]{1,0:T(8,128)(2,1)} %copy-done.5), custom_call_target="tpu_custom_call" | custom-call | flops 67108864 | bytes 2097152 | tf_op jit(solution)/shard_map/merge/pallas_call | solution.py:210
  158.3 46.0 %all_to_all.22 = bf16[32,8,1024]{2,1,0:T(8,128)(2,1)} all-to-all(bf16[32,8,1024]{2,1,0:T(8,128)(2,1)} %bitcast.9), channel_id=1, replica_groups=mesh['ex'=32,'hid'=16] {'ex'}, dimensions={0} | all-to-all | bytes 1048576 | tf_op jit(solution)/shard_map/all_to_all | solution.py:211
  204.4 2.1 %final.1 = bf16[16,2048]{1,0:T(8,128)(2,1)} custom-call(bf16[256,1024]{1,0:T(8,128)(2,1)} %bitcast.10, s32[16,4]{1,0:T(8,128)} %copy.9.route_ref), custom_call_target="tpu_custom_call" | custom-call | flops 67108864 | bytes 2097152 | tf_op jit(solution)/shard_map/final/pallas_call | solution.py:212
  (17 shorter events, 2.8 us)
Async XLA Ops:
  5.2 72.5 %all-to-all-start = ((bf16[32,8,2048]{2,1,0:T(8,128)(2,1)}), bf16[32,8,2048]{2,1,0:T(8,128)(2,1)S(1)}, u32[]{:S(2)}, u32[]{:S(2)}) async-start(bf16[32,8,2048]{2,1,0:T(8,128)(2,1)} %bitcast.8), calls=%async_computation | async-start | bytes 2097152 | tf_op jit(solution)/shard_map/all_to_all | solution.py:181
  23.6 64.6 %collective-permute-start.5 = (bf16[528,2048]{1,0:T(8,128)(2,1)S(1)}, bf16[528,2048]{1,0:T(8,128)(2,1)}, u32[]{:S(2)}, u32[]{:S(2)}) collective-permute-start(bf16[528,2048]{1,0:T(8,128)(2,1)S(1)} %pad_maximum_fusion.refs_4_), channel_id=1, source_target_pairs={{0,2},{1,3},{2,0},{3,1},{4,6},{5,7},{6,4},{7,5},{8,10},{9,11},{10,... | collective-permute-start | bytes 6488072 | tf_op jit(solution)/shard_map/ppermute | solution.py:174
  28.3 93.7 %collective-permute-start.4 = (bf16[528,2048]{1,0:T(8,128)(2,1)S(1)}, bf16[528,2048]{1,0:T(8,128)(2,1)}, u32[]{:S(2)}, u32[]{:S(2)}) collective-permute-start(bf16[528,2048]{1,0:T(8,128)(2,1)S(1)} %pad_maximum_fusion.refs_4_), channel_id=1, source_target_pairs={{0,3},{1,0},{2,1},{3,2},{4,7},{5,4},{6,5},{7,6},{8,11},{9,8},{10,9... | collective-permute-start | bytes 6488072 | tf_op jit(solution)/shard_map/ppermute | solution.py:174
  31.1 91.4 %collective-permute-start.3 = (bf16[528,2048]{1,0:T(8,128)(2,1)S(1)}, bf16[528,2048]{1,0:T(8,128)(2,1)}, u32[]{:S(2)}, u32[]{:S(2)}) collective-permute-start(bf16[528,2048]{1,0:T(8,128)(2,1)S(1)} %pad_maximum_fusion.refs_4_), channel_id=1, source_target_pairs={{0,1},{1,2},{2,3},{3,0},{4,5},{5,6},{6,7},{7,4},{8,9},{9,10},{10,1... | collective-permute-start | bytes 6488072 | tf_op jit(solution)/shard_map/ppermute | solution.py:174
  77.7 1.0 copy-start.2
  81.3 41.2 %collective-permute-start = (bf16[128,2048]{1,0:T(8,128)(2,1)}, bf16[128,2048]{1,0:T(8,128)(2,1)S(1)}, u32[]{:S(2)}, u32[]{:S(2)}) collective-permute-start(bf16[128,2048]{1,0:T(8,128)(2,1)} %get-tuple-element.11.refs_0_), channel_id=1, source_target_pairs={{0,4},{1,5},{2,6},{3,7},{4,0},{5,1},{6,2},{7,3},{8,12},{9,13},{10,... | collective-permute-start | bytes 1572872 | tf_op jit(solution)/shard_map/ppermute | solution.py:174
  84.5 38.0 %collective-permute-start.2 = (bf16[128,2048]{1,0:T(8,128)(2,1)}, bf16[128,2048]{1,0:T(8,128)(2,1)S(1)}, u32[]{:S(2)}, u32[]{:S(2)}) collective-permute-start(bf16[128,2048]{1,0:T(8,128)(2,1)} %get-tuple-element.12), channel_id=1, source_target_pairs={{0,12},{1,13},{2,14},{3,15},{4,8},{5,9},{6,10},{7,11},{8,4},{9,5},... | collective-permute-start | bytes 1572872 | tf_op jit(solution)/shard_map/ppermute | solution.py:174
  88.3 34.2 %collective-permute-start.1 = (bf16[128,2048]{1,0:T(8,128)(2,1)}, bf16[128,2048]{1,0:T(8,128)(2,1)S(1)}, u32[]{:S(2)}, u32[]{:S(2)}) collective-permute-start(bf16[128,2048]{1,0:T(8,128)(2,1)} %get-tuple-element.12), channel_id=1, source_target_pairs={{0,8},{1,9},{2,10},{3,11},{4,12},{5,13},{6,14},{7,15},{8,0},{9,1},... | collective-permute-start | bytes 1572872 | tf_op jit(solution)/shard_map/ppermute | solution.py:174
  122.5 1.0 copy-start.1
  131.0 0.7 copy-start
  131.7 9.7 %collective-permute-start.6 = (bf16[64,2048]{1,0:T(8,128)(2,1)S(1)}, bf16[64,2048]{1,0:T(8,128)(2,1)S(1)}, u32[]{:S(2)}, u32[]{:S(2)}) collective-permute-start(bf16[64,2048]{1,0:T(8,128)(2,1)S(1)} %get-tuple-element.14), channel_id=1, source_target_pairs={{0,4},{1,5},{2,6},{3,7},{4,0},{5,1},{6,2},{7,3},{8,12},{9,13},{10,... | collective-permute-start | bytes 786440 | tf_op jit(solution)/shard_map/ppermute | solution.py:174
  134.8 14.0 %collective-permute-start.7 = (bf16[64,2048]{1,0:T(8,128)(2,1)S(1)}, bf16[64,2048]{1,0:T(8,128)(2,1)S(1)}, u32[]{:S(2)}, u32[]{:S(2)}) collective-permute-start(bf16[64,2048]{1,0:T(8,128)(2,1)S(1)} %get-tuple-element.15), channel_id=1, source_target_pairs={{0,8},{1,9},{2,10},{3,11},{4,12},{5,13},{6,14},{7,15},{8,0},{9,1},... | collective-permute-start | bytes 786440 | tf_op jit(solution)/shard_map/ppermute | solution.py:174
  139.4 15.8 %collective-permute-start.8 = (bf16[64,2048]{1,0:T(8,128)(2,1)S(1)}, bf16[64,2048]{1,0:T(8,128)(2,1)S(1)}, u32[]{:S(2)}, u32[]{:S(2)}) collective-permute-start(bf16[64,2048]{1,0:T(8,128)(2,1)S(1)} %get-tuple-element.16), channel_id=1, source_target_pairs={{0,12},{1,13},{2,14},{3,15},{4,8},{5,9},{6,10},{7,11},{8,4},{9,5},... | collective-permute-start | bytes 786440 | tf_op jit(solution)/shard_map/ppermute | solution.py:174
  141.3 13.9 %copy-start.3 = (bf16[64,2048]{1,0:T(8,128)(2,1)}, bf16[64,2048]{1,0:T(8,128)(2,1)S(1)}, u32[]{:S(2)}) copy-start(bf16[64,2048]{1,0:T(8,128)(2,1)S(1)} %collective-permute-done.6.b_ref) | copy-start | bytes 786436
  148.9 6.4 %copy-start.4 = (bf16[64,2048]{1,0:T(8,128)(2,1)}, bf16[64,2048]{1,0:T(8,128)(2,1)S(1)}, u32[]{:S(2)}) copy-start(bf16[64,2048]{1,0:T(8,128)(2,1)S(1)} %collective-permute-done.7.c_ref) | copy-start | bytes 786436
  155.2 0.7 copy-start.5

commit v2 on v1

v2 whole, which is shorter than its diff:
```python
import functools

import jax
import jax.numpy as jnp
from jax import lax
from jax.experimental import pallas as pl
from jax.experimental.pallas import tpu as pltpu
from jax.sharding import PartitionSpec as P

BF = jnp.bfloat16
F32 = jnp.float32
COLS = 4


def _iota(shape, axis):
    return lax.broadcasted_iota(jnp.int32, shape, axis)


def _select(cond):
    return jnp.where(cond, 1.0, 0.0).astype(F32)


def _named(routes, expert):
    tok, top = routes.shape
    each = [_select(routes[:, k : k + 1] == expert) for k in range(top)]
    named = functools.reduce(lambda a, b: a + b, each)
    earlier = _select(_iota((tok, tok), 1) < _iota((tok, tok), 0)).astype(BF)
    slot = jnp.dot(earlier, named.astype(BF), preferred_element_type=F32)
    return each, named, slot


def pack_kernel(tok_ref, cot_ref, gate_ref, route_ref, out_ref):
    tok, width = tok_ref.shape
    top = route_ref.shape[1]
    rows = out_ref.shape[0]
    r = _iota((tok, rows), 1)
    each, named, slot = _named(route_ref[...], r // 4)
    hit = _select(slot == (r % 2).astype(F32))
    is_x = _select((r // 2) % 2 == 0)
    cot = cot_ref[...].astype(F32)
    parts = [tok_ref[...]]
    picks = [(named * hit * is_x).astype(BF)]
    for k in range(top):
        parts.append((gate_ref[:, k : k + 1] * cot).astype(BF))
        picks.append((each[k] * hit * (1.0 - is_x)).astype(BF))
    data = jnp.concatenate(parts, axis=0)
    pick = jnp.concatenate(picks, axis=0)
    out_ref[...] = lax.dot_general(
        pick, data, (((0,), (0,)), ((), ())), preferred_element_type=F32
    ).astype(BF)


def unpack_kernel(in_ref, out_ref):
    rows = out_ref.shape[0] // 4
    half = rows // 2
    q = _iota((rows, in_ref.shape[0]), 0)
    r = _iota((rows, in_ref.shape[0]), 1)
    want = ((q % half) // 2) * 8 + (q // half) * 2 + q % 2
    data = in_ref[...]
    for local in range(2):
        pick = _select(r == want + 4 * local).astype(BF)
        mine = jnp.dot(pick, data, preferred_element_type=F32).astype(BF)
        for y in (2 * local, 2 * local + 1):
            out_ref[y * rows : (y + 1) * rows, :] = mine


def grad_kernel(rows_in, g_in, u_in, d_in, out, x, y, wg, wu, wd, gate, upper, hidden, sem_r, sem_w):
    n = 4
    half = rows_in.shape[0] // (2 * n)
    width = x.shape[1]
    step = width // COLS
    row_copies = []
    for i in range(n):
        for m, dst in enumerate((x, y)):
            cp = pltpu.make_async_copy(
                rows_in.at[pl.ds((2 * i + m) * half, half)], dst.at[pl.ds(i * half, half)], sem_r.at[2 * i + m]
            )
            cp.start()
            row_copies.append(cp)
    w_copies = []
    for c in range(COLS):
        mine = []
        for m, (src, dst) in enumerate(((g_in, wg), (u_in, wu), (d_in, wd))):
            cp = pltpu.make_async_copy(
                src.at[:, pl.ds(c * step, step)], dst.at[:, pl.ds(c * step, step)], sem_w.at[c * 3 + m]
            )
            cp.start()
            mine.append(cp)
        w_copies.append(mine)
    for cp in row_copies:
        cp.wait()
    dims = (((1,), (1,)), ((), ()))
    for c in range(COLS):
        for cp in w_copies[c]:
            cp.wait()
        at = slice(c * step, (c + 1) * step)
        for acc, left, right in ((gate, x, wg), (upper, x, wu), (hidden, y, wd)):
            part = lax.dot_general(left[:, at], right[:, at], dims, preferred_element_type=F32)
            if c == 0:
                acc[...] = part
            else:
                acc[...] += part
    gv, uv, hv = gate[...], upper[...], hidden[...]
    sig = jax.nn.sigmoid(gv)
    d_up = (hv * gv * sig).astype(BF)
    d_gate = (hv * uv * sig * (1.0 + gv * (1.0 - sig))).astype(BF)
    for c in range(COLS):
        at = slice(c * step, (c + 1) * step)
        out[:, at] = (
            jnp.dot(d_gate, wg[:, at], preferred_element_type=F32)
            + jnp.dot(d_up, wu[:, at], preferred_element_type=F32)
        ).astype(BF)


def merge_kernel(in_ref, out_ref):
    rows = in_ref.shape[0] // 4
    width = out_ref.shape[1]
    data = []
    for local in range(2):
        both = [in_ref[y * rows : (y + 1) * rows, :].astype(F32) for y in (2 * local, 2 * local + 1)]
        total = (both[0] + both[1]).astype(BF)
        data += [total[:, :width], total[:, width:]]
    r = _iota((out_ref.shape[0], 4 * rows), 0)
    q = _iota((out_ref.shape[0], 4 * rows), 1)
    want = ((r // 2) % 2) * 2 * rows + ((r // 4) % 2) * rows + (r // 8) * 2 + r % 2
    out_ref[...] = jnp.dot(
        _select(q == want).astype(BF), jnp.concatenate(data, axis=0), preferred_element_type=F32
    ).astype(BF)


def final_kernel(in_ref, route_ref, out_ref):
    tok = out_ref.shape[0]
    rows, width = in_ref.shape
    r = _iota((tok, rows), 1)
    _, named, slot = _named(route_ref[...], 2 * (r // 8) + (r // 2) % 2)
    pick = named * _select(slot == (r % 2).astype(F32))
    data = in_ref[...]
    for h in range(2):
        mine = (pick * _select((r // 4) % 2 == h)).astype(BF)
        out_ref[:, h * width : (h + 1) * width] = jnp.dot(
            mine, data, preferred_element_type=F32
        ).astype(BF)


def _shape(*dims):
    return jax.ShapeDtypeStruct(dims, BF)


def _call(kernel, out_shape, name, cost, **kw):
    return pl.pallas_call(
        kernel,
        out_shape=out_shape,
        name=name,
        cost_estimate=pl.CostEstimate(flops=cost[0], bytes_accessed=cost[1], transcendentals=0),
        **kw,
    )


def per_device(tokens, cotangent, gates, routes, w_gate, w_up, w_down):
    n_ex = lax.axis_size("ex")
    side = 4
    tok, width = tokens.shape
    unit = w_gate.shape[1]
    along_x = [[y * side + x for x in range(side)] for y in range(side)]
    along_y = [[y * side + x for y in range(side)] for x in range(side)]

    gather = lambda w: lax.all_gather(w[0], "hid", axis=0, tiled=True, axis_index_groups=along_x)
    weights = [gather(w) for w in (w_gate, w_up, w_down)]

    def over_y(v):
        return lax.all_to_all(
            v, "hid", split_axis=0, concat_axis=0, tiled=True, axis_index_groups=along_y
        )

    small = (1 << 26, 1 << 21)
    packed = _call(pack_kernel, _shape(8 * n_ex, width), "pack", small)(tokens, cotangent, gates, routes)
    arrived = lax.all_to_all(packed, "ex", split_axis=0, concat_axis=0, tiled=True)
    spread = _call(unpack_kernel, _shape(16 * n_ex, width), "unpack", small)(arrived)
    rows_all = over_y(spread)

    hid = side * unit
    rows = 8 * n_ex
    parts = _call(
        grad_kernel,
        _shape(rows, width),
        "grad",
        (10 * rows * hid * width, 6 * hid * width),
        in_specs=[pl.BlockSpec(memory_space=pltpu.HBM)] * 4,
        scratch_shapes=[
            pltpu.VMEM((rows, width), BF),
            pltpu.VMEM((rows, width), BF),
            pltpu.VMEM((hid, width), BF),
            pltpu.VMEM((hid, width), BF),
            pltpu.VMEM((hid, width), BF),
            pltpu.VMEM((rows, hid), F32),
            pltpu.VMEM((rows, hid), F32),
            pltpu.VMEM((rows, hid), F32),
            pltpu.SemaphoreType.DMA((8,)),
            pltpu.SemaphoreType.DMA((3 * COLS,)),
        ],
        compiler_params=pltpu.CompilerParams(vmem_limit_bytes=40 * 1024 * 1024),
    )(rows_all, *weights)
    merged = _call(merge_kernel, _shape(8 * n_ex, width // 2), "merge", small)(over_y(parts))
    landed = lax.all_to_all(merged, "ex", split_axis=0, concat_axis=0, tiled=True)
    return _call(final_kernel, _shape(tok, width), "final", small)(landed, routes)


def solution(mesh):
    split = P(("ex", "hid"), None)
    deep = P(("ex", "hid"), None, None)
    return jax.shard_map(
        per_device,
        mesh=mesh,
        in_specs=(split, split, split, split, deep, deep, deep),
        out_specs=split,
        check_vma=False,
    )
```

time: 207 us -> 245 us (1.18)
  waiting for transfers between devices: 89.5 us -> 118 us
  starting transfers between devices: 46 us -> 21 us
  blocking collectives: 46 us -> 65.9 us
  between operations: 0.15 us -> 13.1 us
  local copies, waits for them, and re-layouts: 6.09 us -> 9.14 us
    all_gather x0 -> x3, waiting for transfers between devices: none -> 60.6 us  [per_device(): lax.all_gather(w[0], 'hid', axis=0, tiled=True, axis_index_groups=along_x)]
    ppermute x9 -> x0, waiting for transfers between devices: 45.4 us -> none  [per_device(): move = lambda v, dy, dx: lax.ppermute(v, 'hid', perm(dy, dx))]
    ppermute x9 -> x0, starting transfers between devices: 29.2 us -> none  [per_device(): move = lambda v, dy, dx: lax.ppermute(v, 'hid', perm(dy, dx))]
    all_to_all x0 -> x1, blocking collectives: none -> 18.1 us  [over_y(): lax.all_to_all(v, 'hid', split_axis=0, concat_axis=0, tiled=True, axis_in...]
    all_to_all x1, waiting for transfers between devices: 44.1 us -> 55 us  [per_device(): lax.all_to_all(packed, 'ex', split_axis=0, concat_axis=0, tiled=True)]
    all_to_all x0 -> x1, starting transfers between devices: none -> 4.17 us  [over_y(): lax.all_to_all(v, 'hid', split_axis=0, concat_axis=0, tiled=True, axis_in...]
    unnamed x14 -> x10, local copies, waits for them, and re-layouts: 6.09 us -> 9.14 us
  transfers between devices with their start and end apart: 10 -> 5, of which waited for: 5 -> 3; matrix products, arithmetic and copies ran while one was open for 1% -> 1% of each run, Pallas kernels for 1% -> 2%
where the time goes in v2:
time: 245 us
  waiting for transfers between devices  118 us (48%)
  blocking collectives  65.9 us (27%)
  starting transfers between devices  21 us (9%)
  Pallas kernels  17.9 us (7%)
  between operations  13.1 us (5%)
  local copies, waits for them, and re-layouts  9.14 us (4%)
    all_gather x3, waiting for transfers between devices, per_device(): lax.all_gather(w[0], 'hid', axis=0, tiled=True, axis_index_groups=along_x)  60.6 us
    all_to_all x1, waiting for transfers between devices, per_device(): lax.all_to_all(packed, 'ex', split_axis=0, concat_axis=0, tiled=True)  55 us
    all_to_all x1, blocking collectives, per_device(): lax.all_to_all(merged, 'ex', split_axis=0, concat_axis=0, tiled=True)  47.8 us
    all_to_all x1, blocking collectives, over_y(): lax.all_to_all(v, 'hid', split_axis=0, concat_axis=0, tiled=True, axis_in...  18.1 us
    all_to_all x1, starting transfers between devices, per_device(): lax.all_to_all(packed, 'ex', split_axis=0, concat_axis=0, tiled=True)  16.8 us
    unnamed x10, local copies, waits for them, and re-layouts  9.14 us
    pallas_call x1, Pallas kernels, per_device(): _call(grad_kernel, _shape(rows, width), 'grad', (10 * rows * hid * width,...  7.69 us
  transfers between devices with their start and end apart: 5, of which 3 were waited for; matrix products, arithmetic and copies ran while one was open for 1% of the time, Pallas kernels for 2%

profile of v2, /device:TPU:1, one launch (start us, length us, event | category | flops | bytes accessed | tf_op | source)
XLA Modules:
  0.0 244.7 jit_solution(13731633236161655935)
XLA Ops:
  6.5 0.7 all-gather.7.cloned.1.call-update
  7.3 0.0 all-gather.9.cloned.1.call-start
  7.3 0.7 all-gather.9.cloned.1.call-update
  8.0 1.4 copy.9.route_ref
  9.4 1.4 copy.8.gate_ref
  10.7 2.6 %pack.1 = bf16[256,2048]{1,0:T(8,128)(2,1)} custom-call(bf16[16,2048]{1,0:T(8,128)(2,1)} %tok_ref.1, bf16[16,2048]{1,0:T(8,128)(2,1)} %cot_ref.1, f32[16,4]{1,0:T(8,128)} %copy.8.gate_ref, s32[16,4]{1,0:T(8,128)} %copy.9.route_ref), custom_call_target="tpu_custom_call" | custom-call | flops 67108864 | bytes 2097152 | tf_op jit(solution)/shard_map/pack/pallas_call | solution.py:176
  13.3 16.8 %all-to-all-start = ((bf16[32,8,2048]{2,1,0:T(8,128)(2,1)}), bf16[32,8,2048]{2,1,0:T(8,128)(2,1)S(1)}, u32[]{:S(2)}, u32[]{:S(2)}) async-start(bf16[32,8,2048]{2,1,0:T(8,128)(2,1)} %bitcast.18), calls=%async_computation | async-start | bytes 2097152 | tf_op jit(solution)/shard_map/all_to_all | solution.py:177
  30.0 0.0 all-gather.11.cloned.1.call-start
  30.1 0.7 all-gather.11.cloned.1.call-update
  30.8 55.0 %all-to-all-done = bf16[32,8,2048]{2,1,0:T(8,128)(2,1)S(1)} async-done(((bf16[32,8,2048]{2,1,0:T(8,128)(2,1)}), bf16[32,8,2048]{2,1,0:T(8,128)(2,1)S(1)}, u32[]{:S(2)}, u32[]{:S(2)}) %all-to-all-start) | async-done | bytes 1048608 | tf_op jit(solution)/shard_map/all_to_all | solution.py:177
  85.8 1.0 copy-done.3
  86.7 3.1 %unpack.1 = bf16[512,2048]{1,0:T(8,128)(2,1)} custom-call(bf16[256,2048]{1,0:T(8,128)(2,1)} %bitcast.17), custom_call_target="tpu_custom_call" | custom-call | flops 67108864 | bytes 2097152 | tf_op jit(solution)/shard_map/unpack/pallas_call | solution.py:178
  89.8 4.2 %all-to-all-start.1 = ((bf16[4,128,2048]{2,1,0:T(8,128)(2,1)}), bf16[4,128,2048]{2,1,0:T(8,128)(2,1)S(1)}, u32[]{:S(2)}, u32[]{:S(2)}) async-start(bf16[4,128,2048]{2,1,0:T(8,128)(2,1)} %bitcast.16), calls=%async_computation.1 | async-start | bytes 4194304 | tf_op jit(solution)/shard_map/all_to_all | solution.py:171
  94.0 13.2 %all-gather.9.cloned.1.call-done = bf16[1,704,2048]{2,1,0:T(8,128)(2,1)} async-done(((bf16[1,176,2048]{2,1,0:T(8,128)(2,1)}), bf16[1,704,2048]{2,1,0:T(8,128)(2,1)}) %all-gather.9.cloned.1.call-update) | async-done | bytes 2883600 | tf_op jit(solution)/shard_map/all_gather | solution.py:167
  107.2 47.4 %all-gather.11.cloned.1.call-done = bf16[1,704,2048]{2,1,0:T(8,128)(2,1)} async-done(((bf16[1,176,2048]{2,1,0:T(8,128)(2,1)}), bf16[1,704,2048]{2,1,0:T(8,128)(2,1)}) %all-gather.11.cloned.1.call-update) | async-done | bytes 2883600 | tf_op jit(solution)/shard_map/all_gather | solution.py:167
  154.6 0.0 all-to-all-done.1
  154.6 1.8 copy-done
  156.4 1.8 copy-done.1
  158.2 1.8 copy-done.2
  160.0 7.7 %grad.1 = bf16[256,2048]{1,0:T(8,128)(2,1)S(1)} custom-call(bf16[512,2048]{1,0:T(8,128)(2,1)S(1)} %bitcast.11, bf16[704,2048]{1,0:T(8,128)(2,1)S(1)} %bitcast.13, bf16[704,2048]{1,0:T(8,128)(2,1)S(1)} %bitcast.14, bf16[704,2048]{1,0:T(8,128)(2,1)S(1)} %bitcast.15), custom_call_target="tpu_custom_call" | custom-call | flops 3690987520 | bytes 8650752 | tf_op jit(solution)/shard_map/grad/pallas_call | solution.py:183
  167.7 18.1 %all_to_all.44 = bf16[4,64,2048]{2,1,0:T(8,128)(2,1)} all-to-all(bf16[4,64,2048]{2,1,0:T(8,128)(2,1)S(1)} %bitcast.12), channel_id=1, replica_groups={{0,4,8,12},{1,5,9,13},{2,6,10,14},{3,7,11,15},{16,20,24,28},{17,21,25,2..., dimensions={0} | all-to-all | bytes 2097152 | tf_op jit(solution)/shard_map/all_to_all | solution.py:171
  185.8 2.5 %merge.1 = bf16[256,1024]{1,0:T(8,128)(2,1)} custom-call(bf16[256,2048]{1,0:T(8,128)(2,1)} %bitcast.19), custom_call_target="tpu_custom_call" | custom-call | flops 67108864 | bytes 2097152 | tf_op jit(solution)/shard_map/merge/pallas_call | solution.py:203
  188.3 47.8 %all_to_all.45 = bf16[32,8,1024]{2,1,0:T(8,128)(2,1)} all-to-all(bf16[32,8,1024]{2,1,0:T(8,128)(2,1)} %bitcast.20), channel_id=1, replica_groups=mesh['ex'=32,'hid'=16] {'ex'}, dimensions={0} | all-to-all | bytes 1048576 | tf_op jit(solution)/shard_map/all_to_all | solution.py:204
  236.1 2.1 final.1
  (6 shorter events, 0.0 us)
Async XLA Ops:
  6.5 87.4 %all-gather.7.cloned.1.call-start = ((), (), s32[]{:S(2)}) async-start(), calls=%async_computation.4 | async-start | bytes 3604480 | tf_op jit(solution)/shard_map/all_gather | solution.py:167
  7.3 99.9 %all-gather.9.cloned.1.call-start = ((), (), s32[]{:S(2)}) async-start(), calls=%async_computation.5 | async-start | bytes 3604480 | tf_op jit(solution)/shard_map/all_gather | solution.py:167
  13.3 72.5 %all-to-all-start = ((bf16[32,8,2048]{2,1,0:T(8,128)(2,1)}), bf16[32,8,2048]{2,1,0:T(8,128)(2,1)S(1)}, u32[]{:S(2)}, u32[]{:S(2)}) async-start(bf16[32,8,2048]{2,1,0:T(8,128)(2,1)} %bitcast.18), calls=%async_computation | async-start | bytes 2097152 | tf_op jit(solution)/shard_map/all_to_all | solution.py:177
  30.0 124.6 %all-gather.11.cloned.1.call-start = ((), (), s32[]{:S(2)}) async-start(), calls=%async_computation.6 | async-start | bytes 3604480 | tf_op jit(solution)/shard_map/all_gather | solution.py:167
  85.8 1.0 copy-start.3
  89.8 64.8 %all-to-all-start.1 = ((bf16[4,128,2048]{2,1,0:T(8,128)(2,1)}), bf16[4,128,2048]{2,1,0:T(8,128)(2,1)S(1)}, u32[]{:S(2)}, u32[]{:S(2)}) async-start(bf16[4,128,2048]{2,1,0:T(8,128)(2,1)} %bitcast.16), calls=%async_computation.1 | async-start | bytes 4194304 | tf_op jit(solution)/shard_map/all_to_all | solution.py:171
  154.6 1.8 copy-start
  156.4 1.8 copy-start.1
  158.2 1.8 copy-start.2
Sparse Core Ops, SparseCore 0:
  9.5 50.3 all-gather.6
  61.9 45.2 all-gather.8
  109.3 45.2 all-gather.10

commit v3 on v2

--- a/solution.py
+++ b/solution.py
@@ -21,33 +21,28 @@
 
 
 def _named(routes, expert):
-    tok, top = routes.shape
-    each = [_select(routes[:, k : k + 1] == expert) for k in range(top)]
+    top, tok = routes.shape
+    each = [_select(routes[k : k + 1, :] == expert) for k in range(top)]
     named = functools.reduce(lambda a, b: a + b, each)
-    earlier = _select(_iota((tok, tok), 1) < _iota((tok, tok), 0)).astype(BF)
-    slot = jnp.dot(earlier, named.astype(BF), preferred_element_type=F32)
+    earlier = _select(_iota((tok, tok), 0) < _iota((tok, tok), 1)).astype(BF)
+    slot = jnp.dot(named.astype(BF), earlier, preferred_element_type=F32)
     return each, named, slot
 
 
 def pack_kernel(tok_ref, cot_ref, gate_ref, route_ref, out_ref):
     tok, width = tok_ref.shape
-    top = route_ref.shape[1]
+    top = route_ref.shape[0]
     rows = out_ref.shape[0]
-    r = _iota((tok, rows), 1)
+    r = _iota((rows, tok), 0)
     each, named, slot = _named(route_ref[...], r // 4)
     hit = _select(slot == (r % 2).astype(F32))
     is_x = _select((r // 2) % 2 == 0)
-    cot = cot_ref[...].astype(F32)
-    parts = [tok_ref[...]]
-    picks = [(named * hit * is_x).astype(BF)]
-    for k in range(top):
-        parts.append((gate_ref[:, k : k + 1] * cot).astype(BF))
-        picks.append((each[k] * hit * (1.0 - is_x)).astype(BF))
-    data = jnp.concatenate(parts, axis=0)
-    pick = jnp.concatenate(picks, axis=0)
-    out_ref[...] = lax.dot_general(
-        pick, data, (((0,), (0,)), ((), ())), preferred_element_type=F32
-    ).astype(BF)
+    weight = sum(each[k] * gate_ref[k : k + 1, :] for k in range(top))
+    weight = jnp.sum(weight * hit * (1.0 - is_x) + is_x * (1.0 / tok), axis=1, keepdims=True)
+    pick = named * hit
+    pick = jnp.concatenate([pick * is_x, pick * (1.0 - is_x)], axis=1).astype(BF)
+    data = jnp.concatenate([tok_ref[...], cot_ref[...]], axis=0)
+    out_ref[...] = (weight * jnp.dot(pick, data, preferred_element_type=F32)).astype(BF)
 
 
 def unpack_kernel(in_ref, out_ref):
@@ -64,7 +59,7 @@
             out_ref[y * rows : (y + 1) * rows, :] = mine
 
 
-def grad_kernel(rows_in, g_in, u_in, d_in, out, x, y, wg, wu, wd, gate, upper, hidden, sem_r, sem_w):
+def grad_kernel(rows_in, w_in, out, x, y, wg, wu, wd, gate, upper, hidden, sem_r, sem_w):
     n = 4
     half = rows_in.shape[0] // (2 * n)
     width = x.shape[1]
@@ -77,15 +72,19 @@
             )
             cp.start()
             row_copies.append(cp)
+    unit = w_in.shape[0] // (3 * n)
     w_copies = []
     for c in range(COLS):
         mine = []
-        for m, (src, dst) in enumerate(((g_in, wg), (u_in, wu), (d_in, wd))):
-            cp = pltpu.make_async_copy(
-                src.at[:, pl.ds(c * step, step)], dst.at[:, pl.ds(c * step, step)], sem_w.at[c * 3 + m]
-            )
-            cp.start()
-            mine.append(cp)
+        for m, dst in enumerate((wg, wu, wd)):
+            for i in range(n):
+                cp = pltpu.make_async_copy(
+                    w_in.at[pl.ds((3 * i + m) * unit, unit), pl.ds(c * step, step)],
+                    dst.at[pl.ds(i * unit, unit), pl.ds(c * step, step)],
+                    sem_w.at[(c * 3 + m) * n + i],
+                )
+                cp.start()
+                mine.append(cp)
         w_copies.append(mine)
     for cp in row_copies:
         cp.wait()
@@ -131,14 +130,14 @@
 def final_kernel(in_ref, route_ref, out_ref):
     tok = out_ref.shape[0]
     rows, width = in_ref.shape
-    r = _iota((tok, rows), 1)
+    r = _iota((rows, tok), 0)
     _, named, slot = _named(route_ref[...], 2 * (r // 8) + (r // 2) % 2)
     pick = named * _select(slot == (r % 2).astype(F32))
     data = in_ref[...]
     for h in range(2):
         mine = (pick * _select((r // 4) % 2 == h)).astype(BF)
-        out_ref[:, h * width : (h + 1) * width] = jnp.dot(
-            mine, data, preferred_element_type=F32
+        out_ref[:, h * width : (h + 1) * width] = lax.dot_general(
+            mine, data, (((0,), (0,)), ((), ())), preferred_element_type=F32
         ).astype(BF)
 
 
@@ -146,12 +145,13 @@
     return jax.ShapeDtypeStruct(dims, BF)
 
 
-def _call(kernel, out_shape, name, cost, **kw):
+def _call(kernel, out_shape, name, cost, vmem=16, **kw):
     return pl.pallas_call(
         kernel,
         out_shape=out_shape,
         name=name,
         cost_estimate=pl.CostEstimate(flops=cost[0], bytes_accessed=cost[1], transcendentals=0),
+        compiler_params=pltpu.CompilerParams(vmem_limit_bytes=vmem * 1024 * 1024),
         **kw,
     )
 
@@ -164,8 +164,13 @@
     along_x = [[y * side + x for x in range(side)] for y in range(side)]
     along_y = [[y * side + x for y in range(side)] for x in range(side)]
 
-    gather = lambda w: lax.all_gather(w[0], "hid", axis=0, tiled=True, axis_index_groups=along_x)
-    weights = [gather(w) for w in (w_gate, w_up, w_down)]
+    weights = lax.all_gather(
+        jnp.concatenate([w_gate[0], w_up[0], w_down[0]], axis=0),
+        "hid",
+        axis=0,
+        tiled=True,
+        axis_index_groups=along_x,
+    )
 
     def over_y(v):
         return lax.all_to_all(
@@ -173,7 +178,9 @@
         )
 
     small = (1 << 26, 1 << 21)
-    packed = _call(pack_kernel, _shape(8 * n_ex, width), "pack", small)(tokens, cotangent, gates, routes)
+    packed = _call(pack_kernel, _shape(8 * n_ex, width), "pack", small)(
+        tokens, cotangent, gates.T, routes.T
+    )
     arrived = lax.all_to_all(packed, "ex", split_axis=0, concat_axis=0, tiled=True)
     spread = _call(unpack_kernel, _shape(16 * n_ex, width), "unpack", small)(arrived)
     rows_all = over_y(spread)
@@ -185,7 +192,7 @@
         _shape(rows, width),
         "grad",
         (10 * rows * hid * width, 6 * hid * width),
-        in_specs=[pl.BlockSpec(memory_space=pltpu.HBM)] * 4,
+        in_specs=[pl.BlockSpec(memory_space=pltpu.HBM)] * 2,
         scratch_shapes=[
             pltpu.VMEM((rows, width), BF),
             pltpu.VMEM((rows, width), BF),
@@ -196,13 +203,13 @@
             pltpu.VMEM((rows, hid), F32),
             pltpu.VMEM((rows, hid), F32),
             pltpu.SemaphoreType.DMA((8,)),
-            pltpu.SemaphoreType.DMA((3 * COLS,)),
+            pltpu.SemaphoreType.DMA((12 * COLS,)),
         ],
-        compiler_params=pltpu.CompilerParams(vmem_limit_bytes=40 * 1024 * 1024),
-    )(rows_all, *weights)
+        vmem=56,
+    )(rows_all, weights)
     merged = _call(merge_kernel, _shape(8 * n_ex, width // 2), "merge", small)(over_y(parts))
     landed = lax.all_to_all(merged, "ex", split_axis=0, concat_axis=0, tiled=True)
-    return _call(final_kernel, _shape(tok, width), "final", small)(landed, routes)
+    return _call(final_kernel, _shape(tok, width), "final", small)(landed, routes.T)
 
 
 def solution(mesh):

time: 245 us -> 194 us (0.79)
  waiting for transfers between devices: 118 us -> 0.02 us
  blocking collectives: 65.9 us -> 162 us
  starting transfers between devices: 21 us -> 0.01 us
  local copies, waits for them, and re-layouts: 9.14 us -> 0.84 us
  Pallas kernels: 17.9 us -> 13.6 us
  other arithmetic: 0 us -> 3.23 us
    all_to_all x0 -> x1, blocking collectives: none -> 72.3 us  [per_device(): lax.all_to_all(packed, 'ex', split_axis=0, concat_axis=0, tiled=True)]
    all_gather x3 -> x1, waiting for transfers between devices: 60.6 us -> 0.01 us  [per_device(): lax.all_gather(jnp.concatenate([w_gate[0], w_up[0], w_down[0]], axis=0),...]
    all_to_all x2 -> x0, waiting for transfers between devices: 55 us -> none  [the longest x1 55 us: per_device(): lax.all_to_all(packed, 'ex', split_axis=0, concat_axis=0, tiled=True)]
    all_to_all x1 -> x2, blocking collectives: 18.1 us -> 45.8 us  [over_y(): lax.all_to_all(v, 'hid', split_axis=0, concat_axis=0, tiled=True, axis_in...]
    all_to_all x2 -> x0, starting transfers between devices: 20.9 us -> none  [the longest x1 16.8 us: per_device(): lax.all_to_all(packed, 'ex', split_axis=0, concat_axis=0, tiled=True)]
    unnamed x10 -> x8, local copies, waits for them, and re-layouts: 9.14 us -> 0.84 us
    all_to_all x1, blocking collectives: 47.8 us -> 44.1 us  [per_device(): lax.all_to_all(merged, 'ex', split_axis=0, concat_axis=0, tiled=True)]
    pallas_call x1, Pallas kernels: 7.69 us -> 11 us  [per_device(): _call(grad_kernel, _shape(rows, width), 'grad', (10 * rows * hid * width,...]
  transfers between devices with their start and end apart: 5 -> 1, of which waited for: 3 -> 0; matrix products, arithmetic and copies ran while one was open for 1% -> 0% of each run, Pallas kernels for 2% -> 1%
where the time goes in v3:
time: 194 us; the launch traced here: 193 us
  blocking collectives  162 us (84%)
  Pallas kernels  13.6 us (7%)
  between operations  13.4 us (7%)
  other arithmetic  3.23 us (2%)
    all_to_all x1, blocking collectives, per_device(): lax.all_to_all(packed, 'ex', split_axis=0, concat_axis=0, tiled=True)  72.3 us
    all_to_all x2, blocking collectives, over_y(): lax.all_to_all(v, 'hid', split_axis=0, concat_axis=0, tiled=True, axis_in...  45.8 us
    all_to_all x1, blocking collectives, per_device(): lax.all_to_all(merged, 'ex', split_axis=0, concat_axis=0, tiled=True)  44.1 us
    pallas_call x1, Pallas kernels, per_device(): _call(grad_kernel, _shape(rows, width), 'grad', (10 * rows * hid * width,...  11 us
  transfers between devices with their start and end apart: 1, of which 0 were waited for; matrix products, arithmetic and copies ran while one was open for 0% of the time, Pallas kernels for 1%

profile of v3, /device:TPU:1, one launch (start us, length us, event | category | flops | bytes accessed | tf_op | source)
XLA Modules:
  0.0 193.3 jit_solution(3938325378521407039)
XLA Ops:
  6.5 0.0 all-gather.2.cloned.1.call-start
  6.5 3.2 %pad_maximum_fusion = bf16[528,2048]{1,0:T(8,128)(2,1)} fusion(bf16[176,2048]{1,0:T(8,128)(2,1)} %bitcast.24, bf16[176,2048]{1,0:T(8,128)(2,1)} %bitcast.25, bf16[176,2048]{1,0:T(8,128)(2,1)} %bitcast.26), kind=kLoop, calls=%fused_computation | loop fusion | flops 6488064 | bytes 4325376 | tf_op jit(solution)/shard_map/concatenate | solution.py:168
  9.8 0.0 copy-start
  9.8 0.0 copy-start.1
  9.8 0.0 copy-start.2
  9.8 0.0 copy-start.3
  9.8 0.0 all-gather.2.cloned.1.call-update
  9.8 0.8 copy-done
  10.6 0.0 copy-done.1
  10.6 0.0 copy-done.2
  10.6 0.0 copy-done.3
  10.6 0.6 pack.1
  11.3 72.3 %all_to_all.44 = bf16[32,8,2048]{2,1,0:T(8,128)(2,1)S(1)} all-to-all(bf16[32,8,2048]{2,1,0:T(8,128)(2,1)S(1)} %bitcast.16), channel_id=1, replica_groups=mesh['ex'=32,'hid'=16] {'ex'}, dimensions={0} | all-to-all | bytes 2097152 | tf_op jit(solution)/shard_map/all_to_all | solution.py:184
  83.5 0.5 unpack.1
  84.0 29.4 %all_to_all.45 = bf16[4,128,2048]{2,1,0:T(8,128)(2,1)} all-to-all(bf16[4,128,2048]{2,1,0:T(8,128)(2,1)S(1)} %bitcast.13), channel_id=1, replica_groups={{0,4,8,12},{1,5,9,13},{2,6,10,14},{3,7,11,15},{16,20,24,28},{17,21,25,2..., dimensions={0} | all-to-all | bytes 4194304 | tf_op jit(solution)/shard_map/all_to_all | solution.py:176
  113.4 0.0 all-gather.2.cloned.1.call-done.w_in
  113.4 11.0 %grad.1 = bf16[256,2048]{1,0:T(8,128)(2,1)} custom-call(bf16[512,2048]{1,0:T(8,128)(2,1)} %bitcast.22, bf16[2112,2048]{1,0:T(8,128)(2,1)} %all-gather.2.cloned.1.call-done.w_in), custom_call_target="tpu_custom_call" | custom-call | flops 3690987520 | bytes 8650752 | tf_op jit(solution)/shard_map/grad/pallas_call | solution.py:190
  124.5 16.4 %all_to_all.46 = bf16[4,64,2048]{2,1,0:T(8,128)(2,1)S(1)} all-to-all(bf16[4,64,2048]{2,1,0:T(8,128)(2,1)} %bitcast.23), channel_id=1, replica_groups={{0,4,8,12},{1,5,9,13},{2,6,10,14},{3,7,11,15},{16,20,24,28},{17,21,25,2..., dimensions={0} | all-to-all | bytes 2097152 | tf_op jit(solution)/shard_map/all_to_all | solution.py:176
  140.9 0.4 merge.1
  141.3 44.1 %all_to_all.47 = bf16[32,8,1024]{2,1,0:T(8,128)(2,1)S(1)} all-to-all(bf16[32,8,1024]{2,1,0:T(8,128)(2,1)S(1)} %bitcast.17), channel_id=1, replica_groups=mesh['ex'=32,'hid'=16] {'ex'}, dimensions={0} | all-to-all | bytes 1048576 | tf_op jit(solution)/shard_map/all_to_all | solution.py:211
  185.4 1.1 final.1
Async XLA Ops:
  6.5 106.9 %all-gather.2.cloned.1.call-start = ((), (), s32[]{:S(2)}) async-start(), calls=%async_computation.4 | async-start | bytes 10813440 | tf_op jit(solution)/shard_map/all_gather | solution.py:167
  9.8 0.8 copy-start
  9.8 0.9 copy-start.1
  9.8 0.9 copy-start.2
  9.8 0.9 copy-start.3
Sparse Core Ops, SparseCore 0:
  9.9 98.2 all-gather.1

commit v4 on v3

--- a/solution.py
+++ b/solution.py
@@ -45,6 +45,23 @@
     out_ref[...] = (weight * jnp.dot(pick, data, preferred_element_type=F32)).astype(BF)
 
 
+def split_kernel(*refs):
+    w_in, outs, sem = refs[:3], refs[3:5], refs[5]
+    cut = outs[0].shape[0] // 3
+    copies = []
+    for m, w in enumerate(w_in):
+        for i, (at, size) in enumerate(((0, cut), (cut, w.shape[1] - cut))):
+            copies.append(
+                pltpu.make_async_copy(
+                    w.at[0, pl.ds(at, size)], outs[i].at[pl.ds(m * size, size)], sem.at[2 * m + i]
+                )
+            )
+    for cp in copies:
+        cp.start()
+    for cp in copies:
+        cp.wait()
+
+
 def unpack_kernel(in_ref, out_ref):
     rows = out_ref.shape[0] // 4
     half = rows // 2
@@ -59,8 +76,10 @@
             out_ref[y * rows : (y + 1) * rows, :] = mine
 
 
-def grad_kernel(rows_in, w_in, out, x, y, wg, wu, wd, gate, upper, hidden, sem_r, sem_w):
+def grad_kernel(rows_in, *refs):
     n = 4
+    own, moved, out = refs[:3], refs[3 : 2 * n + 1], refs[2 * n + 1]
+    x, y, wg, wu, wd, gate, upper, hidden, sem_r, sem_w = refs[2 * n + 2 :]
     half = rows_in.shape[0] // (2 * n)
     width = x.shape[1]
     step = width // COLS
@@ -72,16 +91,21 @@
             )
             cp.start()
             row_copies.append(cp)
-    unit = w_in.shape[0] // (3 * n)
+    unit = own[0].shape[1]
+    first = moved[0].shape[0] // 3
     w_copies = []
     for c in range(COLS):
         mine = []
+        at = pl.ds(c * step, step)
         for m, dst in enumerate((wg, wu, wd)):
-            for i in range(n):
+            pieces = [(own[m].at[0, :, at], 0, unit)]
+            for i in range(2 * n - 2):
+                size = first if i % 2 == 0 else unit - first
+                to = unit * (1 + i // 2) + first * (i % 2)
+                pieces.append((moved[i].at[pl.ds(m * size, size), at], to, size))
+            for i, (src, to, size) in enumerate(pieces):
                 cp = pltpu.make_async_copy(
-                    w_in.at[pl.ds((3 * i + m) * unit, unit), pl.ds(c * step, step)],
-                    dst.at[pl.ds(i * unit, unit), pl.ds(c * step, step)],
-                    sem_w.at[(c * 3 + m) * n + i],
+                    src, dst.at[pl.ds(to, size), at], sem_w.at[(c * 3 + m) * (2 * n - 1) + i]
                 )
                 cp.start()
                 mine.append(cp)
@@ -161,17 +185,22 @@
     side = 4
     tok, width = tokens.shape
     unit = w_gate.shape[1]
-    along_x = [[y * side + x for x in range(side)] for y in range(side)]
     along_y = [[y * side + x for y in range(side)] for x in range(side)]
 
-    weights = lax.all_gather(
-        jnp.concatenate([w_gate[0], w_up[0], w_down[0]], axis=0),
-        "hid",
-        axis=0,
-        tiled=True,
-        axis_index_groups=along_x,
-    )
-
+    def shift(v, d):
+        return lax.ppermute(
+            v, "hid", [(y * side + x, y * side + (x + d) % side) for y in range(side) for x in range(side)]
+        )
+
+    cut = (unit // 2 + 15) // 16 * 16
+    early, late = _call(
+        split_kernel,
+        (_shape(3 * cut, width), _shape(3 * (unit - cut), width)),
+        "split",
+        (0, 12 * unit * width),
+        in_specs=[pl.BlockSpec(memory_space=pltpu.HBM)] * 3,
+        scratch_shapes=[pltpu.SemaphoreType.DMA((6,))],
+    )(w_gate, w_up, w_down)
     def over_y(v):
         return lax.all_to_all(
             v, "hid", split_axis=0, concat_axis=0, tiled=True, axis_index_groups=along_y
@@ -182,6 +211,12 @@
         tokens, cotangent, gates.T, routes.T
     )
     arrived = lax.all_to_all(packed, "ex", split_axis=0, concat_axis=0, tiled=True)
+    left_early, right_late = shift(early, 1), shift(late, -1)
+    left_late, right_early = shift(late, 1), shift(early, -1)
+    arrived, left_early, right_late, left_late, right_early = lax.optimization_barrier(
+        (arrived, left_early, right_late, left_late, right_early)
+    )
+    weights = [left_early, left_late, right_early, right_late, shift(left_early, 1), shift(right_late, -1)]
     spread = _call(unpack_kernel, _shape(16 * n_ex, width), "unpack", small)(arrived)
     rows_all = over_y(spread)
 
@@ -192,7 +227,7 @@
         _shape(rows, width),
         "grad",
         (10 * rows * hid * width, 6 * hid * width),
-        in_specs=[pl.BlockSpec(memory_space=pltpu.HBM)] * 2,
+        in_specs=[pl.BlockSpec(memory_space=pl.ANY)] * 10,
         scratch_shapes=[
             pltpu.VMEM((rows, width), BF),
             pltpu.VMEM((rows, width), BF),
@@ -203,10 +238,10 @@
             pltpu.VMEM((rows, hid), F32),
             pltpu.VMEM((rows, hid), F32),
             pltpu.SemaphoreType.DMA((8,)),
-            pltpu.SemaphoreType.DMA((12 * COLS,)),
+            pltpu.SemaphoreType.DMA((21 * COLS,)),
         ],
         vmem=56,
-    )(rows_all, weights)
+    )(rows_all, w_gate, w_up, w_down, *weights)
     merged = _call(merge_kernel, _shape(8 * n_ex, width // 2), "merge", small)(over_y(parts))
     landed = lax.all_to_all(merged, "ex", split_axis=0, concat_axis=0, tiled=True)
     return _call(final_kernel, _shape(tok, width), "final", small)(landed, routes.T)

time: 194 us -> 194 us (level)
  blocking collectives: 162 us -> 64.9 us
  waiting for transfers between devices: 0.02 us -> 64.4 us
  starting transfers between devices: 0.01 us -> 40.3 us
  between operations: 13.4 us -> 0.13 us
  local copies, waits for them, and re-layouts: 0.84 us -> 6.79 us
  Pallas kernels: 13.6 us -> 17.2 us
  other arithmetic: 3.23 us -> 0 us
    all_to_all x1 -> x0, blocking collectives: 72.3 us -> none  [per_device(): lax.all_to_all(packed, 'ex', split_axis=0, concat_axis=0, tiled=True)]
    ppermute x0 -> x6, waiting for transfers between devices: none -> 64.4 us  [shift(): lax.ppermute(v, 'hid', [(y * side + x, y * side + (x + d) % side) for y i...]
    all_to_all x2 -> x1, blocking collectives: 45.8 us -> 16 us  [over_y(): lax.all_to_all(v, 'hid', split_axis=0, concat_axis=0, tiled=True, axis_in...]
    all_to_all x0 -> x2, starting transfers between devices: none -> 21.1 us  [the longest x1 16.9 us: per_device(): lax.all_to_all(packed, 'ex', split_axis=0, concat_axis=0, tiled=True)]
    ppermute x0 -> x6, starting transfers between devices: none -> 19.3 us  [shift(): lax.ppermute(v, 'hid', [(y * side + x, y * side + (x + d) % side) for y i...]
    unnamed x8 -> x28, local copies, waits for them, and re-layouts: 0.84 us -> 6.79 us
    all_to_all x1, blocking collectives: 44.1 us -> 48.9 us  [per_device(): lax.all_to_all(merged, 'ex', split_axis=0, concat_axis=0, tiled=True)]
    concatenate x1 -> x0, other arithmetic: 3.23 us -> none  [per_device(): jnp.concatenate([w_gate[0], w_up[0], w_down[0]], axis=0)]
  transfers between devices with their start and end apart: 1 -> 8, of which waited for: 0 -> 3; matrix products, arithmetic and copies ran while one was open for 0% -> 0% of each run, Pallas kernels for 1% -> 0%
where the time goes in v4:
time: 194 us
  blocking collectives  64.9 us (33%)
  waiting for transfers between devices  64.4 us (33%)
  starting transfers between devices  40.3 us (21%)
  Pallas kernels  17.2 us (9%)
  local copies, waits for them, and re-layouts  6.79 us (4%)
    ppermute x6, waiting for transfers between devices, shift(): lax.ppermute(v, 'hid', [(y * side + x, y * side + (x + d) % side) for y i...  64.4 us
    all_to_all x1, blocking collectives, per_device(): lax.all_to_all(merged, 'ex', split_axis=0, concat_axis=0, tiled=True)  48.9 us
    ppermute x6, starting transfers between devices, shift(): lax.ppermute(v, 'hid', [(y * side + x, y * side + (x + d) % side) for y i...  19.3 us
    all_to_all x1, starting transfers between devices, per_device(): lax.all_to_all(packed, 'ex', split_axis=0, concat_axis=0, tiled=True)  16.9 us
    all_to_all x1, blocking collectives, over_y(): lax.all_to_all(v, 'hid', split_axis=0, concat_axis=0, tiled=True, axis_in...  16 us
    pallas_call x1, Pallas kernels, per_device(): _call(grad_kernel, _shape(rows, width), 'grad', (10 * rows * hid * width,...  11.3 us
    unnamed x28, local copies, waits for them, and re-layouts  6.79 us
    all_to_all x1, starting transfers between devices, over_y(): lax.all_to_all(v, 'hid', split_axis=0, concat_axis=0, tiled=True, axis_in...  4.19 us
  transfers between devices with their start and end apart: 8, of which 3 were waited for; matrix products, arithmetic and copies ran while one was open for 0% of the time, Pallas kernels for 0%

profile of v4, /device:TPU:1, one launch (start us, length us, event | category | flops | bytes accessed | tf_op | source)
XLA Modules:
  0.0 193.7 jit_solution(11955991583106454372)
XLA Ops:
  0.0 0.8 copy-done.3
  0.8 0.8 copy-done.4
  1.7 0.7 copy-done.5
  3.0 1.6 pack.1
  4.7 16.9 %all-to-all-start = ((bf16[32,8,2048]{2,1,0:T(8,128)(2,1)}), bf16[32,8,2048]{2,1,0:T(8,128)(2,1)S(1)}, u32[]{:S(2)}, u32[]{:S(2)}) async-start(bf16[32,8,2048]{2,1,0:T(8,128)(2,1)} %bitcast.2), calls=%async_computation | async-start | bytes 2097152 | tf_op jit(solution)/shard_map/all_to_all | solution.py:213
  21.6 0.9 split.1
  22.5 4.4 %collective-permute-start.3 = (bf16[288,2048]{1,0:T(8,128)(2,1)S(1)}, bf16[288,2048]{1,0:T(8,128)(2,1)S(1)}, u32[]{:S(2)}, u32[]{:S(2)}) collective-permute-start(bf16[288,2048]{1,0:T(8,128)(2,1)S(1)} %get-tuple-element.12), channel_id=1, source_target_pairs={{0,3},{1,0},{2,1},{3,2},{4,7},{5,4},{6,5},{7,6},{8,11},{9,8},{10,9... | collective-permute-start | bytes 3538952 | tf_op jit(solution)/shard_map/ppermute | solution.py:191
  26.9 1.9 collective-permute-start
  28.8 2.1 %collective-permute-start.2 = (bf16[240,2048]{1,0:T(8,128)(2,1)S(1)}, bf16[240,2048]{1,0:T(8,128)(2,1)S(1)}, u32[]{:S(2)}, u32[]{:S(2)}) collective-permute-start(bf16[240,2048]{1,0:T(8,128)(2,1)S(1)} %get-tuple-element.13), channel_id=1, source_target_pairs={{0,1},{1,2},{2,3},{3,0},{4,5},{5,6},{6,7},{7,4},{8,9},{9,10},{10,1... | collective-permute-start | bytes 2949128 | tf_op jit(solution)/shard_map/ppermute | solution.py:191
  30.9 4.4 %collective-permute-start.1 = (bf16[240,2048]{1,0:T(8,128)(2,1)S(1)}, bf16[240,2048]{1,0:T(8,128)(2,1)S(1)}, u32[]{:S(2)}, u32[]{:S(2)}) collective-permute-start(bf16[240,2048]{1,0:T(8,128)(2,1)S(1)} %get-tuple-element.13), channel_id=1, source_target_pairs={{0,3},{1,0},{2,1},{3,2},{4,7},{5,4},{6,5},{7,6},{8,11},{9,8},{10,9... | collective-permute-start | bytes 2949128 | tf_op jit(solution)/shard_map/ppermute | solution.py:191
  35.3 42.8 %collective-permute-done.2.refs_4_ = bf16[240,2048]{1,0:T(8,128)(2,1)S(1)} collective-permute-done((bf16[240,2048]{1,0:T(8,128)(2,1)S(1)}, bf16[240,2048]{1,0:T(8,128)(2,1)S(1)}, u32[]{:S(2)}, u32[]{:S(2)}) %collective-permute-start.2) | collective-permute-done | bytes 983072 | tf_op jit(solution)/shard_map/ppermute | solution.py:191
  78.1 1.1 copy-done.12
  79.2 1.8 unpack.1
  81.0 4.2 %all-to-all-start.1 = ((bf16[4,128,2048]{2,1,0:T(8,128)(2,1)}), bf16[4,128,2048]{2,1,0:T(8,128)(2,1)S(1)}, u32[]{:S(2)}, u32[]{:S(2)}) async-start(bf16[4,128,2048]{2,1,0:T(8,128)(2,1)} %bitcast.4), calls=%async_computation.1 | async-start | bytes 4194304 | tf_op jit(solution)/shard_map/all_to_all | solution.py:205
  85.2 1.9 collective-permute-start.4
  87.1 4.6 %collective-permute-start.5 = (bf16[240,2048]{1,0:T(8,128)(2,1)}, bf16[240,2048]{1,0:T(8,128)(2,1)S(1)}, u32[]{:S(2)}, u32[]{:S(2)}) collective-permute-start(bf16[240,2048]{1,0:T(8,128)(2,1)} %copy-done.12), channel_id=1, source_target_pairs={{0,3},{1,0},{2,1},{3,2},{4,7},{5,4},{6,5},{7,6},{8,11},{9,8},{10,9... | collective-permute-start | bytes 2949128 | tf_op jit(solution)/shard_map/ppermute | solution.py:191
  91.7 19.4 %collective-permute-done.5.refs_8_ = bf16[240,2048]{1,0:T(8,128)(2,1)S(1)} collective-permute-done((bf16[240,2048]{1,0:T(8,128)(2,1)}, bf16[240,2048]{1,0:T(8,128)(2,1)S(1)}, u32[]{:S(2)}, u32[]{:S(2)}) %collective-permute-start.5) | collective-permute-done | bytes 983072 | tf_op jit(solution)/shard_map/ppermute | solution.py:191
  111.1 1.0 copy-done.13
  112.1 2.2 %collective-permute-done.4.refs_7_ = bf16[288,2048]{1,0:T(8,128)(2,1)S(1)} collective-permute-done((bf16[288,2048]{1,0:T(8,128)(2,1)}, bf16[288,2048]{1,0:T(8,128)(2,1)S(1)}, u32[]{:S(2)}, u32[]{:S(2)}) %collective-permute-start.4) | collective-permute-done | bytes 1179680 | tf_op jit(solution)/shard_map/ppermute | solution.py:191
  114.3 1.1 copy-done.10
  116.0 11.3 %grad.1 = bf16[256,2048]{1,0:T(8,128)(2,1)} custom-call(bf16[512,2048]{1,0:T(8,128)(2,1)} %bitcast.17, bf16[1,176,2048]{2,1,0:T(8,128)(2,1)} %refs_0_.3, bf16[1,176,2048]{2,1,0:T(8,128)(2,1)} %refs_1_.3, bf16[1,176,2048]{2,1,0:T(8,128)(2,1)} %refs_2_.3, bf16[288,2048]{1,0:T(8,128)(2,1)} %collective-permute-done.refs_3_, bf16[240,2048]{1,0:T(8,128)(2,1)} %copy-done.11, ...), custom_call_target="tpu_custom_call" | custom-call | flops 3690987520 | bytes 8650752 | tf_op jit(solution)/shard_map/grad/pallas_call | solution.py:225
  127.3 16.0 %all_to_all.45 = bf16[4,64,2048]{2,1,0:T(8,128)(2,1)S(1)} all-to-all(bf16[4,64,2048]{2,1,0:T(8,128)(2,1)} %bitcast.18), channel_id=1, replica_groups={{0,4,8,12},{1,5,9,13},{2,6,10,14},{3,7,11,15},{16,20,24,28},{17,21,25,2..., dimensions={0} | all-to-all | bytes 2097152 | tf_op jit(solution)/shard_map/all_to_all | solution.py:205
  143.7 48.9 %all_to_all.46 = bf16[32,8,1024]{2,1,0:T(8,128)(2,1)S(1)} all-to-all(bf16[32,8,1024]{2,1,0:T(8,128)(2,1)S(1)} %bitcast.12), channel_id=1, replica_groups=mesh['ex'=32,'hid'=16] {'ex'}, dimensions={0} | all-to-all | bytes 1048576 | tf_op jit(solution)/shard_map/all_to_all | solution.py:246
  192.6 1.1 final.1
  (28 shorter events, 1.8 us)
Async XLA Ops:
  0.0 0.8 copy-start.3
  0.8 0.8 copy-start.4
  1.7 0.7 copy-start.5
  2.4 0.7 copy-start.7
  3.0 18.5 %copy-start.2 = (bf16[1,176,2048]{2,1,0:T(8,128)(2,1)S(1)}, bf16[1,176,2048]{2,1,0:T(8,128)(2,1)}, u32[]{:S(2)}) copy-start(bf16[1,176,2048]{2,1,0:T(8,128)(2,1)} %refs_2_.3) | copy-start | bytes 2162692
  4.7 16.9 %copy-start = (bf16[1,176,2048]{2,1,0:T(8,128)(2,1)S(1)}, bf16[1,176,2048]{2,1,0:T(8,128)(2,1)}, u32[]{:S(2)}) copy-start(bf16[1,176,2048]{2,1,0:T(8,128)(2,1)} %refs_0_.3) | copy-start | bytes 2162692
  4.7 16.9 %copy-start.1 = (bf16[1,176,2048]{2,1,0:T(8,128)(2,1)S(1)}, bf16[1,176,2048]{2,1,0:T(8,128)(2,1)}, u32[]{:S(2)}) copy-start(bf16[1,176,2048]{2,1,0:T(8,128)(2,1)} %refs_1_.3) | copy-start | bytes 2162692
  4.7 74.5 %all-to-all-start = ((bf16[32,8,2048]{2,1,0:T(8,128)(2,1)}), bf16[32,8,2048]{2,1,0:T(8,128)(2,1)S(1)}, u32[]{:S(2)}, u32[]{:S(2)}) async-start(bf16[32,8,2048]{2,1,0:T(8,128)(2,1)} %bitcast.2), calls=%async_computation | async-start | bytes 2097152 | tf_op jit(solution)/shard_map/all_to_all | solution.py:213
  22.5 55.6 %collective-permute-start.3 = (bf16[288,2048]{1,0:T(8,128)(2,1)S(1)}, bf16[288,2048]{1,0:T(8,128)(2,1)S(1)}, u32[]{:S(2)}, u32[]{:S(2)}) collective-permute-start(bf16[288,2048]{1,0:T(8,128)(2,1)S(1)} %get-tuple-element.12), channel_id=1, source_target_pairs={{0,3},{1,0},{2,1},{3,2},{4,7},{5,4},{6,5},{7,6},{8,11},{9,8},{10,9... | collective-permute-start | bytes 3538952 | tf_op jit(solution)/shard_map/ppermute | solution.py:191
  26.9 52.3 %collective-permute-start = (bf16[288,2048]{1,0:T(8,128)(2,1)S(1)}, bf16[288,2048]{1,0:T(8,128)(2,1)}, u32[]{:S(2)}, u32[]{:S(2)}) collective-permute-start(bf16[288,2048]{1,0:T(8,128)(2,1)S(1)} %get-tuple-element.12), channel_id=1, source_target_pairs={{0,1},{1,2},{2,3},{3,0},{4,5},{5,6},{6,7},{7,4},{8,9},{9,10},{10,1... | collective-permute-start | bytes 3538952 | tf_op jit(solution)/shard_map/ppermute | solution.py:191
  28.8 49.3 %collective-permute-start.2 = (bf16[240,2048]{1,0:T(8,128)(2,1)S(1)}, bf16[240,2048]{1,0:T(8,128)(2,1)S(1)}, u32[]{:S(2)}, u32[]{:S(2)}) collective-permute-start(bf16[240,2048]{1,0:T(8,128)(2,1)S(1)} %get-tuple-element.13), channel_id=1, source_target_pairs={{0,1},{1,2},{2,3},{3,0},{4,5},{5,6},{6,7},{7,4},{8,9},{9,10},{10,1... | collective-permute-start | bytes 2949128 | tf_op jit(solution)/shard_map/ppermute | solution.py:191
  30.9 47.2 %collective-permute-start.1 = (bf16[240,2048]{1,0:T(8,128)(2,1)S(1)}, bf16[240,2048]{1,0:T(8,128)(2,1)S(1)}, u32[]{:S(2)}, u32[]{:S(2)}) collective-permute-start(bf16[240,2048]{1,0:T(8,128)(2,1)S(1)} %get-tuple-element.13), channel_id=1, source_target_pairs={{0,3},{1,0},{2,1},{3,2},{4,7},{5,4},{6,5},{7,6},{8,11},{9,8},{10,9... | collective-permute-start | bytes 2949128 | tf_op jit(solution)/shard_map/ppermute | solution.py:191
  78.1 2.9 %copy-start.11 = (bf16[240,2048]{1,0:T(8,128)(2,1)}, bf16[240,2048]{1,0:T(8,128)(2,1)S(1)}, u32[]{:S(2)}) copy-start(bf16[240,2048]{1,0:T(8,128)(2,1)S(1)} %collective-permute-done.2.refs_4_) | copy-start | bytes 2949124
  78.1 1.1 copy-start.12
  79.2 1.8 copy-start.9
  81.0 33.3 %all-to-all-start.1 = ((bf16[4,128,2048]{2,1,0:T(8,128)(2,1)}), bf16[4,128,2048]{2,1,0:T(8,128)(2,1)S(1)}, u32[]{:S(2)}, u32[]{:S(2)}) async-start(bf16[4,128,2048]{2,1,0:T(8,128)(2,1)} %bitcast.4), calls=%async_computation.1 | async-start | bytes 4194304 | tf_op jit(solution)/shard_map/all_to_all | solution.py:205
  85.2 29.1 %collective-permute-start.4 = (bf16[288,2048]{1,0:T(8,128)(2,1)}, bf16[288,2048]{1,0:T(8,128)(2,1)S(1)}, u32[]{:S(2)}, u32[]{:S(2)}) collective-permute-start(bf16[288,2048]{1,0:T(8,128)(2,1)} %collective-permute-done.refs_3_), channel_id=1, source_target_pairs={{0,1},{1,2},{2,3},{3,0},{4,5},{5,6},{6,7},{7,4},{8,9},{9,10},{10,1... | collective-permute-start | bytes 3538952 | tf_op jit(solution)/shard_map/ppermute | solution.py:191
  87.1 24.0 %collective-permute-start.5 = (bf16[240,2048]{1,0:T(8,128)(2,1)}, bf16[240,2048]{1,0:T(8,128)(2,1)S(1)}, u32[]{:S(2)}, u32[]{:S(2)}) collective-permute-start(bf16[240,2048]{1,0:T(8,128)(2,1)} %copy-done.12), channel_id=1, source_target_pairs={{0,3},{1,0},{2,1},{3,2},{4,7},{5,4},{6,5},{7,6},{8,11},{9,8},{10,9... | collective-permute-start | bytes 2949128 | tf_op jit(solution)/shard_map/ppermute | solution.py:191
  111.1 1.0 copy-start.13
  114.3 1.1 copy-start.10
  114.3 1.7 copy-start.8
  143.3 49.3 %copy-start.6 = (s32[16,4]{0,1:T(4,128)S(1)}, s32[16,4]{0,1:T(4,128)}, u32[]{:S(2)}) copy-start(s32[16,4]{0,1:T(4,128)} %param.10) | copy-start | bytes 772

commit v5 on v4

--- a/solution.py
+++ b/solution.py
@@ -29,7 +29,17 @@
     return each, named, slot
 
 
-def pack_kernel(tok_ref, cot_ref, gate_ref, route_ref, out_ref):
+def pack_kernel(tok_in, cot_in, gate_in, route_in, out_ref, tok_ref, cot_ref, gate_ref, route_ref, sem):
+    copies = [
+        pltpu.make_async_copy(src, dst, sem.at[i])
+        for i, (src, dst) in enumerate(
+            ((route_in, route_ref), (gate_in, gate_ref), (tok_in, tok_ref), (cot_in, cot_ref))
+        )
+    ]
+    for cp in copies:
+        cp.start()
+    for cp in copies:
+        cp.wait()
     tok, width = tok_ref.shape
     top = route_ref.shape[0]
     rows = out_ref.shape[0]
@@ -79,54 +89,44 @@
 def grad_kernel(rows_in, *refs):
     n = 4
     own, moved, out = refs[:3], refs[3 : 2 * n + 1], refs[2 * n + 1]
-    x, y, wg, wu, wd, gate, upper, hidden, sem_r, sem_w = refs[2 * n + 2 :]
+    x, y, wg, wu, wd, sem_r, sem_w = refs[2 * n + 2 :]
     half = rows_in.shape[0] // (2 * n)
-    width = x.shape[1]
-    step = width // COLS
-    row_copies = []
-    for i in range(n):
-        for m, dst in enumerate((x, y)):
-            cp = pltpu.make_async_copy(
-                rows_in.at[pl.ds((2 * i + m) * half, half)], dst.at[pl.ds(i * half, half)], sem_r.at[2 * i + m]
+    unit, first = own[0].shape[1], moved[0].shape[0] // 3
+    each = 2 * n - 1
+
+    def rows_of(m, dst):
+        return [
+            pltpu.make_async_copy(
+                rows_in.at[pl.ds((2 * i + m) * half, half)], dst.at[pl.ds(i * half, half)], sem_r.at[m * n + i]
             )
+            for i in range(n)
+        ]
+
+    def weight(m, dst):
+        pieces = [(own[m].at[0], 0, unit)]
+        for i in range(each - 1):
+            size = first if i % 2 == 0 else unit - first
+            pieces.append((moved[i].at[pl.ds(m * size, size)], unit * (1 + i // 2) + first * (i % 2), size))
+        return [
+            pltpu.make_async_copy(src, dst.at[pl.ds(to, size)], sem_w.at[m * each + i])
+            for i, (src, to, size) in enumerate(pieces)
+        ]
+
+    stages = [rows_of(0, x) + weight(0, wg), weight(1, wu), rows_of(1, y) + weight(2, wd)]
+    for copies in stages:
+        for cp in copies:
             cp.start()
-            row_copies.append(cp)
-    unit = own[0].shape[1]
-    first = moved[0].shape[0] // 3
-    w_copies = []
-    for c in range(COLS):
-        mine = []
-        at = pl.ds(c * step, step)
-        for m, dst in enumerate((wg, wu, wd)):
-            pieces = [(own[m].at[0, :, at], 0, unit)]
-            for i in range(2 * n - 2):
-                size = first if i % 2 == 0 else unit - first
-                to = unit * (1 + i // 2) + first * (i % 2)
-                pieces.append((moved[i].at[pl.ds(m * size, size), at], to, size))
-            for i, (src, to, size) in enumerate(pieces):
-                cp = pltpu.make_async_copy(
-                    src, dst.at[pl.ds(to, size), at], sem_w.at[(c * 3 + m) * (2 * n - 1) + i]
-                )
-                cp.start()
-                mine.append(cp)
-        w_copies.append(mine)
-    for cp in row_copies:
-        cp.wait()
     dims = (((1,), (1,)), ((), ()))
-    for c in range(COLS):
-        for cp in w_copies[c]:
+    inner = []
+    for copies, left, right in zip(stages, (x, x, y), (wg, wu, wd)):
+        for cp in copies:
             cp.wait()
-        at = slice(c * step, (c + 1) * step)
-        for acc, left, right in ((gate, x, wg), (upper, x, wu), (hidden, y, wd)):
-            part = lax.dot_general(left[:, at], right[:, at], dims, preferred_element_type=F32)
-            if c == 0:
-                acc[...] = part
-            else:
-                acc[...] += part
-    gv, uv, hv = gate[...], upper[...], hidden[...]
+        inner.append(lax.dot_general(left[...], right[...], dims, preferred_element_type=F32))
+    gv, uv, hv = inner
     sig = jax.nn.sigmoid(gv)
     d_up = (hv * gv * sig).astype(BF)
     d_gate = (hv * uv * sig * (1.0 + gv * (1.0 - sig))).astype(BF)
+    step = x.shape[1] // COLS
     for c in range(COLS):
         at = slice(c * step, (c + 1) * step)
         out[:, at] = (
@@ -207,9 +207,16 @@
         )
 
     small = (1 << 26, 1 << 21)
-    packed = _call(pack_kernel, _shape(8 * n_ex, width), "pack", small)(
-        tokens, cotangent, gates.T, routes.T
-    )
+    packed = _call(pack_kernel, _shape(8 * n_ex, width), "pack", small, vmem=60,
+        in_specs=[pl.BlockSpec(memory_space=pl.ANY)] * 4,
+        scratch_shapes=[
+            pltpu.VMEM(tokens.shape, BF),
+            pltpu.VMEM(tokens.shape, BF),
+            pltpu.VMEM(gates.shape[::-1], F32),
+            pltpu.VMEM(routes.shape[::-1], jnp.int32),
+            pltpu.SemaphoreType.DMA((4,)),
+        ],
+    )(tokens, cotangent, gates.T, routes.T)
     arrived = lax.all_to_all(packed, "ex", split_axis=0, concat_axis=0, tiled=True)
     left_early, right_late = shift(early, 1), shift(late, -1)
     left_late, right_early = shift(late, 1), shift(early, -1)
@@ -234,13 +241,10 @@
             pltpu.VMEM((hid, width), BF),
             pltpu.VMEM((hid, width), BF),
             pltpu.VMEM((hid, width), BF),
-            pltpu.VMEM((rows, hid), F32),
-            pltpu.VMEM((rows, hid), F32),
-            pltpu.VMEM((rows, hid), F32),
             pltpu.SemaphoreType.DMA((8,)),
-            pltpu.SemaphoreType.DMA((21 * COLS,)),
+            pltpu.SemaphoreType.DMA((21,)),
         ],
-        vmem=56,
+        vmem=60,
     )(rows_all, w_gate, w_up, w_down, *weights)
     merged = _call(merge_kernel, _shape(8 * n_ex, width // 2), "merge", small)(over_y(parts))
     landed = lax.all_to_all(merged, "ex", split_axis=0, concat_axis=0, tiled=True)

time: 194 us -> 191 us (0.985)
  local copies, waits for them, and re-layouts: 6.79 us -> 3.77 us
    unnamed x28 -> x20, local copies, waits for them, and re-layouts: 6.79 us -> 3.77 us
where the time goes in v5:
time: 191 us; the launch traced here: 190 us
  blocking collectives  64.9 us (34%)
  waiting for transfers between devices  64.4 us (34%)
  starting transfers between devices  40.4 us (21%)
  Pallas kernels  16.6 us (9%)
  local copies, waits for them, and re-layouts  3.77 us (2%)
    ppermute x6, waiting for transfers between devices, shift(): lax.ppermute(v, 'hid', [(y * side + x, y * side + (x + d) % side) for y i...  64.4 us
    all_to_all x1, blocking collectives, per_device(): lax.all_to_all(merged, 'ex', split_axis=0, concat_axis=0, tiled=True)  48.9 us
    ppermute x6, starting transfers between devices, shift(): lax.ppermute(v, 'hid', [(y * side + x, y * side + (x + d) % side) for y i...  19.3 us
    all_to_all x1, starting transfers between devices, per_device(): lax.all_to_all(packed, 'ex', split_axis=0, concat_axis=0, tiled=True)  16.9 us
    all_to_all x1, blocking collectives, over_y(): lax.all_to_all(v, 'hid', split_axis=0, concat_axis=0, tiled=True, axis_in...  16 us
    pallas_call x1, Pallas kernels, per_device(): _call(grad_kernel, _shape(rows, width), 'grad', (10 * rows * hid * width,...  9.77 us
    all_to_all x1, starting transfers between devices, over_y(): lax.all_to_all(v, 'hid', split_axis=0, concat_axis=0, tiled=True, axis_in...  4.18 us
  transfers between devices with their start and end apart: 8, of which 3 were waited for; matrix products, arithmetic and copies ran while one was open for 0% of the time, Pallas kernels for 0%

profile of v5, /device:TPU:1, one launch (start us, length us, event | category | flops | bytes accessed | tf_op | source)
XLA Modules:
  0.0 190.2 jit_solution(6594339732466506455)
XLA Ops:
  0.0 2.6 %pack.1 = bf16[256,2048]{1,0:T(8,128)(2,1)} custom-call(bf16[16,2048]{1,0:T(8,128)(2,1)} %tok_in.1, bf16[16,2048]{1,0:T(8,128)(2,1)} %cot_in.1, f32[4,16]{1,0:T(4,128)} %bitcast.19, s32[4,16]{1,0:T(4,128)} %bitcast.14), custom_call_target="tpu_custom_call" | custom-call | flops 67108864 | bytes 2097152 | tf_op jit(solution)/shard_map/pack/pallas_call | solution.py:210
  2.6 0.0 copy-start
  2.7 16.9 %all-to-all-start = ((bf16[32,8,2048]{2,1,0:T(8,128)(2,1)}), bf16[32,8,2048]{2,1,0:T(8,128)(2,1)S(1)}, u32[]{:S(2)}, u32[]{:S(2)}) async-start(bf16[32,8,2048]{2,1,0:T(8,128)(2,1)} %bitcast.16), calls=%async_computation | async-start | bytes 2097152 | tf_op jit(solution)/shard_map/all_to_all | solution.py:220
  19.6 0.9 split.1
  20.5 4.4 %collective-permute-start.3 = (bf16[288,2048]{1,0:T(8,128)(2,1)S(1)}, bf16[288,2048]{1,0:T(8,128)(2,1)S(1)}, u32[]{:S(2)}, u32[]{:S(2)}) collective-permute-start(bf16[288,2048]{1,0:T(8,128)(2,1)S(1)} %get-tuple-element.12), channel_id=1, source_target_pairs={{0,3},{1,0},{2,1},{3,2},{4,7},{5,4},{6,5},{7,6},{8,11},{9,8},{10,9... | collective-permute-start | bytes 3538952 | tf_op jit(solution)/shard_map/ppermute | solution.py:191
  24.9 1.9 %collective-permute-start = (bf16[288,2048]{1,0:T(8,128)(2,1)S(1)}, bf16[288,2048]{1,0:T(8,128)(2,1)}, u32[]{:S(2)}, u32[]{:S(2)}) collective-permute-start(bf16[288,2048]{1,0:T(8,128)(2,1)S(1)} %get-tuple-element.12), channel_id=1, source_target_pairs={{0,1},{1,2},{2,3},{3,0},{4,5},{5,6},{6,7},{7,4},{8,9},{9,10},{10,1... | collective-permute-start | bytes 3538952 | tf_op jit(solution)/shard_map/ppermute | solution.py:191
  26.9 2.1 %collective-permute-start.2 = (bf16[240,2048]{1,0:T(8,128)(2,1)S(1)}, bf16[240,2048]{1,0:T(8,128)(2,1)S(1)}, u32[]{:S(2)}, u32[]{:S(2)}) collective-permute-start(bf16[240,2048]{1,0:T(8,128)(2,1)S(1)} %get-tuple-element.13), channel_id=1, source_target_pairs={{0,1},{1,2},{2,3},{3,0},{4,5},{5,6},{6,7},{7,4},{8,9},{9,10},{10,1... | collective-permute-start | bytes 2949128 | tf_op jit(solution)/shard_map/ppermute | solution.py:191
  29.0 4.4 %collective-permute-start.1 = (bf16[240,2048]{1,0:T(8,128)(2,1)S(1)}, bf16[240,2048]{1,0:T(8,128)(2,1)S(1)}, u32[]{:S(2)}, u32[]{:S(2)}) collective-permute-start(bf16[240,2048]{1,0:T(8,128)(2,1)S(1)} %get-tuple-element.13), channel_id=1, source_target_pairs={{0,3},{1,0},{2,1},{3,2},{4,7},{5,4},{6,5},{7,6},{8,11},{9,8},{10,9... | collective-permute-start | bytes 2949128 | tf_op jit(solution)/shard_map/ppermute | solution.py:191
  33.4 42.8 %collective-permute-done.2.refs_4_ = bf16[240,2048]{1,0:T(8,128)(2,1)S(1)} collective-permute-done((bf16[240,2048]{1,0:T(8,128)(2,1)S(1)}, bf16[240,2048]{1,0:T(8,128)(2,1)S(1)}, u32[]{:S(2)}, u32[]{:S(2)}) %collective-permute-start.2) | collective-permute-done | bytes 983072 | tf_op jit(solution)/shard_map/ppermute | solution.py:191
  76.1 1.1 copy-done.8
  77.2 1.8 unpack.1
  79.0 4.2 %all-to-all-start.1 = ((bf16[4,128,2048]{2,1,0:T(8,128)(2,1)}), bf16[4,128,2048]{2,1,0:T(8,128)(2,1)S(1)}, u32[]{:S(2)}, u32[]{:S(2)}) async-start(bf16[4,128,2048]{2,1,0:T(8,128)(2,1)} %bitcast.4), calls=%async_computation.1 | async-start | bytes 4194304 | tf_op jit(solution)/shard_map/all_to_all | solution.py:205
  83.2 1.9 %collective-permute-start.4 = (bf16[288,2048]{1,0:T(8,128)(2,1)}, bf16[288,2048]{1,0:T(8,128)(2,1)S(1)}, u32[]{:S(2)}, u32[]{:S(2)}) collective-permute-start(bf16[288,2048]{1,0:T(8,128)(2,1)} %collective-permute-done.refs_3_), channel_id=1, source_target_pairs={{0,1},{1,2},{2,3},{3,0},{4,5},{5,6},{6,7},{7,4},{8,9},{9,10},{10,1... | collective-permute-start | bytes 3538952 | tf_op jit(solution)/shard_map/ppermute | solution.py:191
  85.1 4.6 %collective-permute-start.5 = (bf16[240,2048]{1,0:T(8,128)(2,1)}, bf16[240,2048]{1,0:T(8,128)(2,1)S(1)}, u32[]{:S(2)}, u32[]{:S(2)}) collective-permute-start(bf16[240,2048]{1,0:T(8,128)(2,1)} %copy-done.8), channel_id=1, source_target_pairs={{0,3},{1,0},{2,1},{3,2},{4,7},{5,4},{6,5},{7,6},{8,11},{9,8},{10,9... | collective-permute-start | bytes 2949128 | tf_op jit(solution)/shard_map/ppermute | solution.py:191
  89.7 19.4 %collective-permute-done.5.refs_8_ = bf16[240,2048]{1,0:T(8,128)(2,1)S(1)} collective-permute-done((bf16[240,2048]{1,0:T(8,128)(2,1)}, bf16[240,2048]{1,0:T(8,128)(2,1)S(1)}, u32[]{:S(2)}, u32[]{:S(2)}) %collective-permute-start.5) | collective-permute-done | bytes 983072 | tf_op jit(solution)/shard_map/ppermute | solution.py:191
  109.1 1.0 copy-done.9
  110.1 2.2 %collective-permute-done.4.refs_7_ = bf16[288,2048]{1,0:T(8,128)(2,1)S(1)} collective-permute-done((bf16[288,2048]{1,0:T(8,128)(2,1)}, bf16[288,2048]{1,0:T(8,128)(2,1)S(1)}, u32[]{:S(2)}, u32[]{:S(2)}) %collective-permute-start.4) | collective-permute-done | bytes 1179680 | tf_op jit(solution)/shard_map/ppermute | solution.py:191
  112.3 1.0 copy-done.6
  113.4 0.7 copy-done.4
  114.0 9.8 %grad.1 = bf16[256,2048]{1,0:T(8,128)(2,1)} custom-call(bf16[512,2048]{1,0:T(8,128)(2,1)} %bitcast.17, bf16[1,176,2048]{2,1,0:T(8,128)(2,1)} %refs_0_.3, bf16[1,176,2048]{2,1,0:T(8,128)(2,1)} %refs_1_.3, bf16[1,176,2048]{2,1,0:T(8,128)(2,1)} %refs_2_.3, bf16[288,2048]{1,0:T(8,128)(2,1)} %collective-permute-done.refs_3_, bf16[240,2048]{1,0:T(8,128)(2,1)} %copy-done.7, ...), custom_call_target="tpu_custom_call" | custom-call | flops 3690987520 | bytes 8650752 | tf_op jit(solution)/shard_map/grad/pallas_call | solution.py:232
  123.8 16.0 %all_to_all.45 = bf16[4,64,2048]{2,1,0:T(8,128)(2,1)S(1)} all-to-all(bf16[4,64,2048]{2,1,0:T(8,128)(2,1)} %bitcast.18), channel_id=1, replica_groups={{0,4,8,12},{1,5,9,13},{2,6,10,14},{3,7,11,15},{16,20,24,28},{17,21,25,2..., dimensions={0} | all-to-all | bytes 2097152 | tf_op jit(solution)/shard_map/all_to_all | solution.py:205
  139.8 0.4 merge.1
  140.2 48.9 %all_to_all.46 = bf16[32,8,1024]{2,1,0:T(8,128)(2,1)S(1)} all-to-all(bf16[32,8,1024]{2,1,0:T(8,128)(2,1)S(1)} %bitcast.12), channel_id=1, replica_groups=mesh['ex'=32,'hid'=16] {'ex'}, dimensions={0} | all-to-all | bytes 1048576 | tf_op jit(solution)/shard_map/all_to_all | solution.py:250
  189.1 1.1 final.1
  (20 shorter events, 0.0 us)
Async XLA Ops:
  0.0 19.6 %copy-start.2 = (bf16[1,176,2048]{2,1,0:T(8,128)(2,1)S(1)}, bf16[1,176,2048]{2,1,0:T(8,128)(2,1)}, u32[]{:S(2)}) copy-start(bf16[1,176,2048]{2,1,0:T(8,128)(2,1)} %refs_2_.3) | copy-start | bytes 2162692
  2.6 16.9 %copy-start = (bf16[1,176,2048]{2,1,0:T(8,128)(2,1)S(1)}, bf16[1,176,2048]{2,1,0:T(8,128)(2,1)}, u32[]{:S(2)}) copy-start(bf16[1,176,2048]{2,1,0:T(8,128)(2,1)} %refs_0_.3) | copy-start | bytes 2162692
  2.6 16.9 %copy-start.1 = (bf16[1,176,2048]{2,1,0:T(8,128)(2,1)S(1)}, bf16[1,176,2048]{2,1,0:T(8,128)(2,1)}, u32[]{:S(2)}) copy-start(bf16[1,176,2048]{2,1,0:T(8,128)(2,1)} %refs_1_.3) | copy-start | bytes 2162692
  2.7 74.6 %all-to-all-start = ((bf16[32,8,2048]{2,1,0:T(8,128)(2,1)}), bf16[32,8,2048]{2,1,0:T(8,128)(2,1)S(1)}, u32[]{:S(2)}, u32[]{:S(2)}) async-start(bf16[32,8,2048]{2,1,0:T(8,128)(2,1)} %bitcast.16), calls=%async_computation | async-start | bytes 2097152 | tf_op jit(solution)/shard_map/all_to_all | solution.py:220
  20.5 55.6 %collective-permute-start.3 = (bf16[288,2048]{1,0:T(8,128)(2,1)S(1)}, bf16[288,2048]{1,0:T(8,128)(2,1)S(1)}, u32[]{:S(2)}, u32[]{:S(2)}) collective-permute-start(bf16[288,2048]{1,0:T(8,128)(2,1)S(1)} %get-tuple-element.12), channel_id=1, source_target_pairs={{0,3},{1,0},{2,1},{3,2},{4,7},{5,4},{6,5},{7,6},{8,11},{9,8},{10,9... | collective-permute-start | bytes 3538952 | tf_op jit(solution)/shard_map/ppermute | solution.py:191
  24.9 52.3 %collective-permute-start = (bf16[288,2048]{1,0:T(8,128)(2,1)S(1)}, bf16[288,2048]{1,0:T(8,128)(2,1)}, u32[]{:S(2)}, u32[]{:S(2)}) collective-permute-start(bf16[288,2048]{1,0:T(8,128)(2,1)S(1)} %get-tuple-element.12), channel_id=1, source_target_pairs={{0,1},{1,2},{2,3},{3,0},{4,5},{5,6},{6,7},{7,4},{8,9},{9,10},{10,1... | collective-permute-start | bytes 3538952 | tf_op jit(solution)/shard_map/ppermute | solution.py:191
  26.9 49.3 %collective-permute-start.2 = (bf16[240,2048]{1,0:T(8,128)(2,1)S(1)}, bf16[240,2048]{1,0:T(8,128)(2,1)S(1)}, u32[]{:S(2)}, u32[]{:S(2)}) collective-permute-start(bf16[240,2048]{1,0:T(8,128)(2,1)S(1)} %get-tuple-element.13), channel_id=1, source_target_pairs={{0,1},{1,2},{2,3},{3,0},{4,5},{5,6},{6,7},{7,4},{8,9},{9,10},{10,1... | collective-permute-start | bytes 2949128 | tf_op jit(solution)/shard_map/ppermute | solution.py:191
  29.0 47.2 %collective-permute-start.1 = (bf16[240,2048]{1,0:T(8,128)(2,1)S(1)}, bf16[240,2048]{1,0:T(8,128)(2,1)S(1)}, u32[]{:S(2)}, u32[]{:S(2)}) collective-permute-start(bf16[240,2048]{1,0:T(8,128)(2,1)S(1)} %get-tuple-element.13), channel_id=1, source_target_pairs={{0,3},{1,0},{2,1},{3,2},{4,7},{5,4},{6,5},{7,6},{8,11},{9,8},{10,9... | collective-permute-start | bytes 2949128 | tf_op jit(solution)/shard_map/ppermute | solution.py:191
  76.1 2.9 %copy-start.7 = (bf16[240,2048]{1,0:T(8,128)(2,1)}, bf16[240,2048]{1,0:T(8,128)(2,1)S(1)}, u32[]{:S(2)}) copy-start(bf16[240,2048]{1,0:T(8,128)(2,1)S(1)} %collective-permute-done.2.refs_4_) | copy-start | bytes 2949124
  76.1 1.1 copy-start.8
  77.2 1.8 copy-start.5
  79.0 33.3 %all-to-all-start.1 = ((bf16[4,128,2048]{2,1,0:T(8,128)(2,1)}), bf16[4,128,2048]{2,1,0:T(8,128)(2,1)S(1)}, u32[]{:S(2)}, u32[]{:S(2)}) async-start(bf16[4,128,2048]{2,1,0:T(8,128)(2,1)} %bitcast.4), calls=%async_computation.1 | async-start | bytes 4194304 | tf_op jit(solution)/shard_map/all_to_all | solution.py:205
  83.2 29.1 %collective-permute-start.4 = (bf16[288,2048]{1,0:T(8,128)(2,1)}, bf16[288,2048]{1,0:T(8,128)(2,1)S(1)}, u32[]{:S(2)}, u32[]{:S(2)}) collective-permute-start(bf16[288,2048]{1,0:T(8,128)(2,1)} %collective-permute-done.refs_3_), channel_id=1, source_target_pairs={{0,1},{1,2},{2,3},{3,0},{4,5},{5,6},{6,7},{7,4},{8,9},{9,10},{10,1... | collective-permute-start | bytes 3538952 | tf_op jit(solution)/shard_map/ppermute | solution.py:191
  85.1 24.0 %collective-permute-start.5 = (bf16[240,2048]{1,0:T(8,128)(2,1)}, bf16[240,2048]{1,0:T(8,128)(2,1)S(1)}, u32[]{:S(2)}, u32[]{:S(2)}) collective-permute-start(bf16[240,2048]{1,0:T(8,128)(2,1)} %copy-done.8), channel_id=1, source_target_pairs={{0,3},{1,0},{2,1},{3,2},{4,7},{5,4},{6,5},{7,6},{8,11},{9,8},{10,9... | collective-permute-start | bytes 2949128 | tf_op jit(solution)/shard_map/ppermute | solution.py:191
  109.1 1.0 copy-start.9
  112.3 1.0 copy-start.6
  112.3 1.7 copy-start.4
  139.8 49.3 %copy-start.3 = (s32[16,4]{0,1:T(4,128)S(1)}, s32[16,4]{0,1:T(4,128)}, u32[]{:S(2)}) copy-start(s32[16,4]{0,1:T(4,128)} %param.10) | copy-start | bytes 772

commit v6 on v5

--- a/solution.py
+++ b/solution.py
@@ -72,67 +72,80 @@
         cp.wait()
 
 
-def unpack_kernel(in_ref, out_ref):
-    rows = out_ref.shape[0] // 4
+def unpack_kernel(in_ref, own_ref, other_ref):
+    g = lax.axis_index("hid") // 8
+    rows = own_ref.shape[0]
     half = rows // 2
     q = _iota((rows, in_ref.shape[0]), 0)
     r = _iota((rows, in_ref.shape[0]), 1)
     want = ((q % half) // 2) * 8 + (q // half) * 2 + q % 2
     data = in_ref[...]
-    for local in range(2):
-        pick = _select(r == want + 4 * local).astype(BF)
-        mine = jnp.dot(pick, data, preferred_element_type=F32).astype(BF)
-        for y in (2 * local, 2 * local + 1):
-            out_ref[y * rows : (y + 1) * rows, :] = mine
-
-
-def grad_kernel(rows_in, *refs):
+    for o, ref in enumerate((own_ref, other_ref)):
+        pick = _select(r == want + 4 * jnp.bitwise_xor(g, o)).astype(BF)
+        ref[...] = jnp.dot(pick, data, preferred_element_type=F32).astype(BF)
+
+
+def _parts(unit, first):
+    return [(0, unit)] + [
+        (unit * (1 + i // 2) + first * (i % 2), first if i % 2 == 0 else unit - first) for i in range(6)
+    ]
+
+
+def stage_kernel(*refs):
+    own, moved, mains, rests, sem = refs[:3], refs[3:7], refs[7:10], refs[10:13], refs[13]
+    unit, first = own[0].shape[1], moved[0].shape[0] // 3
+    main = mains[0].shape[0]
+    copies = []
+    for m in range(3):
+        for i, (at, size) in enumerate(_parts(unit, first)[:5]):
+            src = own[m].at[0] if i == 0 else moved[i - 1].at[pl.ds(m * size, size)]
+            fit = min(size, main - at)
+            copies.append((src.at[pl.ds(0, fit)], mains[m].at[pl.ds(at, fit)]))
+            if fit < size:
+                copies.append((src.at[pl.ds(fit, size - fit)], rests[m]))
+    copies = [pltpu.make_async_copy(src, dst, sem.at[i]) for i, (src, dst) in enumerate(copies)]
+    for cp in copies:
+        cp.start()
+    for cp in copies:
+        cp.wait()
+
+
+def grad_kernel(*refs):
     n = 4
-    own, moved, out = refs[:3], refs[3 : 2 * n + 1], refs[2 * n + 1]
-    x, y, wg, wu, wd, sem_r, sem_w = refs[2 * n + 2 :]
-    half = rows_in.shape[0] // (2 * n)
-    unit, first = own[0].shape[1], moved[0].shape[0] // 3
-    each = 2 * n - 1
-
-    def rows_of(m, dst):
-        return [
-            pltpu.make_async_copy(
-                rows_in.at[pl.ds((2 * i + m) * half, half)], dst.at[pl.ds(i * half, half)], sem_r.at[m * n + i]
-            )
-            for i in range(n)
-        ]
-
-    def weight(m, dst):
-        pieces = [(own[m].at[0], 0, unit)]
-        for i in range(each - 1):
-            size = first if i % 2 == 0 else unit - first
-            pieces.append((moved[i].at[pl.ds(m * size, size)], unit * (1 + i // 2) + first * (i % 2), size))
-        return [
-            pltpu.make_async_copy(src, dst.at[pl.ds(to, size)], sem_w.at[m * each + i])
-            for i, (src, to, size) in enumerate(pieces)
-        ]
-
-    stages = [rows_of(0, x) + weight(0, wg), weight(1, wu), rows_of(1, y) + weight(2, wd)]
-    for copies in stages:
-        for cp in copies:
-            cp.start()
+    rows_in, mains, rests, last, out = refs[:n], refs[n : n + 3], refs[n + 3 : n + 6], refs[n + 6 : n + 8], refs[n + 8]
+    x, y, tails = refs[n + 9], refs[n + 10], refs[n + 11 :]
+    half = rows_in[0].shape[0] // 2
+    me = lax.axis_index("hid") // n
+    for i in range(n):
+        at = pl.ds(pl.multiple_of(jnp.bitwise_xor(me, i) * half, half), half)
+        x[at, :] = rows_in[i][0:half, :]
+        y[at, :] = rows_in[i][half : 2 * half, :]
+    for m in range(3):
+        at = rests[m].shape[0]
+        tails[m][0:at, :] = rests[m][...]
+        for piece in last:
+            size = piece.shape[0] // 3
+            tails[m][at : at + size, :] = piece[m * size : (m + 1) * size, :]
+            at += size
     dims = (((1,), (1,)), ((), ()))
+    dot = lambda a, w: lax.dot_general(a[...], w[...], dims, preferred_element_type=F32)
     inner = []
-    for copies, left, right in zip(stages, (x, x, y), (wg, wu, wd)):
-        for cp in copies:
-            cp.wait()
-        inner.append(lax.dot_general(left[...], right[...], dims, preferred_element_type=F32))
-    gv, uv, hv = inner
-    sig = jax.nn.sigmoid(gv)
-    d_up = (hv * gv * sig).astype(BF)
-    d_gate = (hv * uv * sig * (1.0 + gv * (1.0 - sig))).astype(BF)
-    step = x.shape[1] // COLS
+    for w in (mains, tails):
+        gv, uv, hv = dot(x, w[0]), dot(x, w[1]), dot(y, w[2])
+        sig = jax.nn.sigmoid(gv)
+        d_up = (hv * gv * sig).astype(BF)
+        d_gate = (hv * uv * sig * (1.0 + gv * (1.0 - sig))).astype(BF)
+        inner.append((d_gate, d_up))
+    width = out.shape[1]
+    step = width // COLS
     for c in range(COLS):
         at = slice(c * step, (c + 1) * step)
-        out[:, at] = (
-            jnp.dot(d_gate, wg[:, at], preferred_element_type=F32)
-            + jnp.dot(d_up, wu[:, at], preferred_element_type=F32)
-        ).astype(BF)
+        total = None
+        for (d_gate, d_up), w in zip(inner, (mains, tails)):
+            for d, ref in ((d_gate, w[0]), (d_up, w[1])):
+                part = jnp.dot(d, ref[:, at], preferred_element_type=F32)
+                total = part if total is None else total + part
+        out[:, at] = total.astype(BF)
 
 
 def merge_kernel(in_ref, out_ref):
@@ -223,29 +236,33 @@
     arrived, left_early, right_late, left_late, right_early = lax.optimization_barrier(
         (arrived, left_early, right_late, left_late, right_early)
     )
-    weights = [left_early, left_late, right_early, right_late, shift(left_early, 1), shift(right_late, -1)]
-    spread = _call(unpack_kernel, _shape(16 * n_ex, width), "unpack", small)(arrived)
-    rows_all = over_y(spread)
-
+    last = [shift(left_early, 1), shift(right_late, -1)]
+    own, other = _call(unpack_kernel, (_shape(4 * n_ex, width),) * 2, "unpack", small)(arrived)
+    flip = lambda v, d: lax.ppermute(
+        v, "hid", [(y * side + x, (y ^ d) * side + x) for y in range(side) for x in range(side)]
+    )
+    rows_all = [own, flip(own, 1), flip(other, 2), flip(other, 3)]
     hid = side * unit
+    main = 3 * unit // 256 * 256
+    rest = 3 * unit - main
+    _, *pieces = lax.optimization_barrier((own, left_early, left_late, right_early, right_late))
+    staged = _call(
+        stage_kernel,
+        (_shape(main, width),) * 3 + (_shape(rest, width),) * 3,
+        "stage",
+        (0, 24 * 3 * unit * width),
+        in_specs=[pl.BlockSpec(memory_space=pl.ANY)] * 7,
+        scratch_shapes=[pltpu.SemaphoreType.DMA((18,))],
+    )(w_gate, w_up, w_down, *pieces)
     rows = 8 * n_ex
     parts = _call(
         grad_kernel,
         _shape(rows, width),
         "grad",
         (10 * rows * hid * width, 6 * hid * width),
-        in_specs=[pl.BlockSpec(memory_space=pl.ANY)] * 10,
-        scratch_shapes=[
-            pltpu.VMEM((rows, width), BF),
-            pltpu.VMEM((rows, width), BF),
-            pltpu.VMEM((hid, width), BF),
-            pltpu.VMEM((hid, width), BF),
-            pltpu.VMEM((hid, width), BF),
-            pltpu.SemaphoreType.DMA((8,)),
-            pltpu.SemaphoreType.DMA((21,)),
-        ],
-        vmem=60,
-    )(rows_all, w_gate, w_up, w_down, *weights)
+        vmem=36,
+        scratch_shapes=[pltpu.VMEM((rows, width), BF)] * 2 + [pltpu.VMEM((rest + unit, width), BF)] * 3,
+    )(*rows_all, *staged, *last)
     merged = _call(merge_kernel, _shape(8 * n_ex, width // 2), "merge", small)(over_y(parts))
     landed = lax.all_to_all(merged, "ex", split_axis=0, concat_axis=0, tiled=True)
     return _call(final_kernel, _shape(tok, width), "final", small)(landed, routes.T)

time: 191 us -> 188 us (0.984)
  waiting for transfers between devices: 64.4 us -> 58.4 us
  starting transfers between devices: 40.4 us -> 45 us
  Pallas kernels: 16.6 us -> 12.7 us
  local copies, waits for them, and re-layouts: 3.77 us -> 7.09 us
    ppermute x6, waiting for transfers between devices: 64.4 us -> 41.3 us  [shift(): lax.ppermute(v, 'hid', [(y * side + x, y * side + (x + d) % side) for y i...]
    ppermute x0 -> x3, waiting for transfers between devices: none -> 17.1 us  [per_device(): lax.ppermute(v, 'hid', [(y * side + x, (y ^ d) * side + x) for y in range...]
    ppermute x0 -> x3, starting transfers between devices: none -> 9.66 us  [per_device(): lax.ppermute(v, 'hid', [(y * side + x, (y ^ d) * side + x) for y in range...]
    pallas_call x1, Pallas kernels: 9.77 us -> 4.43 us  [per_device(): _call(grad_kernel, _shape(rows, width), 'grad', (10 * rows * hid * width,...]
    all_to_all x1 -> x0, starting transfers between devices: 4.18 us -> none  [over_y(): lax.all_to_all(v, 'hid', split_axis=0, concat_axis=0, tiled=True, axis_in...]
    unnamed x20 -> x24, local copies, waits for them, and re-layouts: 3.77 us -> 7.09 us
  transfers between devices with their start and end apart: 8 -> 10, of which waited for: 3 -> 3; matrix products, arithmetic and copies ran while one was open for 0% -> 0% of each run, Pallas kernels for 0% -> 2%
where the time goes in v6:
time: 188 us; the launch traced here: 187 us
  blocking collectives  63.5 us (34%)
  waiting for transfers between devices  58.4 us (31%)
  starting transfers between devices  45 us (24%)
  Pallas kernels  12.7 us (7%)
  local copies, waits for them, and re-layouts  7.09 us (4%)
    all_to_all x1, blocking collectives, per_device(): lax.all_to_all(merged, 'ex', split_axis=0, concat_axis=0, tiled=True)  49 us
    ppermute x6, waiting for transfers between devices, shift(): lax.ppermute(v, 'hid', [(y * side + x, y * side + (x + d) % side) for y i...  41.3 us
    ppermute x6, starting transfers between devices, shift(): lax.ppermute(v, 'hid', [(y * side + x, y * side + (x + d) % side) for y i...  18.4 us
    ppermute x3, waiting for transfers between devices, per_device(): lax.ppermute(v, 'hid', [(y * side + x, (y ^ d) * side + x) for y in range...  17.1 us
    all_to_all x1, starting transfers between devices, per_device(): lax.all_to_all(packed, 'ex', split_axis=0, concat_axis=0, tiled=True)  16.9 us
    all_to_all x1, blocking collectives, over_y(): lax.all_to_all(v, 'hid', split_axis=0, concat_axis=0, tiled=True, axis_in...  14.5 us
    ppermute x3, starting transfers between devices, per_device(): lax.ppermute(v, 'hid', [(y * side + x, (y ^ d) * side + x) for y in range...  9.66 us
    unnamed x24, local copies, waits for them, and re-layouts  7.09 us
  transfers between devices with their start and end apart: 10, of which 3 were waited for; matrix products, arithmetic and copies ran while one was open for 0% of the time, Pallas kernels for 2%

profile of v6, /device:TPU:1, one launch (start us, length us, event | category | flops | bytes accessed | tf_op | source)
XLA Modules:
  0.0 186.9 jit_solution(18319695381963201241)
XLA Ops:
  0.0 2.6 %pack.1 = bf16[256,2048]{1,0:T(8,128)(2,1)} custom-call(bf16[16,2048]{1,0:T(8,128)(2,1)} %tok_in.1, bf16[16,2048]{1,0:T(8,128)(2,1)} %cot_in.1, f32[4,16]{1,0:T(4,128)} %bitcast.16, s32[4,16]{1,0:T(4,128)} %bitcast.13), custom_call_target="tpu_custom_call" | custom-call | flops 67108864 | bytes 2097152 | tf_op jit(solution)/shard_map/pack/pallas_call | solution.py:223
  2.7 16.9 %all-to-all-start = ((bf16[32,8,2048]{2,1,0:T(8,128)(2,1)}), bf16[32,8,2048]{2,1,0:T(8,128)(2,1)S(1)}, u32[]{:S(2)}, u32[]{:S(2)}) async-start(bf16[32,8,2048]{2,1,0:T(8,128)(2,1)} %bitcast.15), calls=%async_computation | async-start | bytes 2097152 | tf_op jit(solution)/shard_map/all_to_all | solution.py:233
  20.5 3.1 %collective-permute-start = (bf16[288,2048]{1,0:T(8,128)(2,1)S(1)}, bf16[288,2048]{1,0:T(8,128)(2,1)S(1)}, u32[]{:S(2)}, u32[]{:S(2)}) collective-permute-start(bf16[288,2048]{1,0:T(8,128)(2,1)S(1)} %get-tuple-element.24), channel_id=1, source_target_pairs={{0,1},{1,2},{2,3},{3,0},{4,5},{5,6},{6,7},{7,4},{8,9},{9,10},{10,1... | collective-permute-start | bytes 3538952 | tf_op jit(solution)/shard_map/ppermute | solution.py:204
  23.7 3.4 %collective-permute-start.3 = (bf16[288,2048]{1,0:T(8,128)(2,1)S(1)}, bf16[288,2048]{1,0:T(8,128)(2,1)S(1)}, u32[]{:S(2)}, u32[]{:S(2)}) collective-permute-start(bf16[288,2048]{1,0:T(8,128)(2,1)S(1)} %get-tuple-element.24), channel_id=1, source_target_pairs={{0,3},{1,0},{2,1},{3,2},{4,7},{5,4},{6,5},{7,6},{8,11},{9,8},{10,9... | collective-permute-start | bytes 3538952 | tf_op jit(solution)/shard_map/ppermute | solution.py:204
  27.0 3.2 %collective-permute-start.1 = (bf16[240,2048]{1,0:T(8,128)(2,1)S(1)}, bf16[240,2048]{1,0:T(8,128)(2,1)S(1)}, u32[]{:S(2)}, u32[]{:S(2)}) collective-permute-start(bf16[240,2048]{1,0:T(8,128)(2,1)S(1)} %get-tuple-element.25), channel_id=1, source_target_pairs={{0,3},{1,0},{2,1},{3,2},{4,7},{5,4},{6,5},{7,6},{8,11},{9,8},{10,9... | collective-permute-start | bytes 2949128 | tf_op jit(solution)/shard_map/ppermute | solution.py:204
  30.2 2.1 %collective-permute-start.2 = (bf16[240,2048]{1,0:T(8,128)(2,1)S(1)}, bf16[240,2048]{1,0:T(8,128)(2,1)S(1)}, u32[]{:S(2)}, u32[]{:S(2)}) collective-permute-start(bf16[240,2048]{1,0:T(8,128)(2,1)S(1)} %get-tuple-element.25), channel_id=1, source_target_pairs={{0,1},{1,2},{2,3},{3,0},{4,5},{5,6},{6,7},{7,4},{8,9},{9,10},{10,1... | collective-permute-start | bytes 2949128 | tf_op jit(solution)/shard_map/ppermute | solution.py:204
  32.3 41.3 %collective-permute-done.1.refs_6_ = bf16[240,2048]{1,0:T(8,128)(2,1)S(1)} collective-permute-done((bf16[240,2048]{1,0:T(8,128)(2,1)S(1)}, bf16[240,2048]{1,0:T(8,128)(2,1)S(1)}, u32[]{:S(2)}, u32[]{:S(2)}) %collective-permute-start.1) | collective-permute-done | bytes 983072 | tf_op jit(solution)/shard_map/ppermute | solution.py:204
  73.6 1.0 copy-done.9
  74.9 1.0 copy-done.3
  77.0 3.2 %collective-permute-start.7 = (bf16[288,2048]{1,0:T(8,128)(2,1)}, bf16[288,2048]{1,0:T(8,128)(2,1)S(1)}, u32[]{:S(2)}, u32[]{:S(2)}) collective-permute-start(bf16[288,2048]{1,0:T(8,128)(2,1)} %copy-done.3), channel_id=1, source_target_pairs={{0,1},{1,2},{2,3},{3,0},{4,5},{5,6},{6,7},{7,4},{8,9},{9,10},{10,1... | collective-permute-start | bytes 3538952 | tf_op jit(solution)/shard_map/ppermute | solution.py:204
  80.2 3.4 %collective-permute-start.8 = (bf16[240,2048]{1,0:T(8,128)(2,1)}, bf16[240,2048]{1,0:T(8,128)(2,1)S(1)}, u32[]{:S(2)}, u32[]{:S(2)}) collective-permute-start(bf16[240,2048]{1,0:T(8,128)(2,1)} %copy-done.7), channel_id=1, source_target_pairs={{0,3},{1,0},{2,1},{3,2},{4,7},{5,4},{6,5},{7,6},{8,11},{9,8},{10,9... | collective-permute-start | bytes 2949128 | tf_op jit(solution)/shard_map/ppermute | solution.py:204
  84.1 3.2 %collective-permute-start.4 = (bf16[128,2048]{1,0:T(8,128)(2,1)S(1)}, bf16[128,2048]{1,0:T(8,128)(2,1)S(1)}, u32[]{:S(2)}, u32[]{:S(2)}) collective-permute-start(bf16[128,2048]{1,0:T(8,128)(2,1)S(1)} %get-tuple-element.27.refs_0_), channel_id=1, source_target_pairs={{0,4},{1,5},{2,6},{3,7},{4,0},{5,1},{6,2},{7,3},{8,12},{9,13},{10,... | collective-permute-start | bytes 1572872 | tf_op jit(solution)/shard_map/ppermute | solution.py:241
  87.3 4.5 %collective-permute-start.5 = (bf16[128,2048]{1,0:T(8,128)(2,1)S(1)}, bf16[128,2048]{1,0:T(8,128)(2,1)S(1)}, u32[]{:S(2)}, u32[]{:S(2)}) collective-permute-start(bf16[128,2048]{1,0:T(8,128)(2,1)S(1)} %get-tuple-element.28), channel_id=1, source_target_pairs={{0,8},{1,9},{2,10},{3,11},{4,12},{5,13},{6,14},{7,15},{8,0},{9,1},... | collective-permute-start | bytes 1572872 | tf_op jit(solution)/shard_map/ppermute | solution.py:241
  91.8 1.9 %collective-permute-start.6 = (bf16[128,2048]{1,0:T(8,128)(2,1)S(1)}, bf16[128,2048]{1,0:T(8,128)(2,1)S(1)}, u32[]{:S(2)}, u32[]{:S(2)}) collective-permute-start(bf16[128,2048]{1,0:T(8,128)(2,1)S(1)} %get-tuple-element.28), channel_id=1, source_target_pairs={{0,12},{1,13},{2,14},{3,15},{4,8},{5,9},{6,10},{7,11},{8,4},{9,5},... | collective-permute-start | bytes 1572872 | tf_op jit(solution)/shard_map/ppermute | solution.py:241
  93.8 1.3 copy-done.4
  95.1 1.3 copy-done.6
  96.3 1.2 copy-done.10
  97.5 2.8 %stage.1 = (bf16[512,2048]{1,0:T(8,128)(2,1)S(1)}, bf16[512,2048]{1,0:T(8,128)(2,1)S(1)}, bf16[512,2048]{1,0:T(8,128)(2,1)S(1)}, bf16[16,2048]{1,0:T(8,128)(2,1)...) custom-call(bf16[1,176,2048]{2,1,0:T(8,128)(2,1)S(1)} %copy-done, bf16[1,176,2048]{2,1,0:T(8,128)(2,1)S(1)} %copy-done.1, ...), custom_call_target="tpu_custom_call" | custom-call | bytes 25952256 | tf_op jit(solution)/shard_map/stage/pallas_call | solution.py:249
  100.3 10.9 %collective-permute-done.5.refs_2_ = bf16[128,2048]{1,0:T(8,128)(2,1)S(1)} collective-permute-done((bf16[128,2048]{1,0:T(8,128)(2,1)S(1)}, bf16[128,2048]{1,0:T(8,128)(2,1)S(1)}, u32[]{:S(2)}, u32[]{:S(2)}) %collective-permute-start.5) | collective-permute-done | bytes 524320 | tf_op jit(solution)/shard_map/ppermute | solution.py:241
  111.2 6.2 %collective-permute-done.6.refs_3_ = bf16[128,2048]{1,0:T(8,128)(2,1)S(1)} collective-permute-done((bf16[128,2048]{1,0:T(8,128)(2,1)S(1)}, bf16[128,2048]{1,0:T(8,128)(2,1)S(1)}, u32[]{:S(2)}, u32[]{:S(2)}) %collective-permute-start.6) | collective-permute-done | bytes 524320 | tf_op jit(solution)/shard_map/ppermute | solution.py:241
  117.5 4.4 %grad.1 = bf16[256,2048]{1,0:T(8,128)(2,1)S(1)} custom-call(bf16[128,2048]{1,0:T(8,128)(2,1)S(1)} %get-tuple-element.27.refs_0_, bf16[128,2048]{1,0:T(8,128)(2,1)S(1)} %collective-permute-done.4.refs_1_, bf16[128,2048]{1,0:T(8,128)(2,1)S(1)} %collective-permute-done.5.refs_2_, bf16[128,2048]{1,0:T(8,128)(2,1)S(1)} %collective-permute-done.6.refs_3_, ...), custom_call_target="tpu_custom_call" | custom-call | flops 3690987520 | bytes 8650752 | tf_op jit(solution)/shard_map/grad/pallas_call | solution.py:258
  121.9 14.5 %all_to_all.34 = bf16[4,64,2048]{2,1,0:T(8,128)(2,1)S(1)} all-to-all(bf16[4,64,2048]{2,1,0:T(8,128)(2,1)S(1)} %bitcast.12), channel_id=1, replica_groups={{0,4,8,12},{1,5,9,13},{2,6,10,14},{3,7,11,15},{16,20,24,28},{17,21,25,2..., dimensions={0} | all-to-all | bytes 2097152 | tf_op jit(solution)/shard_map/all_to_all | solution.py:218
  136.8 49.0 %all_to_all.35 = bf16[32,8,1024]{2,1,0:T(8,128)(2,1)S(1)} all-to-all(bf16[32,8,1024]{2,1,0:T(8,128)(2,1)S(1)} %bitcast.10), channel_id=1, replica_groups=mesh['ex'=32,'hid'=16] {'ex'}, dimensions={0} | all-to-all | bytes 1048576 | tf_op jit(solution)/shard_map/all_to_all | solution.py:267
  185.8 1.1 final.1
  (29 shorter events, 3.1 us)
Async XLA Ops:
  0.0 19.6 %copy-start.2 = (bf16[1,176,2048]{2,1,0:T(8,128)(2,1)S(1)}, bf16[1,176,2048]{2,1,0:T(8,128)(2,1)}, u32[]{:S(2)}) copy-start(bf16[1,176,2048]{2,1,0:T(8,128)(2,1)} %refs_2_.3) | copy-start | bytes 2162692
  2.6 16.9 %copy-start = (bf16[1,176,2048]{2,1,0:T(8,128)(2,1)S(1)}, bf16[1,176,2048]{2,1,0:T(8,128)(2,1)}, u32[]{:S(2)}) copy-start(bf16[1,176,2048]{2,1,0:T(8,128)(2,1)} %refs_0_.3) | copy-start | bytes 2162692
  2.6 16.9 %copy-start.1 = (bf16[1,176,2048]{2,1,0:T(8,128)(2,1)S(1)}, bf16[1,176,2048]{2,1,0:T(8,128)(2,1)}, u32[]{:S(2)}) copy-start(bf16[1,176,2048]{2,1,0:T(8,128)(2,1)} %refs_1_.3) | copy-start | bytes 2162692
  2.7 74.3 %all-to-all-start = ((bf16[32,8,2048]{2,1,0:T(8,128)(2,1)}), bf16[32,8,2048]{2,1,0:T(8,128)(2,1)S(1)}, u32[]{:S(2)}, u32[]{:S(2)}) async-start(bf16[32,8,2048]{2,1,0:T(8,128)(2,1)} %bitcast.15), calls=%async_computation | async-start | bytes 2097152 | tf_op jit(solution)/shard_map/all_to_all | solution.py:233
  20.5 54.1 %collective-permute-start = (bf16[288,2048]{1,0:T(8,128)(2,1)S(1)}, bf16[288,2048]{1,0:T(8,128)(2,1)S(1)}, u32[]{:S(2)}, u32[]{:S(2)}) collective-permute-start(bf16[288,2048]{1,0:T(8,128)(2,1)S(1)} %get-tuple-element.24), channel_id=1, source_target_pairs={{0,1},{1,2},{2,3},{3,0},{4,5},{5,6},{6,7},{7,4},{8,9},{9,10},{10,1... | collective-permute-start | bytes 3538952 | tf_op jit(solution)/shard_map/ppermute | solution.py:204
  23.7 52.3 %collective-permute-start.3 = (bf16[288,2048]{1,0:T(8,128)(2,1)S(1)}, bf16[288,2048]{1,0:T(8,128)(2,1)S(1)}, u32[]{:S(2)}, u32[]{:S(2)}) collective-permute-start(bf16[288,2048]{1,0:T(8,128)(2,1)S(1)} %get-tuple-element.24), channel_id=1, source_target_pairs={{0,3},{1,0},{2,1},{3,2},{4,7},{5,4},{6,5},{7,6},{8,11},{9,8},{10,9... | collective-permute-start | bytes 3538952 | tf_op jit(solution)/shard_map/ppermute | solution.py:204
  27.0 46.6 %collective-permute-start.1 = (bf16[240,2048]{1,0:T(8,128)(2,1)S(1)}, bf16[240,2048]{1,0:T(8,128)(2,1)S(1)}, u32[]{:S(2)}, u32[]{:S(2)}) collective-permute-start(bf16[240,2048]{1,0:T(8,128)(2,1)S(1)} %get-tuple-element.25), channel_id=1, source_target_pairs={{0,3},{1,0},{2,1},{3,2},{4,7},{5,4},{6,5},{7,6},{8,11},{9,8},{10,9... | collective-permute-start | bytes 2949128 | tf_op jit(solution)/shard_map/ppermute | solution.py:204
  30.2 43.4 %collective-permute-start.2 = (bf16[240,2048]{1,0:T(8,128)(2,1)S(1)}, bf16[240,2048]{1,0:T(8,128)(2,1)S(1)}, u32[]{:S(2)}, u32[]{:S(2)}) collective-permute-start(bf16[240,2048]{1,0:T(8,128)(2,1)S(1)} %get-tuple-element.25), channel_id=1, source_target_pairs={{0,1},{1,2},{2,3},{3,0},{4,5},{5,6},{6,7},{7,4},{8,9},{9,10},{10,1... | collective-permute-start | bytes 2949128 | tf_op jit(solution)/shard_map/ppermute | solution.py:204
  73.6 1.3 copy-start.7
  73.6 1.0 copy-start.9
  74.9 1.0 copy-start.3
  76.0 1.0 copy-start.5
  77.0 16.8 %copy-start.8 = (bf16[240,2048]{1,0:T(8,128)(2,1)S(1)}, bf16[240,2048]{1,0:T(8,128)(2,1)}, u32[]{:S(2)}) copy-start(bf16[240,2048]{1,0:T(8,128)(2,1)} %copy-done.7) | copy-start | bytes 2949124
  77.0 40.5 %collective-permute-start.7 = (bf16[288,2048]{1,0:T(8,128)(2,1)}, bf16[288,2048]{1,0:T(8,128)(2,1)S(1)}, u32[]{:S(2)}, u32[]{:S(2)}) collective-permute-start(bf16[288,2048]{1,0:T(8,128)(2,1)} %copy-done.3), channel_id=1, source_target_pairs={{0,1},{1,2},{2,3},{3,0},{4,5},{5,6},{6,7},{7,4},{8,9},{9,10},{10,1... | collective-permute-start | bytes 3538952 | tf_op jit(solution)/shard_map/ppermute | solution.py:204
  80.2 37.2 %collective-permute-start.8 = (bf16[240,2048]{1,0:T(8,128)(2,1)}, bf16[240,2048]{1,0:T(8,128)(2,1)S(1)}, u32[]{:S(2)}, u32[]{:S(2)}) collective-permute-start(bf16[240,2048]{1,0:T(8,128)(2,1)} %copy-done.7), channel_id=1, source_target_pairs={{0,3},{1,0},{2,1},{3,2},{4,7},{5,4},{6,5},{7,6},{8,11},{9,8},{10,9... | collective-permute-start | bytes 2949128 | tf_op jit(solution)/shard_map/ppermute | solution.py:204
  84.1 16.2 %collective-permute-start.4 = (bf16[128,2048]{1,0:T(8,128)(2,1)S(1)}, bf16[128,2048]{1,0:T(8,128)(2,1)S(1)}, u32[]{:S(2)}, u32[]{:S(2)}) collective-permute-start(bf16[128,2048]{1,0:T(8,128)(2,1)S(1)} %get-tuple-element.27.refs_0_), channel_id=1, source_target_pairs={{0,4},{1,5},{2,6},{3,7},{4,0},{5,1},{6,2},{7,3},{8,12},{9,13},{10,... | collective-permute-start | bytes 1572872 | tf_op jit(solution)/shard_map/ppermute | solution.py:241
  87.3 23.9 %collective-permute-start.5 = (bf16[128,2048]{1,0:T(8,128)(2,1)S(1)}, bf16[128,2048]{1,0:T(8,128)(2,1)S(1)}, u32[]{:S(2)}, u32[]{:S(2)}) collective-permute-start(bf16[128,2048]{1,0:T(8,128)(2,1)S(1)} %get-tuple-element.28), channel_id=1, source_target_pairs={{0,8},{1,9},{2,10},{3,11},{4,12},{5,13},{6,14},{7,15},{8,0},{9,1},... | collective-permute-start | bytes 1572872 | tf_op jit(solution)/shard_map/ppermute | solution.py:241
  91.8 25.6 %collective-permute-start.6 = (bf16[128,2048]{1,0:T(8,128)(2,1)S(1)}, bf16[128,2048]{1,0:T(8,128)(2,1)S(1)}, u32[]{:S(2)}, u32[]{:S(2)}) collective-permute-start(bf16[128,2048]{1,0:T(8,128)(2,1)S(1)} %get-tuple-element.28), channel_id=1, source_target_pairs={{0,12},{1,13},{2,14},{3,15},{4,8},{5,9},{6,10},{7,11},{8,4},{9,5},... | collective-permute-start | bytes 1572872 | tf_op jit(solution)/shard_map/ppermute | solution.py:241
  93.8 1.3 copy-start.4
  95.1 1.3 copy-start.6
  96.3 1.2 copy-start.10
  136.4 49.4 %copy-start.11 = (s32[16,4]{0,1:T(4,128)S(1)}, s32[16,4]{0,1:T(4,128)}, u32[]{:S(2)}) copy-start(s32[16,4]{0,1:T(4,128)} %param.10) | copy-start | bytes 772

commit v7 on v6

--- a/solution.py
+++ b/solution.py
@@ -38,7 +38,7 @@
     ]
     for cp in copies:
         cp.start()
-    for cp in copies:
+    for cp in copies[:2]:
         cp.wait()
     tok, width = tok_ref.shape
     top = route_ref.shape[0]
@@ -51,6 +51,8 @@
     weight = jnp.sum(weight * hit * (1.0 - is_x) + is_x * (1.0 / tok), axis=1, keepdims=True)
     pick = named * hit
     pick = jnp.concatenate([pick * is_x, pick * (1.0 - is_x)], axis=1).astype(BF)
+    for cp in copies[2:]:
+        cp.wait()
     data = jnp.concatenate([tok_ref[...], cot_ref[...]], axis=0)
     out_ref[...] = (weight * jnp.dot(pick, data, preferred_element_type=F32)).astype(BF)
 
@@ -233,19 +235,19 @@
     arrived = lax.all_to_all(packed, "ex", split_axis=0, concat_axis=0, tiled=True)
     left_early, right_late = shift(early, 1), shift(late, -1)
     left_late, right_early = shift(late, 1), shift(early, -1)
-    arrived, left_early, right_late, left_late, right_early = lax.optimization_barrier(
-        (arrived, left_early, right_late, left_late, right_early)
+    own, other = _call(unpack_kernel, (_shape(4 * n_ex, width),) * 2, "unpack", small)(arrived)
+    own, other, left_early, right_late, left_late, right_early = lax.optimization_barrier(
+        (own, other, left_early, right_late, left_late, right_early)
     )
     last = [shift(left_early, 1), shift(right_late, -1)]
-    own, other = _call(unpack_kernel, (_shape(4 * n_ex, width),) * 2, "unpack", small)(arrived)
     flip = lambda v, d: lax.ppermute(
         v, "hid", [(y * side + x, (y ^ d) * side + x) for y in range(side) for x in range(side)]
     )
-    rows_all = [own, flip(own, 1), flip(other, 2), flip(other, 3)]
+    two, three = flip(other, 2), flip(other, 3)
+    rows_all = [own, flip(own, 1), two, three]
     hid = side * unit
     main = 3 * unit // 256 * 256
     rest = 3 * unit - main
-    _, *pieces = lax.optimization_barrier((own, left_early, left_late, right_early, right_late))
     staged = _call(
         stage_kernel,
         (_shape(main, width),) * 3 + (_shape(rest, width),) * 3,
@@ -253,7 +255,7 @@
         (0, 24 * 3 * unit * width),
         in_specs=[pl.BlockSpec(memory_space=pl.ANY)] * 7,
         scratch_shapes=[pltpu.SemaphoreType.DMA((18,))],
-    )(w_gate, w_up, w_down, *pieces)
+    )(w_gate, w_up, w_down, left_early, left_late, right_early, right_late)
     rows = 8 * n_ex
     parts = _call(
         grad_kernel,

time: 188 us -> 185 us (0.984)
  local copies, waits for them, and re-layouts: 7.09 us -> 0.02 us
  waiting for transfers between devices: 58.4 us -> 62.6 us
    all_to_all x1, waiting for transfers between devices: 0.01 us -> 41.5 us  [per_device(): lax.all_to_all(packed, 'ex', split_axis=0, concat_axis=0, tiled=True)]
    ppermute x6, waiting for transfers between devices: 41.3 us -> 0.02 us  [shift(): lax.ppermute(v, 'hid', [(y * side + x, y * side + (x + d) % side) for y i...]
    unnamed x24 -> x8, local copies, waits for them, and re-layouts: 7.09 us -> 0.02 us
    ppermute x3, waiting for transfers between devices: 17.1 us -> 21 us  [per_device(): lax.ppermute(v, 'hid', [(y * side + x, (y ^ d) * side + x) for y in range...]
  transfers between devices with their start and end apart: 10 -> 10, of which waited for: 3 -> 4; matrix products, arithmetic and copies ran while one was open for 0% -> 0% of each run, Pallas kernels for 2% -> 3%
where the time goes in v7:
time: 185 us
  blocking collectives  63 us (34%)
  waiting for transfers between devices  62.6 us (34%)
  starting transfers between devices  44.8 us (24%)
  Pallas kernels  14 us (8%)
    all_to_all x1, blocking collectives, per_device(): lax.all_to_all(merged, 'ex', split_axis=0, concat_axis=0, tiled=True)  48.4 us
    all_to_all x1, waiting for transfers between devices, per_device(): lax.all_to_all(packed, 'ex', split_axis=0, concat_axis=0, tiled=True)  41.5 us
    ppermute x3, waiting for transfers between devices, per_device(): lax.ppermute(v, 'hid', [(y * side + x, (y ^ d) * side + x) for y in range...  21 us
    ppermute x6, starting transfers between devices, shift(): lax.ppermute(v, 'hid', [(y * side + x, y * side + (x + d) % side) for y i...  18.3 us
    all_to_all x1, starting transfers between devices, per_device(): lax.all_to_all(packed, 'ex', split_axis=0, concat_axis=0, tiled=True)  16.9 us
    all_to_all x1, blocking collectives, over_y(): lax.all_to_all(v, 'hid', split_axis=0, concat_axis=0, tiled=True, axis_in...  14.6 us
    ppermute x3, starting transfers between devices, per_device(): lax.ppermute(v, 'hid', [(y * side + x, (y ^ d) * side + x) for y in range...  9.65 us
    pallas_call x1, Pallas kernels, per_device(): _call(grad_kernel, _shape(rows, width), 'grad', (10 * rows * hid * width,...  4.42 us
  transfers between devices with their start and end apart: 10, of which 4 were waited for; matrix products, arithmetic and copies ran while one was open for 0% of the time, Pallas kernels for 3%

profile of v7, /device:TPU:1, one launch (start us, length us, event | category | flops | bytes accessed | tf_op | source)
XLA Modules:
  0.0 184.6 jit_solution(11746766365065110579)
XLA Ops:
  0.0 2.6 %pack.1 = bf16[256,2048]{1,0:T(8,128)(2,1)} custom-call(bf16[16,2048]{1,0:T(8,128)(2,1)} %tok_in.1, bf16[16,2048]{1,0:T(8,128)(2,1)} %cot_in.1, f32[4,16]{1,0:T(4,128)} %bitcast.16, s32[4,16]{1,0:T(4,128)} %bitcast.13), custom_call_target="tpu_custom_call" | custom-call | flops 67108864 | bytes 2097152 | tf_op jit(solution)/shard_map/pack/pallas_call | solution.py:225
  2.6 0.0 copy-start
  2.6 16.9 %all-to-all-start = ((bf16[32,8,2048]{2,1,0:T(8,128)(2,1)}), bf16[32,8,2048]{2,1,0:T(8,128)(2,1)S(1)}, u32[]{:S(2)}, u32[]{:S(2)}) async-start(bf16[32,8,2048]{2,1,0:T(8,128)(2,1)} %bitcast.15), calls=%async_computation | async-start | bytes 2097152 | tf_op jit(solution)/shard_map/all_to_all | solution.py:235
  19.5 2.3 %split.1 = (bf16[288,2048]{1,0:T(8,128)(2,1)}, bf16[240,2048]{1,0:T(8,128)(2,1)}) custom-call(bf16[1,176,2048]{2,1,0:T(8,128)(2,1)S(1)} %copy-done, bf16[1,176,2048]{2,1,0:T(8,128)(2,1)S(1)} %copy-done.1, bf16[1,176,2048]{2,1,0:T(8,128)(2,1)S(1)} %copy-done.2), custom_call_target="tpu_custom_call" | custom-call | bytes 4325376 | tf_op jit(solution)/shard_map/split/pallas_call | solution.py:211
  21.9 3.1 %collective-permute-start = (bf16[288,2048]{1,0:T(8,128)(2,1)}, bf16[288,2048]{1,0:T(8,128)(2,1)}, u32[]{:S(2)}, u32[]{:S(2)}) collective-permute-start(bf16[288,2048]{1,0:T(8,128)(2,1)} %get-tuple-element.23), channel_id=1, source_target_pairs={{0,1},{1,2},{2,3},{3,0},{4,5},{5,6},{6,7},{7,4},{8,9},{9,10},{10,1... | collective-permute-start | bytes 3538952 | tf_op jit(solution)/shard_map/ppermute | solution.py:206
  25.0 3.4 %collective-permute-start.3 = (bf16[288,2048]{1,0:T(8,128)(2,1)}, bf16[288,2048]{1,0:T(8,128)(2,1)}, u32[]{:S(2)}, u32[]{:S(2)}) collective-permute-start(bf16[288,2048]{1,0:T(8,128)(2,1)} %get-tuple-element.23), channel_id=1, source_target_pairs={{0,3},{1,0},{2,1},{3,2},{4,7},{5,4},{6,5},{7,6},{8,11},{9,8},{10,9... | collective-permute-start | bytes 3538952 | tf_op jit(solution)/shard_map/ppermute | solution.py:206
  28.4 3.2 %collective-permute-start.1 = (bf16[240,2048]{1,0:T(8,128)(2,1)}, bf16[240,2048]{1,0:T(8,128)(2,1)}, u32[]{:S(2)}, u32[]{:S(2)}) collective-permute-start(bf16[240,2048]{1,0:T(8,128)(2,1)} %get-tuple-element.24), channel_id=1, source_target_pairs={{0,3},{1,0},{2,1},{3,2},{4,7},{5,4},{6,5},{7,6},{8,11},{9,8},{10,9... | collective-permute-start | bytes 2949128 | tf_op jit(solution)/shard_map/ppermute | solution.py:206
  31.6 2.1 %collective-permute-start.2 = (bf16[240,2048]{1,0:T(8,128)(2,1)}, bf16[240,2048]{1,0:T(8,128)(2,1)}, u32[]{:S(2)}, u32[]{:S(2)}) collective-permute-start(bf16[240,2048]{1,0:T(8,128)(2,1)} %get-tuple-element.24), channel_id=1, source_target_pairs={{0,1},{1,2},{2,3},{3,0},{4,5},{5,6},{6,7},{7,4},{8,9},{9,10},{10,1... | collective-permute-start | bytes 2949128 | tf_op jit(solution)/shard_map/ppermute | solution.py:206
  33.7 41.5 %all-to-all-done = bf16[32,8,2048]{2,1,0:T(8,128)(2,1)S(1)} async-done(((bf16[32,8,2048]{2,1,0:T(8,128)(2,1)}), bf16[32,8,2048]{2,1,0:T(8,128)(2,1)S(1)}, u32[]{:S(2)}, u32[]{:S(2)}) %all-to-all-start) | async-done | bytes 1048608 | tf_op jit(solution)/shard_map/all_to_all | solution.py:235
  75.2 0.5 unpack.1
  75.7 3.1 %collective-permute-start.7 = (bf16[288,2048]{1,0:T(8,128)(2,1)}, bf16[288,2048]{1,0:T(8,128)(2,1)S(1)}, u32[]{:S(2)}, u32[]{:S(2)}) collective-permute-start(bf16[288,2048]{1,0:T(8,128)(2,1)} %collective-permute-done.refs_3_), channel_id=1, source_target_pairs={{0,1},{1,2},{2,3},{3,0},{4,5},{5,6},{6,7},{7,4},{8,9},{9,10},{10,1... | collective-permute-start | bytes 3538952 | tf_op jit(solution)/shard_map/ppermute | solution.py:206
  78.9 3.4 %collective-permute-start.8 = (bf16[240,2048]{1,0:T(8,128)(2,1)}, bf16[240,2048]{1,0:T(8,128)(2,1)S(1)}, u32[]{:S(2)}, u32[]{:S(2)}) collective-permute-start(bf16[240,2048]{1,0:T(8,128)(2,1)} %collective-permute-done.1.refs_6_), channel_id=1, source_target_pairs={{0,3},{1,0},{2,1},{3,2},{4,7},{5,4},{6,5},{7,6},{8,11},{9,8},{10,9... | collective-permute-start | bytes 2949128 | tf_op jit(solution)/shard_map/ppermute | solution.py:206
  82.2 3.2 %collective-permute-start.4 = (bf16[128,2048]{1,0:T(8,128)(2,1)S(1)}, bf16[128,2048]{1,0:T(8,128)(2,1)S(1)}, u32[]{:S(2)}, u32[]{:S(2)}) collective-permute-start(bf16[128,2048]{1,0:T(8,128)(2,1)S(1)} %get-tuple-element.25.refs_0_), channel_id=1, source_target_pairs={{0,4},{1,5},{2,6},{3,7},{4,0},{5,1},{6,2},{7,3},{8,12},{9,13},{10,... | collective-permute-start | bytes 1572872 | tf_op jit(solution)/shard_map/ppermute | solution.py:243
  85.5 4.5 %collective-permute-start.5 = (bf16[128,2048]{1,0:T(8,128)(2,1)S(1)}, bf16[128,2048]{1,0:T(8,128)(2,1)S(1)}, u32[]{:S(2)}, u32[]{:S(2)}) collective-permute-start(bf16[128,2048]{1,0:T(8,128)(2,1)S(1)} %get-tuple-element.26), channel_id=1, source_target_pairs={{0,8},{1,9},{2,10},{3,11},{4,12},{5,13},{6,14},{7,15},{8,0},{9,1},... | collective-permute-start | bytes 1572872 | tf_op jit(solution)/shard_map/ppermute | solution.py:243
  90.0 1.9 %collective-permute-start.6 = (bf16[128,2048]{1,0:T(8,128)(2,1)S(1)}, bf16[128,2048]{1,0:T(8,128)(2,1)S(1)}, u32[]{:S(2)}, u32[]{:S(2)}) collective-permute-start(bf16[128,2048]{1,0:T(8,128)(2,1)S(1)} %get-tuple-element.26), channel_id=1, source_target_pairs={{0,12},{1,13},{2,14},{3,15},{4,8},{5,9},{6,10},{7,11},{8,4},{9,5},... | collective-permute-start | bytes 1572872 | tf_op jit(solution)/shard_map/ppermute | solution.py:243
  91.9 2.7 %stage.1 = (bf16[512,2048]{1,0:T(8,128)(2,1)S(1)}, bf16[512,2048]{1,0:T(8,128)(2,1)S(1)}, bf16[512,2048]{1,0:T(8,128)(2,1)S(1)}, bf16[16,2048]{1,0:T(8,128)(2,1)...) custom-call(bf16[1,176,2048]{2,1,0:T(8,128)(2,1)S(1)} %copy-done, bf16[1,176,2048]{2,1,0:T(8,128)(2,1)S(1)} %copy-done.1, ...), custom_call_target="tpu_custom_call" | custom-call | bytes 25952256 | tf_op jit(solution)/shard_map/stage/pallas_call | solution.py:251
  94.7 1.4 collective-permute-done.4.refs_1_
  96.0 13.7 %collective-permute-done.5.refs_2_ = bf16[128,2048]{1,0:T(8,128)(2,1)S(1)} collective-permute-done((bf16[128,2048]{1,0:T(8,128)(2,1)S(1)}, bf16[128,2048]{1,0:T(8,128)(2,1)S(1)}, u32[]{:S(2)}, u32[]{:S(2)}) %collective-permute-start.5) | collective-permute-done | bytes 524320 | tf_op jit(solution)/shard_map/ppermute | solution.py:243
  109.8 5.9 %collective-permute-done.6.refs_3_ = bf16[128,2048]{1,0:T(8,128)(2,1)S(1)} collective-permute-done((bf16[128,2048]{1,0:T(8,128)(2,1)S(1)}, bf16[128,2048]{1,0:T(8,128)(2,1)S(1)}, u32[]{:S(2)}, u32[]{:S(2)}) %collective-permute-start.6) | collective-permute-done | bytes 524320 | tf_op jit(solution)/shard_map/ppermute | solution.py:243
  115.7 4.4 %grad.1 = bf16[256,2048]{1,0:T(8,128)(2,1)S(1)} custom-call(bf16[128,2048]{1,0:T(8,128)(2,1)S(1)} %get-tuple-element.25.refs_0_, bf16[128,2048]{1,0:T(8,128)(2,1)S(1)} %collective-permute-done.4.refs_1_, bf16[128,2048]{1,0:T(8,128)(2,1)S(1)} %collective-permute-done.5.refs_2_, bf16[128,2048]{1,0:T(8,128)(2,1)S(1)} %collective-permute-done.6.refs_3_, ...), custom_call_target="tpu_custom_call" | custom-call | flops 3690987520 | bytes 8650752 | tf_op jit(solution)/shard_map/grad/pallas_call | solution.py:260
  120.1 14.6 %all_to_all.33 = bf16[4,64,2048]{2,1,0:T(8,128)(2,1)S(1)} all-to-all(bf16[4,64,2048]{2,1,0:T(8,128)(2,1)S(1)} %bitcast.12), channel_id=1, replica_groups={{0,4,8,12},{1,5,9,13},{2,6,10,14},{3,7,11,15},{16,20,24,28},{17,21,25,2..., dimensions={0} | all-to-all | bytes 2097152 | tf_op jit(solution)/shard_map/all_to_all | solution.py:220
  134.7 0.4 merge.1
  135.1 48.4 %all_to_all.34 = bf16[32,8,1024]{2,1,0:T(8,128)(2,1)S(1)} all-to-all(bf16[32,8,1024]{2,1,0:T(8,128)(2,1)S(1)} %bitcast.10), channel_id=1, replica_groups=mesh['ex'=32,'hid'=16] {'ex'}, dimensions={0} | all-to-all | bytes 1048576 | tf_op jit(solution)/shard_map/all_to_all | solution.py:269
  183.5 1.1 final.1
  (13 shorter events, 0.0 us)
Async XLA Ops:
  0.0 19.5 %copy-start.2 = (bf16[1,176,2048]{2,1,0:T(8,128)(2,1)S(1)}, bf16[1,176,2048]{2,1,0:T(8,128)(2,1)}, u32[]{:S(2)}) copy-start(bf16[1,176,2048]{2,1,0:T(8,128)(2,1)} %refs_2_.3) | copy-start | bytes 2162692
  2.6 16.9 %copy-start = (bf16[1,176,2048]{2,1,0:T(8,128)(2,1)S(1)}, bf16[1,176,2048]{2,1,0:T(8,128)(2,1)}, u32[]{:S(2)}) copy-start(bf16[1,176,2048]{2,1,0:T(8,128)(2,1)} %refs_0_.3) | copy-start | bytes 2162692
  2.6 16.9 %copy-start.1 = (bf16[1,176,2048]{2,1,0:T(8,128)(2,1)S(1)}, bf16[1,176,2048]{2,1,0:T(8,128)(2,1)}, u32[]{:S(2)}) copy-start(bf16[1,176,2048]{2,1,0:T(8,128)(2,1)} %refs_1_.3) | copy-start | bytes 2162692
  2.6 72.6 %all-to-all-start = ((bf16[32,8,2048]{2,1,0:T(8,128)(2,1)}), bf16[32,8,2048]{2,1,0:T(8,128)(2,1)S(1)}, u32[]{:S(2)}, u32[]{:S(2)}) async-start(bf16[32,8,2048]{2,1,0:T(8,128)(2,1)} %bitcast.15), calls=%async_computation | async-start | bytes 2097152 | tf_op jit(solution)/shard_map/all_to_all | solution.py:235
  21.9 53.8 %collective-permute-start = (bf16[288,2048]{1,0:T(8,128)(2,1)}, bf16[288,2048]{1,0:T(8,128)(2,1)}, u32[]{:S(2)}, u32[]{:S(2)}) collective-permute-start(bf16[288,2048]{1,0:T(8,128)(2,1)} %get-tuple-element.23), channel_id=1, source_target_pairs={{0,1},{1,2},{2,3},{3,0},{4,5},{5,6},{6,7},{7,4},{8,9},{9,10},{10,1... | collective-permute-start | bytes 3538952 | tf_op jit(solution)/shard_map/ppermute | solution.py:206
  25.0 50.7 %collective-permute-start.3 = (bf16[288,2048]{1,0:T(8,128)(2,1)}, bf16[288,2048]{1,0:T(8,128)(2,1)}, u32[]{:S(2)}, u32[]{:S(2)}) collective-permute-start(bf16[288,2048]{1,0:T(8,128)(2,1)} %get-tuple-element.23), channel_id=1, source_target_pairs={{0,3},{1,0},{2,1},{3,2},{4,7},{5,4},{6,5},{7,6},{8,11},{9,8},{10,9... | collective-permute-start | bytes 3538952 | tf_op jit(solution)/shard_map/ppermute | solution.py:206
  28.4 47.3 %collective-permute-start.1 = (bf16[240,2048]{1,0:T(8,128)(2,1)}, bf16[240,2048]{1,0:T(8,128)(2,1)}, u32[]{:S(2)}, u32[]{:S(2)}) collective-permute-start(bf16[240,2048]{1,0:T(8,128)(2,1)} %get-tuple-element.24), channel_id=1, source_target_pairs={{0,3},{1,0},{2,1},{3,2},{4,7},{5,4},{6,5},{7,6},{8,11},{9,8},{10,9... | collective-permute-start | bytes 2949128 | tf_op jit(solution)/shard_map/ppermute | solution.py:206
  31.6 44.1 %collective-permute-start.2 = (bf16[240,2048]{1,0:T(8,128)(2,1)}, bf16[240,2048]{1,0:T(8,128)(2,1)}, u32[]{:S(2)}, u32[]{:S(2)}) collective-permute-start(bf16[240,2048]{1,0:T(8,128)(2,1)} %get-tuple-element.24), channel_id=1, source_target_pairs={{0,1},{1,2},{2,3},{3,0},{4,5},{5,6},{6,7},{7,4},{8,9},{9,10},{10,1... | collective-permute-start | bytes 2949128 | tf_op jit(solution)/shard_map/ppermute | solution.py:206
  75.7 40.0 %collective-permute-start.7 = (bf16[288,2048]{1,0:T(8,128)(2,1)}, bf16[288,2048]{1,0:T(8,128)(2,1)S(1)}, u32[]{:S(2)}, u32[]{:S(2)}) collective-permute-start(bf16[288,2048]{1,0:T(8,128)(2,1)} %collective-permute-done.refs_3_), channel_id=1, source_target_pairs={{0,1},{1,2},{2,3},{3,0},{4,5},{5,6},{6,7},{7,4},{8,9},{9,10},{10,1... | collective-permute-start | bytes 3538952 | tf_op jit(solution)/shard_map/ppermute | solution.py:206
  78.9 36.8 %collective-permute-start.8 = (bf16[240,2048]{1,0:T(8,128)(2,1)}, bf16[240,2048]{1,0:T(8,128)(2,1)S(1)}, u32[]{:S(2)}, u32[]{:S(2)}) collective-permute-start(bf16[240,2048]{1,0:T(8,128)(2,1)} %collective-permute-done.1.refs_6_), channel_id=1, source_target_pairs={{0,3},{1,0},{2,1},{3,2},{4,7},{5,4},{6,5},{7,6},{8,11},{9,8},{10,9... | collective-permute-start | bytes 2949128 | tf_op jit(solution)/shard_map/ppermute | solution.py:206
  82.2 13.8 %collective-permute-start.4 = (bf16[128,2048]{1,0:T(8,128)(2,1)S(1)}, bf16[128,2048]{1,0:T(8,128)(2,1)S(1)}, u32[]{:S(2)}, u32[]{:S(2)}) collective-permute-start(bf16[128,2048]{1,0:T(8,128)(2,1)S(1)} %get-tuple-element.25.refs_0_), channel_id=1, source_target_pairs={{0,4},{1,5},{2,6},{3,7},{4,0},{5,1},{6,2},{7,3},{8,12},{9,13},{10,... | collective-permute-start | bytes 1572872 | tf_op jit(solution)/shard_map/ppermute | solution.py:243
  85.5 24.3 %collective-permute-start.5 = (bf16[128,2048]{1,0:T(8,128)(2,1)S(1)}, bf16[128,2048]{1,0:T(8,128)(2,1)S(1)}, u32[]{:S(2)}, u32[]{:S(2)}) collective-permute-start(bf16[128,2048]{1,0:T(8,128)(2,1)S(1)} %get-tuple-element.26), channel_id=1, source_target_pairs={{0,8},{1,9},{2,10},{3,11},{4,12},{5,13},{6,14},{7,15},{8,0},{9,1},... | collective-permute-start | bytes 1572872 | tf_op jit(solution)/shard_map/ppermute | solution.py:243
  90.0 25.7 %collective-permute-start.6 = (bf16[128,2048]{1,0:T(8,128)(2,1)S(1)}, bf16[128,2048]{1,0:T(8,128)(2,1)S(1)}, u32[]{:S(2)}, u32[]{:S(2)}) collective-permute-start(bf16[128,2048]{1,0:T(8,128)(2,1)S(1)} %get-tuple-element.26), channel_id=1, source_target_pairs={{0,12},{1,13},{2,14},{3,15},{4,8},{5,9},{6,10},{7,11},{8,4},{9,5},... | collective-permute-start | bytes 1572872 | tf_op jit(solution)/shard_map/ppermute | solution.py:243
  134.7 48.8 %copy-start.3 = (s32[16,4]{0,1:T(4,128)S(1)}, s32[16,4]{0,1:T(4,128)}, u32[]{:S(2)}) copy-start(s32[16,4]{0,1:T(4,128)} %param.10) | copy-start | bytes 772

commit v8 on v7

--- a/solution.py
+++ b/solution.py
@@ -118,8 +118,8 @@
     x, y, tails = refs[n + 9], refs[n + 10], refs[n + 11 :]
     half = rows_in[0].shape[0] // 2
     me = lax.axis_index("hid") // n
-    for i in range(n):
-        at = pl.ds(pl.multiple_of(jnp.bitwise_xor(me, i) * half, half), half)
+    for i, d in enumerate((2, 3, 1, 0)):
+        at = pl.ds(pl.multiple_of(jnp.bitwise_xor(me, d) * half, half), half)
         x[at, :] = rows_in[i][0:half, :]
         y[at, :] = rows_in[i][half : 2 * half, :]
     for m in range(3):
@@ -236,15 +236,13 @@
     left_early, right_late = shift(early, 1), shift(late, -1)
     left_late, right_early = shift(late, 1), shift(early, -1)
     own, other = _call(unpack_kernel, (_shape(4 * n_ex, width),) * 2, "unpack", small)(arrived)
-    own, other, left_early, right_late, left_late, right_early = lax.optimization_barrier(
-        (own, other, left_early, right_late, left_late, right_early)
-    )
+    own, left_early, right_late = lax.optimization_barrier((own, left_early, right_late))
     last = [shift(left_early, 1), shift(right_late, -1)]
+    own, other, left_late, right_early = lax.optimization_barrier((own, other, left_late, right_early))
     flip = lambda v, d: lax.ppermute(
         v, "hid", [(y * side + x, (y ^ d) * side + x) for y in range(side) for x in range(side)]
     )
-    two, three = flip(other, 2), flip(other, 3)
-    rows_all = [own, flip(own, 1), two, three]
+    rows_all = [flip(other, 2), flip(other, 3), flip(own, 1), own]
     hid = side * unit
     main = 3 * unit // 256 * 256
     rest = 3 * unit - main

time: 185 us -> 175 us (0.946)
  blocking collectives: 63 us -> 58 us
  waiting for transfers between devices: 62.6 us -> 57.9 us
    all_to_all x1, blocking collectives: 48.4 us -> 39.9 us  [per_device(): lax.all_to_all(merged, 'ex', split_axis=0, concat_axis=0, tiled=True)]
    ppermute x3, waiting for transfers between devices: 21 us -> 16.3 us  [per_device(): lax.ppermute(v, 'hid', [(y * side + x, (y ^ d) * side + x) for y in range...]
    all_to_all x1, blocking collectives: 14.6 us -> 18.1 us  [over_y(): lax.all_to_all(v, 'hid', split_axis=0, concat_axis=0, tiled=True, axis_in...]
  transfers between devices with their start and end apart: 10 -> 10, of which waited for: 4 -> 3; matrix products, arithmetic and copies ran while one was open for 0% -> 0% of each run, Pallas kernels for 3% -> 3%
where the time goes in v8:
time: 175 us
  blocking collectives  58 us (33%)
  waiting for transfers between devices  57.9 us (33%)
  starting transfers between devices  44.6 us (25%)
  Pallas kernels  13.9 us (8%)
    all_to_all x1, waiting for transfers between devices, per_device(): lax.all_to_all(packed, 'ex', split_axis=0, concat_axis=0, tiled=True)  41.6 us
    all_to_all x1, blocking collectives, per_device(): lax.all_to_all(merged, 'ex', split_axis=0, concat_axis=0, tiled=True)  39.9 us
    ppermute x6, starting transfers between devices, shift(): lax.ppermute(v, 'hid', [(y * side + x, y * side + (x + d) % side) for y i...  18.3 us
    all_to_all x1, blocking collectives, over_y(): lax.all_to_all(v, 'hid', split_axis=0, concat_axis=0, tiled=True, axis_in...  18.1 us
    all_to_all x1, starting transfers between devices, per_device(): lax.all_to_all(packed, 'ex', split_axis=0, concat_axis=0, tiled=True)  16.9 us
    ppermute x3, waiting for transfers between devices, per_device(): lax.ppermute(v, 'hid', [(y * side + x, (y ^ d) * side + x) for y in range...  16.3 us
    ppermute x3, starting transfers between devices, per_device(): lax.ppermute(v, 'hid', [(y * side + x, (y ^ d) * side + x) for y in range...  9.43 us
    pallas_call x1, Pallas kernels, per_device(): _call(grad_kernel, _shape(rows, width), 'grad', (10 * rows * hid * width,...  4.43 us
  transfers between devices with their start and end apart: 10, of which 3 were waited for; matrix products, arithmetic and copies ran while one was open for 0% of the time, Pallas kernels for 3%

profile of v8, /device:TPU:1, one launch (start us, length us, event | category | flops | bytes accessed | tf_op | source)
XLA Modules:
  0.0 174.7 jit_solution(7267098073567524697)
XLA Ops:
  0.0 2.6 %pack.1 = bf16[256,2048]{1,0:T(8,128)(2,1)} custom-call(bf16[16,2048]{1,0:T(8,128)(2,1)} %tok_in.1, bf16[16,2048]{1,0:T(8,128)(2,1)} %cot_in.1, f32[4,16]{1,0:T(4,128)} %bitcast.16, s32[4,16]{1,0:T(4,128)} %bitcast.13), custom_call_target="tpu_custom_call" | custom-call | flops 67108864 | bytes 2097152 | tf_op jit(solution)/shard_map/pack/pallas_call | solution.py:225
  2.6 0.0 copy-start
  2.6 0.0 copy-start.1
  2.6 16.9 %all-to-all-start = ((bf16[32,8,2048]{2,1,0:T(8,128)(2,1)}), bf16[32,8,2048]{2,1,0:T(8,128)(2,1)S(1)}, u32[]{:S(2)}, u32[]{:S(2)}) async-start(bf16[32,8,2048]{2,1,0:T(8,128)(2,1)} %bitcast.15), calls=%async_computation | async-start | bytes 2097152 | tf_op jit(solution)/shard_map/all_to_all | solution.py:235
  19.5 2.3 %split.1 = (bf16[288,2048]{1,0:T(8,128)(2,1)}, bf16[240,2048]{1,0:T(8,128)(2,1)}) custom-call(bf16[1,176,2048]{2,1,0:T(8,128)(2,1)S(1)} %copy-done, bf16[1,176,2048]{2,1,0:T(8,128)(2,1)S(1)} %copy-done.1, bf16[1,176,2048]{2,1,0:T(8,128)(2,1)S(1)} %copy-done.2), custom_call_target="tpu_custom_call" | custom-call | bytes 4325376 | tf_op jit(solution)/shard_map/split/pallas_call | solution.py:211
  21.8 3.1 %collective-permute-start = (bf16[288,2048]{1,0:T(8,128)(2,1)}, bf16[288,2048]{1,0:T(8,128)(2,1)}, u32[]{:S(2)}, u32[]{:S(2)}) collective-permute-start(bf16[288,2048]{1,0:T(8,128)(2,1)} %get-tuple-element.23), channel_id=1, source_target_pairs={{0,1},{1,2},{2,3},{3,0},{4,5},{5,6},{6,7},{7,4},{8,9},{9,10},{10,1... | collective-permute-start | bytes 3538952 | tf_op jit(solution)/shard_map/ppermute | solution.py:206
  24.9 3.4 %collective-permute-start.1 = (bf16[240,2048]{1,0:T(8,128)(2,1)}, bf16[240,2048]{1,0:T(8,128)(2,1)}, u32[]{:S(2)}, u32[]{:S(2)}) collective-permute-start(bf16[240,2048]{1,0:T(8,128)(2,1)} %get-tuple-element.24), channel_id=1, source_target_pairs={{0,3},{1,0},{2,1},{3,2},{4,7},{5,4},{6,5},{7,6},{8,11},{9,8},{10,9... | collective-permute-start | bytes 2949128 | tf_op jit(solution)/shard_map/ppermute | solution.py:206
  28.3 3.2 %collective-permute-start.3 = (bf16[288,2048]{1,0:T(8,128)(2,1)}, bf16[288,2048]{1,0:T(8,128)(2,1)}, u32[]{:S(2)}, u32[]{:S(2)}) collective-permute-start(bf16[288,2048]{1,0:T(8,128)(2,1)} %get-tuple-element.23), channel_id=1, source_target_pairs={{0,3},{1,0},{2,1},{3,2},{4,7},{5,4},{6,5},{7,6},{8,11},{9,8},{10,9... | collective-permute-start | bytes 3538952 | tf_op jit(solution)/shard_map/ppermute | solution.py:206
  31.5 2.1 %collective-permute-start.2 = (bf16[240,2048]{1,0:T(8,128)(2,1)}, bf16[240,2048]{1,0:T(8,128)(2,1)}, u32[]{:S(2)}, u32[]{:S(2)}) collective-permute-start(bf16[240,2048]{1,0:T(8,128)(2,1)} %get-tuple-element.24), channel_id=1, source_target_pairs={{0,1},{1,2},{2,3},{3,0},{4,5},{5,6},{6,7},{7,4},{8,9},{9,10},{10,1... | collective-permute-start | bytes 2949128 | tf_op jit(solution)/shard_map/ppermute | solution.py:206
  33.6 41.6 %all-to-all-done = bf16[32,8,2048]{2,1,0:T(8,128)(2,1)S(1)} async-done(((bf16[32,8,2048]{2,1,0:T(8,128)(2,1)}), bf16[32,8,2048]{2,1,0:T(8,128)(2,1)S(1)}, u32[]{:S(2)}, u32[]{:S(2)}) %all-to-all-start) | async-done | bytes 1048608 | tf_op jit(solution)/shard_map/all_to_all | solution.py:235
  75.2 0.5 unpack.1
  75.7 3.1 %collective-permute-start.7 = (bf16[288,2048]{1,0:T(8,128)(2,1)}, bf16[288,2048]{1,0:T(8,128)(2,1)S(1)}, u32[]{:S(2)}, u32[]{:S(2)}) collective-permute-start(bf16[288,2048]{1,0:T(8,128)(2,1)} %collective-permute-done.refs_3_), channel_id=1, source_target_pairs={{0,1},{1,2},{2,3},{3,0},{4,5},{5,6},{6,7},{7,4},{8,9},{9,10},{10,1... | collective-permute-start | bytes 3538952 | tf_op jit(solution)/shard_map/ppermute | solution.py:206
  78.8 3.4 %collective-permute-start.8 = (bf16[240,2048]{1,0:T(8,128)(2,1)}, bf16[240,2048]{1,0:T(8,128)(2,1)S(1)}, u32[]{:S(2)}, u32[]{:S(2)}) collective-permute-start(bf16[240,2048]{1,0:T(8,128)(2,1)} %collective-permute-done.1.refs_6_), channel_id=1, source_target_pairs={{0,3},{1,0},{2,1},{3,2},{4,7},{5,4},{6,5},{7,6},{8,11},{9,8},{10,9... | collective-permute-start | bytes 2949128 | tf_op jit(solution)/shard_map/ppermute | solution.py:206
  82.2 4.8 %collective-permute-start.4 = (bf16[128,2048]{1,0:T(8,128)(2,1)S(1)}, bf16[128,2048]{1,0:T(8,128)(2,1)S(1)}, u32[]{:S(2)}, u32[]{:S(2)}) collective-permute-start(bf16[128,2048]{1,0:T(8,128)(2,1)S(1)} %get-tuple-element.27), channel_id=1, source_target_pairs={{0,8},{1,9},{2,10},{3,11},{4,12},{5,13},{6,14},{7,15},{8,0},{9,1},... | collective-permute-start | bytes 1572872 | tf_op jit(solution)/shard_map/ppermute | solution.py:242
  87.1 2.7 %collective-permute-start.5 = (bf16[128,2048]{1,0:T(8,128)(2,1)S(1)}, bf16[128,2048]{1,0:T(8,128)(2,1)S(1)}, u32[]{:S(2)}, u32[]{:S(2)}) collective-permute-start(bf16[128,2048]{1,0:T(8,128)(2,1)S(1)} %get-tuple-element.27), channel_id=1, source_target_pairs={{0,12},{1,13},{2,14},{3,15},{4,8},{5,9},{6,10},{7,11},{8,4},{9,5},... | collective-permute-start | bytes 1572872 | tf_op jit(solution)/shard_map/ppermute | solution.py:242
  89.8 1.9 %collective-permute-start.6 = (bf16[128,2048]{1,0:T(8,128)(2,1)S(1)}, bf16[128,2048]{1,0:T(8,128)(2,1)S(1)}, u32[]{:S(2)}, u32[]{:S(2)}) collective-permute-start(bf16[128,2048]{1,0:T(8,128)(2,1)S(1)} %get-tuple-element.28.refs_3_), channel_id=1, source_target_pairs={{0,4},{1,5},{2,6},{3,7},{4,0},{5,1},{6,2},{7,3},{8,12},{9,13},{10,... | collective-permute-start | bytes 1572872 | tf_op jit(solution)/shard_map/ppermute | solution.py:242
  91.7 2.7 %stage.1 = (bf16[512,2048]{1,0:T(8,128)(2,1)S(1)}, bf16[512,2048]{1,0:T(8,128)(2,1)S(1)}, bf16[512,2048]{1,0:T(8,128)(2,1)S(1)}, bf16[16,2048]{1,0:T(8,128)(2,1)...) custom-call(bf16[1,176,2048]{2,1,0:T(8,128)(2,1)S(1)} %copy-done, bf16[1,176,2048]{2,1,0:T(8,128)(2,1)S(1)} %copy-done.1, ...), custom_call_target="tpu_custom_call" | custom-call | bytes 25952256 | tf_op jit(solution)/shard_map/stage/pallas_call | solution.py:249
  94.4 3.6 %collective-permute-done.4.refs_0_ = bf16[128,2048]{1,0:T(8,128)(2,1)S(1)} collective-permute-done((bf16[128,2048]{1,0:T(8,128)(2,1)S(1)}, bf16[128,2048]{1,0:T(8,128)(2,1)S(1)}, u32[]{:S(2)}, u32[]{:S(2)}) %collective-permute-start.4) | collective-permute-done | bytes 524320 | tf_op jit(solution)/shard_map/ppermute | solution.py:242
  98.0 12.7 %collective-permute-done.5.refs_1_ = bf16[128,2048]{1,0:T(8,128)(2,1)S(1)} collective-permute-done((bf16[128,2048]{1,0:T(8,128)(2,1)S(1)}, bf16[128,2048]{1,0:T(8,128)(2,1)S(1)}, u32[]{:S(2)}, u32[]{:S(2)}) %collective-permute-start.5) | collective-permute-done | bytes 524320 | tf_op jit(solution)/shard_map/ppermute | solution.py:242
  110.7 4.4 %grad.1 = bf16[256,2048]{1,0:T(8,128)(2,1)S(1)} custom-call(bf16[128,2048]{1,0:T(8,128)(2,1)S(1)} %collective-permute-done.4.refs_0_, bf16[128,2048]{1,0:T(8,128)(2,1)S(1)} %collective-permute-done.5.refs_1_, bf16[128,2048]{1,0:T(8,128)(2,1)S(1)} %collective-permute-done.6.refs_2_, bf16[128,2048]{1,0:T(8,128)(2,1)S(1)} %get-tuple-element.28.refs_3_, ...), custom_call_target="tpu_custom_call" | custom-call | flops 3690987520 | bytes 8650752 | tf_op jit(solution)/shard_map/grad/pallas_call | solution.py:258
  115.2 18.1 %all_to_all.33 = bf16[4,64,2048]{2,1,0:T(8,128)(2,1)S(1)} all-to-all(bf16[4,64,2048]{2,1,0:T(8,128)(2,1)S(1)} %bitcast.12), channel_id=1, replica_groups={{0,4,8,12},{1,5,9,13},{2,6,10,14},{3,7,11,15},{16,20,24,28},{17,21,25,2..., dimensions={0} | all-to-all | bytes 2097152 | tf_op jit(solution)/shard_map/all_to_all | solution.py:220
  133.3 0.4 merge.1
  133.7 39.9 %all_to_all.34 = bf16[32,8,1024]{2,1,0:T(8,128)(2,1)S(1)} all-to-all(bf16[32,8,1024]{2,1,0:T(8,128)(2,1)S(1)} %bitcast.10), channel_id=1, replica_groups=mesh['ex'=32,'hid'=16] {'ex'}, dimensions={0} | all-to-all | bytes 1048576 | tf_op jit(solution)/shard_map/all_to_all | solution.py:267
  173.6 1.1 final.1
  (13 shorter events, 0.0 us)
Async XLA Ops:
  0.0 19.5 %copy-start.2 = (bf16[1,176,2048]{2,1,0:T(8,128)(2,1)S(1)}, bf16[1,176,2048]{2,1,0:T(8,128)(2,1)}, u32[]{:S(2)}) copy-start(bf16[1,176,2048]{2,1,0:T(8,128)(2,1)} %refs_2_.3) | copy-start | bytes 2162692
  2.6 16.9 %copy-start = (bf16[1,176,2048]{2,1,0:T(8,128)(2,1)S(1)}, bf16[1,176,2048]{2,1,0:T(8,128)(2,1)}, u32[]{:S(2)}) copy-start(bf16[1,176,2048]{2,1,0:T(8,128)(2,1)} %refs_0_.3) | copy-start | bytes 2162692
  2.6 16.9 %copy-start.1 = (bf16[1,176,2048]{2,1,0:T(8,128)(2,1)S(1)}, bf16[1,176,2048]{2,1,0:T(8,128)(2,1)}, u32[]{:S(2)}) copy-start(bf16[1,176,2048]{2,1,0:T(8,128)(2,1)} %refs_1_.3) | copy-start | bytes 2162692
  2.6 72.6 %all-to-all-start = ((bf16[32,8,2048]{2,1,0:T(8,128)(2,1)}), bf16[32,8,2048]{2,1,0:T(8,128)(2,1)S(1)}, u32[]{:S(2)}, u32[]{:S(2)}) async-start(bf16[32,8,2048]{2,1,0:T(8,128)(2,1)} %bitcast.15), calls=%async_computation | async-start | bytes 2097152 | tf_op jit(solution)/shard_map/all_to_all | solution.py:235
  21.8 53.9 %collective-permute-start = (bf16[288,2048]{1,0:T(8,128)(2,1)}, bf16[288,2048]{1,0:T(8,128)(2,1)}, u32[]{:S(2)}, u32[]{:S(2)}) collective-permute-start(bf16[288,2048]{1,0:T(8,128)(2,1)} %get-tuple-element.23), channel_id=1, source_target_pairs={{0,1},{1,2},{2,3},{3,0},{4,5},{5,6},{6,7},{7,4},{8,9},{9,10},{10,1... | collective-permute-start | bytes 3538952 | tf_op jit(solution)/shard_map/ppermute | solution.py:206
  24.9 50.7 %collective-permute-start.1 = (bf16[240,2048]{1,0:T(8,128)(2,1)}, bf16[240,2048]{1,0:T(8,128)(2,1)}, u32[]{:S(2)}, u32[]{:S(2)}) collective-permute-start(bf16[240,2048]{1,0:T(8,128)(2,1)} %get-tuple-element.24), channel_id=1, source_target_pairs={{0,3},{1,0},{2,1},{3,2},{4,7},{5,4},{6,5},{7,6},{8,11},{9,8},{10,9... | collective-permute-start | bytes 2949128 | tf_op jit(solution)/shard_map/ppermute | solution.py:206
  28.3 53.9 %collective-permute-start.3 = (bf16[288,2048]{1,0:T(8,128)(2,1)}, bf16[288,2048]{1,0:T(8,128)(2,1)}, u32[]{:S(2)}, u32[]{:S(2)}) collective-permute-start(bf16[288,2048]{1,0:T(8,128)(2,1)} %get-tuple-element.23), channel_id=1, source_target_pairs={{0,3},{1,0},{2,1},{3,2},{4,7},{5,4},{6,5},{7,6},{8,11},{9,8},{10,9... | collective-permute-start | bytes 3538952 | tf_op jit(solution)/shard_map/ppermute | solution.py:206
  31.5 50.7 %collective-permute-start.2 = (bf16[240,2048]{1,0:T(8,128)(2,1)}, bf16[240,2048]{1,0:T(8,128)(2,1)}, u32[]{:S(2)}, u32[]{:S(2)}) collective-permute-start(bf16[240,2048]{1,0:T(8,128)(2,1)} %get-tuple-element.24), channel_id=1, source_target_pairs={{0,1},{1,2},{2,3},{3,0},{4,5},{5,6},{6,7},{7,4},{8,9},{9,10},{10,1... | collective-permute-start | bytes 2949128 | tf_op jit(solution)/shard_map/ppermute | solution.py:206
  75.7 35.0 %collective-permute-start.7 = (bf16[288,2048]{1,0:T(8,128)(2,1)}, bf16[288,2048]{1,0:T(8,128)(2,1)S(1)}, u32[]{:S(2)}, u32[]{:S(2)}) collective-permute-start(bf16[288,2048]{1,0:T(8,128)(2,1)} %collective-permute-done.refs_3_), channel_id=1, source_target_pairs={{0,1},{1,2},{2,3},{3,0},{4,5},{5,6},{6,7},{7,4},{8,9},{9,10},{10,1... | collective-permute-start | bytes 3538952 | tf_op jit(solution)/shard_map/ppermute | solution.py:206
  78.8 31.9 %collective-permute-start.8 = (bf16[240,2048]{1,0:T(8,128)(2,1)}, bf16[240,2048]{1,0:T(8,128)(2,1)S(1)}, u32[]{:S(2)}, u32[]{:S(2)}) collective-permute-start(bf16[240,2048]{1,0:T(8,128)(2,1)} %collective-permute-done.1.refs_6_), channel_id=1, source_target_pairs={{0,3},{1,0},{2,1},{3,2},{4,7},{5,4},{6,5},{7,6},{8,11},{9,8},{10,9... | collective-permute-start | bytes 2949128 | tf_op jit(solution)/shard_map/ppermute | solution.py:206
  82.2 15.8 %collective-permute-start.4 = (bf16[128,2048]{1,0:T(8,128)(2,1)S(1)}, bf16[128,2048]{1,0:T(8,128)(2,1)S(1)}, u32[]{:S(2)}, u32[]{:S(2)}) collective-permute-start(bf16[128,2048]{1,0:T(8,128)(2,1)S(1)} %get-tuple-element.27), channel_id=1, source_target_pairs={{0,8},{1,9},{2,10},{3,11},{4,12},{5,13},{6,14},{7,15},{8,0},{9,1},... | collective-permute-start | bytes 1572872 | tf_op jit(solution)/shard_map/ppermute | solution.py:242
  87.1 23.6 %collective-permute-start.5 = (bf16[128,2048]{1,0:T(8,128)(2,1)S(1)}, bf16[128,2048]{1,0:T(8,128)(2,1)S(1)}, u32[]{:S(2)}, u32[]{:S(2)}) collective-permute-start(bf16[128,2048]{1,0:T(8,128)(2,1)S(1)} %get-tuple-element.27), channel_id=1, source_target_pairs={{0,12},{1,13},{2,14},{3,15},{4,8},{5,9},{6,10},{7,11},{8,4},{9,5},... | collective-permute-start | bytes 1572872 | tf_op jit(solution)/shard_map/ppermute | solution.py:242
  89.8 21.0 %collective-permute-start.6 = (bf16[128,2048]{1,0:T(8,128)(2,1)S(1)}, bf16[128,2048]{1,0:T(8,128)(2,1)S(1)}, u32[]{:S(2)}, u32[]{:S(2)}) collective-permute-start(bf16[128,2048]{1,0:T(8,128)(2,1)S(1)} %get-tuple-element.28.refs_3_), channel_id=1, source_target_pairs={{0,4},{1,5},{2,6},{3,7},{4,0},{5,1},{6,2},{7,3},{8,12},{9,13},{10,... | collective-permute-start | bytes 1572872 | tf_op jit(solution)/shard_map/ppermute | solution.py:242
  133.3 40.3 %copy-start.3 = (s32[16,4]{0,1:T(4,128)S(1)}, s32[16,4]{0,1:T(4,128)}, u32[]{:S(2)}) copy-start(s32[16,4]{0,1:T(4,128)} %param.10) | copy-start | bytes 772

commit v9 on v8

--- a/solution.py
+++ b/solution.py
@@ -236,9 +236,7 @@
     left_early, right_late = shift(early, 1), shift(late, -1)
     left_late, right_early = shift(late, 1), shift(early, -1)
     own, other = _call(unpack_kernel, (_shape(4 * n_ex, width),) * 2, "unpack", small)(arrived)
-    own, left_early, right_late = lax.optimization_barrier((own, left_early, right_late))
     last = [shift(left_early, 1), shift(right_late, -1)]
-    own, other, left_late, right_early = lax.optimization_barrier((own, other, left_late, right_early))
     flip = lambda v, d: lax.ppermute(
         v, "hid", [(y * side + x, (y ^ d) * side + x) for y in range(side) for x in range(side)]
     )

time: 175 us -> 172 us (0.983)
  waiting for transfers between devices: 57.9 us -> 51.3 us
  blocking collectives: 58 us -> 59.8 us
    ppermute x6, waiting for transfers between devices: 0.02 us -> 30 us  [shift(): lax.ppermute(v, 'hid', [(y * side + x, y * side + (x + d) % side) for y i...]
    all_to_all x1, waiting for transfers between devices: 41.6 us -> 16.1 us  [per_device(): lax.all_to_all(packed, 'ex', split_axis=0, concat_axis=0, tiled=True)]
    ppermute x3, waiting for transfers between devices: 16.3 us -> 5.2 us  [per_device(): lax.ppermute(v, 'hid', [(y * side + x, (y ^ d) * side + x) for y in range...]
    all_to_all x1, blocking collectives: 39.9 us -> 41.7 us  [per_device(): lax.all_to_all(merged, 'ex', split_axis=0, concat_axis=0, tiled=True)]
  transfers between devices with their start and end apart: 10 -> 10, of which waited for: 3 -> 5; matrix products, arithmetic and copies ran while one was open for 0% -> 0% of each run, Pallas kernels for 3% -> 3%
where the time goes in v9:
time: 172 us; the launch traced here: 171 us
  blocking collectives  59.8 us (35%)
  waiting for transfers between devices  51.3 us (30%)
  starting transfers between devices  44.6 us (26%)
  Pallas kernels  15.6 us (9%)
    all_to_all x1, blocking collectives, per_device(): lax.all_to_all(merged, 'ex', split_axis=0, concat_axis=0, tiled=True)  41.7 us
    ppermute x6, waiting for transfers between devices, shift(): lax.ppermute(v, 'hid', [(y * side + x, y * side + (x + d) % side) for y i...  30 us
    ppermute x6, starting transfers between devices, shift(): lax.ppermute(v, 'hid', [(y * side + x, y * side + (x + d) % side) for y i...  18.3 us
    all_to_all x1, blocking collectives, over_y(): lax.all_to_all(v, 'hid', split_axis=0, concat_axis=0, tiled=True, axis_in...  18.1 us
    all_to_all x1, starting transfers between devices, per_device(): lax.all_to_all(packed, 'ex', split_axis=0, concat_axis=0, tiled=True)  16.9 us
    all_to_all x1, waiting for transfers between devices, per_device(): lax.all_to_all(packed, 'ex', split_axis=0, concat_axis=0, tiled=True)  16.1 us
    ppermute x3, starting transfers between devices, per_device(): lax.ppermute(v, 'hid', [(y * side + x, (y ^ d) * side + x) for y in range...  9.42 us
    pallas_call x1, Pallas kernels, per_device(): _call(grad_kernel, _shape(rows, width), 'grad', (10 * rows * hid * width,...  5.98 us
  transfers between devices with their start and end apart: 10, of which 5 were waited for; matrix products, arithmetic and copies ran while one was open for 0% of the time, Pallas kernels for 3%

profile of v9, /device:TPU:1, one launch (start us, length us, event | category | flops | bytes accessed | tf_op | source)
XLA Modules:
  0.0 171.5 jit_solution(13631590764141003875)
XLA Ops:
  0.0 2.6 %pack.1 = bf16[256,2048]{1,0:T(8,128)(2,1)} custom-call(bf16[16,2048]{1,0:T(8,128)(2,1)} %tok_in.1, bf16[16,2048]{1,0:T(8,128)(2,1)} %cot_in.1, f32[4,16]{1,0:T(4,128)} %bitcast.16, s32[4,16]{1,0:T(4,128)} %bitcast.13), custom_call_target="tpu_custom_call" | custom-call | flops 67108864 | bytes 2097152 | tf_op jit(solution)/shard_map/pack/pallas_call | solution.py:225
  2.6 16.9 %all-to-all-start = ((bf16[32,8,2048]{2,1,0:T(8,128)(2,1)}), bf16[32,8,2048]{2,1,0:T(8,128)(2,1)S(1)}, u32[]{:S(2)}, u32[]{:S(2)}) async-start(bf16[32,8,2048]{2,1,0:T(8,128)(2,1)} %bitcast.15), calls=%async_computation | async-start | bytes 2097152 | tf_op jit(solution)/shard_map/all_to_all | solution.py:235
  19.5 2.3 %split.1 = (bf16[288,2048]{1,0:T(8,128)(2,1)}, bf16[240,2048]{1,0:T(8,128)(2,1)}) custom-call(bf16[1,176,2048]{2,1,0:T(8,128)(2,1)S(1)} %copy-done, bf16[1,176,2048]{2,1,0:T(8,128)(2,1)S(1)} %copy-done.1, bf16[1,176,2048]{2,1,0:T(8,128)(2,1)S(1)} %copy-done.2), custom_call_target="tpu_custom_call" | custom-call | bytes 4325376 | tf_op jit(solution)/shard_map/split/pallas_call | solution.py:211
  21.9 3.1 %collective-permute-start.3 = (bf16[288,2048]{1,0:T(8,128)(2,1)}, bf16[288,2048]{1,0:T(8,128)(2,1)}, u32[]{:S(2)}, u32[]{:S(2)}) collective-permute-start(bf16[288,2048]{1,0:T(8,128)(2,1)} %get-tuple-element.17), channel_id=1, source_target_pairs={{0,1},{1,2},{2,3},{3,0},{4,5},{5,6},{6,7},{7,4},{8,9},{9,10},{10,1... | collective-permute-start | bytes 3538952 | tf_op jit(solution)/shard_map/ppermute | solution.py:206
  25.0 3.4 %collective-permute-start.6 = (bf16[240,2048]{1,0:T(8,128)(2,1)}, bf16[240,2048]{1,0:T(8,128)(2,1)}, u32[]{:S(2)}, u32[]{:S(2)}) collective-permute-start(bf16[240,2048]{1,0:T(8,128)(2,1)} %get-tuple-element.18), channel_id=1, source_target_pairs={{0,3},{1,0},{2,1},{3,2},{4,7},{5,4},{6,5},{7,6},{8,11},{9,8},{10,9... | collective-permute-start | bytes 2949128 | tf_op jit(solution)/shard_map/ppermute | solution.py:206
  28.4 3.2 %collective-permute-start.5 = (bf16[288,2048]{1,0:T(8,128)(2,1)}, bf16[288,2048]{1,0:T(8,128)(2,1)}, u32[]{:S(2)}, u32[]{:S(2)}) collective-permute-start(bf16[288,2048]{1,0:T(8,128)(2,1)} %get-tuple-element.17), channel_id=1, source_target_pairs={{0,3},{1,0},{2,1},{3,2},{4,7},{5,4},{6,5},{7,6},{8,11},{9,8},{10,9... | collective-permute-start | bytes 3538952 | tf_op jit(solution)/shard_map/ppermute | solution.py:206
  31.6 2.1 %collective-permute-start.4 = (bf16[240,2048]{1,0:T(8,128)(2,1)}, bf16[240,2048]{1,0:T(8,128)(2,1)}, u32[]{:S(2)}, u32[]{:S(2)}) collective-permute-start(bf16[240,2048]{1,0:T(8,128)(2,1)} %get-tuple-element.18), channel_id=1, source_target_pairs={{0,1},{1,2},{2,3},{3,0},{4,5},{5,6},{6,7},{7,4},{8,9},{9,10},{10,1... | collective-permute-start | bytes 2949128 | tf_op jit(solution)/shard_map/ppermute | solution.py:206
  33.7 18.9 %collective-permute-done.3.refs_3_ = bf16[288,2048]{1,0:T(8,128)(2,1)} collective-permute-done((bf16[288,2048]{1,0:T(8,128)(2,1)}, bf16[288,2048]{1,0:T(8,128)(2,1)}, u32[]{:S(2)}, u32[]{:S(2)}) %collective-permute-start.3) | collective-permute-done | bytes 1179680 | tf_op jit(solution)/shard_map/ppermute | solution.py:206
  52.6 1.9 %collective-permute-start.7 = (bf16[288,2048]{1,0:T(8,128)(2,1)}, bf16[288,2048]{1,0:T(8,128)(2,1)}, u32[]{:S(2)}, u32[]{:S(2)}) collective-permute-start(bf16[288,2048]{1,0:T(8,128)(2,1)} %collective-permute-done.3.refs_3_), channel_id=1, source_target_pairs={{0,1},{1,2},{2,3},{3,0},{4,5},{5,6},{6,7},{7,4},{8,9},{9,10},{10,1... | collective-permute-start | bytes 3538952 | tf_op jit(solution)/shard_map/ppermute | solution.py:206
  54.5 4.6 %collective-permute-start.8 = (bf16[240,2048]{1,0:T(8,128)(2,1)}, bf16[240,2048]{1,0:T(8,128)(2,1)}, u32[]{:S(2)}, u32[]{:S(2)}) collective-permute-start(bf16[240,2048]{1,0:T(8,128)(2,1)} %collective-permute-done.6.refs_6_), channel_id=1, source_target_pairs={{0,3},{1,0},{2,1},{3,2},{4,7},{5,4},{6,5},{7,6},{8,11},{9,8},{10,9... | collective-permute-start | bytes 2949128 | tf_op jit(solution)/shard_map/ppermute | solution.py:206
  59.1 16.1 %all-to-all-done = bf16[32,8,2048]{2,1,0:T(8,128)(2,1)S(1)} async-done(((bf16[32,8,2048]{2,1,0:T(8,128)(2,1)}), bf16[32,8,2048]{2,1,0:T(8,128)(2,1)S(1)}, u32[]{:S(2)}, u32[]{:S(2)}) %all-to-all-start) | async-done | bytes 1048608 | tf_op jit(solution)/shard_map/all_to_all | solution.py:235
  75.2 0.5 unpack.1
  75.7 4.8 %collective-permute-start = (bf16[128,2048]{1,0:T(8,128)(2,1)S(1)}, bf16[128,2048]{1,0:T(8,128)(2,1)S(1)}, u32[]{:S(2)}, u32[]{:S(2)}) collective-permute-start(bf16[128,2048]{1,0:T(8,128)(2,1)S(1)} %get-tuple-element.15), channel_id=1, source_target_pairs={{0,8},{1,9},{2,10},{3,11},{4,12},{5,13},{6,14},{7,15},{8,0},{9,1},... | collective-permute-start | bytes 1572872 | tf_op jit(solution)/shard_map/ppermute | solution.py:240
  80.5 2.7 %collective-permute-start.1 = (bf16[128,2048]{1,0:T(8,128)(2,1)S(1)}, bf16[128,2048]{1,0:T(8,128)(2,1)S(1)}, u32[]{:S(2)}, u32[]{:S(2)}) collective-permute-start(bf16[128,2048]{1,0:T(8,128)(2,1)S(1)} %get-tuple-element.15), channel_id=1, source_target_pairs={{0,12},{1,13},{2,14},{3,15},{4,8},{5,9},{6,10},{7,11},{8,4},{9,5},... | collective-permute-start | bytes 1572872 | tf_op jit(solution)/shard_map/ppermute | solution.py:240
  83.2 1.9 %collective-permute-start.2 = (bf16[128,2048]{1,0:T(8,128)(2,1)S(1)}, bf16[128,2048]{1,0:T(8,128)(2,1)S(1)}, u32[]{:S(2)}, u32[]{:S(2)}) collective-permute-start(bf16[128,2048]{1,0:T(8,128)(2,1)S(1)} %get-tuple-element.16.refs_3_), channel_id=1, source_target_pairs={{0,4},{1,5},{2,6},{3,7},{4,0},{5,1},{6,2},{7,3},{8,12},{9,13},{10,... | collective-permute-start | bytes 1572872 | tf_op jit(solution)/shard_map/ppermute | solution.py:240
  85.2 2.7 %stage.1 = (bf16[512,2048]{1,0:T(8,128)(2,1)S(1)}, bf16[512,2048]{1,0:T(8,128)(2,1)S(1)}, bf16[512,2048]{1,0:T(8,128)(2,1)S(1)}, bf16[16,2048]{1,0:T(8,128)(2,1)...) custom-call(bf16[1,176,2048]{2,1,0:T(8,128)(2,1)S(1)} %copy-done, bf16[1,176,2048]{2,1,0:T(8,128)(2,1)S(1)} %copy-done.1, ...), custom_call_target="tpu_custom_call" | custom-call | bytes 25952256 | tf_op jit(solution)/shard_map/stage/pallas_call | solution.py:247
  87.9 8.5 %collective-permute-done.8.refs_11_ = bf16[240,2048]{1,0:T(8,128)(2,1)} collective-permute-done((bf16[240,2048]{1,0:T(8,128)(2,1)}, bf16[240,2048]{1,0:T(8,128)(2,1)}, u32[]{:S(2)}, u32[]{:S(2)}) %collective-permute-start.8) | collective-permute-done | bytes 983072 | tf_op jit(solution)/shard_map/ppermute | solution.py:206
  96.4 2.6 %collective-permute-done.7.refs_10_ = bf16[288,2048]{1,0:T(8,128)(2,1)} collective-permute-done((bf16[288,2048]{1,0:T(8,128)(2,1)}, bf16[288,2048]{1,0:T(8,128)(2,1)}, u32[]{:S(2)}, u32[]{:S(2)}) %collective-permute-start.7) | collective-permute-done | bytes 1179680 | tf_op jit(solution)/shard_map/ppermute | solution.py:206
  99.0 5.2 %collective-permute-done.1.refs_1_ = bf16[128,2048]{1,0:T(8,128)(2,1)S(1)} collective-permute-done((bf16[128,2048]{1,0:T(8,128)(2,1)S(1)}, bf16[128,2048]{1,0:T(8,128)(2,1)S(1)}, u32[]{:S(2)}, u32[]{:S(2)}) %collective-permute-start.1) | collective-permute-done | bytes 524320 | tf_op jit(solution)/shard_map/ppermute | solution.py:240
  104.2 6.0 %grad.1 = bf16[256,2048]{1,0:T(8,128)(2,1)S(1)} custom-call(bf16[128,2048]{1,0:T(8,128)(2,1)S(1)} %collective-permute-done.refs_0_, bf16[128,2048]{1,0:T(8,128)(2,1)S(1)} %collective-permute-done.1.refs_1_, bf16[128,2048]{1,0:T(8,128)(2,1)S(1)} %collective-permute-done.2.refs_2_, bf16[128,2048]{1,0:T(8,128)(2,1)S(1)} %get-tuple-element.16.refs_3_, ...), custom_call_target="tpu_custom_call" | custom-call | flops 3690987520 | bytes 8650752 | tf_op jit(solution)/shard_map/grad/pallas_call | solution.py:256
  110.2 18.1 %all_to_all.33 = bf16[4,64,2048]{2,1,0:T(8,128)(2,1)S(1)} all-to-all(bf16[4,64,2048]{2,1,0:T(8,128)(2,1)S(1)} %bitcast.12), channel_id=1, replica_groups={{0,4,8,12},{1,5,9,13},{2,6,10,14},{3,7,11,15},{16,20,24,28},{17,21,25,2..., dimensions={0} | all-to-all | bytes 2097152 | tf_op jit(solution)/shard_map/all_to_all | solution.py:220
  128.2 0.4 merge.1
  128.7 41.7 %all_to_all.34 = bf16[32,8,1024]{2,1,0:T(8,128)(2,1)S(1)} all-to-all(bf16[32,8,1024]{2,1,0:T(8,128)(2,1)S(1)} %bitcast.10), channel_id=1, replica_groups=mesh['ex'=32,'hid'=16] {'ex'}, dimensions={0} | all-to-all | bytes 1048576 | tf_op jit(solution)/shard_map/all_to_all | solution.py:265
  170.4 1.1 final.1
  (13 shorter events, 0.0 us)
Async XLA Ops:
  0.0 19.5 %copy-start.2 = (bf16[1,176,2048]{2,1,0:T(8,128)(2,1)S(1)}, bf16[1,176,2048]{2,1,0:T(8,128)(2,1)}, u32[]{:S(2)}) copy-start(bf16[1,176,2048]{2,1,0:T(8,128)(2,1)} %refs_2_.3) | copy-start | bytes 2162692
  2.6 16.9 %copy-start = (bf16[1,176,2048]{2,1,0:T(8,128)(2,1)S(1)}, bf16[1,176,2048]{2,1,0:T(8,128)(2,1)}, u32[]{:S(2)}) copy-start(bf16[1,176,2048]{2,1,0:T(8,128)(2,1)} %refs_0_.3) | copy-start | bytes 2162692
  2.6 16.9 %copy-start.1 = (bf16[1,176,2048]{2,1,0:T(8,128)(2,1)S(1)}, bf16[1,176,2048]{2,1,0:T(8,128)(2,1)}, u32[]{:S(2)}) copy-start(bf16[1,176,2048]{2,1,0:T(8,128)(2,1)} %refs_1_.3) | copy-start | bytes 2162692
  2.6 72.6 %all-to-all-start = ((bf16[32,8,2048]{2,1,0:T(8,128)(2,1)}), bf16[32,8,2048]{2,1,0:T(8,128)(2,1)S(1)}, u32[]{:S(2)}, u32[]{:S(2)}) async-start(bf16[32,8,2048]{2,1,0:T(8,128)(2,1)} %bitcast.15), calls=%async_computation | async-start | bytes 2097152 | tf_op jit(solution)/shard_map/all_to_all | solution.py:235
  21.9 30.8 %collective-permute-start.3 = (bf16[288,2048]{1,0:T(8,128)(2,1)}, bf16[288,2048]{1,0:T(8,128)(2,1)}, u32[]{:S(2)}, u32[]{:S(2)}) collective-permute-start(bf16[288,2048]{1,0:T(8,128)(2,1)} %get-tuple-element.17), channel_id=1, source_target_pairs={{0,1},{1,2},{2,3},{3,0},{4,5},{5,6},{6,7},{7,4},{8,9},{9,10},{10,1... | collective-permute-start | bytes 3538952 | tf_op jit(solution)/shard_map/ppermute | solution.py:206
  25.0 29.5 %collective-permute-start.6 = (bf16[240,2048]{1,0:T(8,128)(2,1)}, bf16[240,2048]{1,0:T(8,128)(2,1)}, u32[]{:S(2)}, u32[]{:S(2)}) collective-permute-start(bf16[240,2048]{1,0:T(8,128)(2,1)} %get-tuple-element.18), channel_id=1, source_target_pairs={{0,3},{1,0},{2,1},{3,2},{4,7},{5,4},{6,5},{7,6},{8,11},{9,8},{10,9... | collective-permute-start | bytes 2949128 | tf_op jit(solution)/shard_map/ppermute | solution.py:206
  28.4 54.8 %collective-permute-start.5 = (bf16[288,2048]{1,0:T(8,128)(2,1)}, bf16[288,2048]{1,0:T(8,128)(2,1)}, u32[]{:S(2)}, u32[]{:S(2)}) collective-permute-start(bf16[288,2048]{1,0:T(8,128)(2,1)} %get-tuple-element.17), channel_id=1, source_target_pairs={{0,3},{1,0},{2,1},{3,2},{4,7},{5,4},{6,5},{7,6},{8,11},{9,8},{10,9... | collective-permute-start | bytes 3538952 | tf_op jit(solution)/shard_map/ppermute | solution.py:206
  31.6 49.0 %collective-permute-start.4 = (bf16[240,2048]{1,0:T(8,128)(2,1)}, bf16[240,2048]{1,0:T(8,128)(2,1)}, u32[]{:S(2)}, u32[]{:S(2)}) collective-permute-start(bf16[240,2048]{1,0:T(8,128)(2,1)} %get-tuple-element.18), channel_id=1, source_target_pairs={{0,1},{1,2},{2,3},{3,0},{4,5},{5,6},{6,7},{7,4},{8,9},{9,10},{10,1... | collective-permute-start | bytes 2949128 | tf_op jit(solution)/shard_map/ppermute | solution.py:206
  52.6 46.3 %collective-permute-start.7 = (bf16[288,2048]{1,0:T(8,128)(2,1)}, bf16[288,2048]{1,0:T(8,128)(2,1)}, u32[]{:S(2)}, u32[]{:S(2)}) collective-permute-start(bf16[288,2048]{1,0:T(8,128)(2,1)} %collective-permute-done.3.refs_3_), channel_id=1, source_target_pairs={{0,1},{1,2},{2,3},{3,0},{4,5},{5,6},{6,7},{7,4},{8,9},{9,10},{10,1... | collective-permute-start | bytes 3538952 | tf_op jit(solution)/shard_map/ppermute | solution.py:206
  54.5 41.8 %collective-permute-start.8 = (bf16[240,2048]{1,0:T(8,128)(2,1)}, bf16[240,2048]{1,0:T(8,128)(2,1)}, u32[]{:S(2)}, u32[]{:S(2)}) collective-permute-start(bf16[240,2048]{1,0:T(8,128)(2,1)} %collective-permute-done.6.refs_6_), channel_id=1, source_target_pairs={{0,3},{1,0},{2,1},{3,2},{4,7},{5,4},{6,5},{7,6},{8,11},{9,8},{10,9... | collective-permute-start | bytes 2949128 | tf_op jit(solution)/shard_map/ppermute | solution.py:206
  75.7 23.3 %collective-permute-start = (bf16[128,2048]{1,0:T(8,128)(2,1)S(1)}, bf16[128,2048]{1,0:T(8,128)(2,1)S(1)}, u32[]{:S(2)}, u32[]{:S(2)}) collective-permute-start(bf16[128,2048]{1,0:T(8,128)(2,1)S(1)} %get-tuple-element.15), channel_id=1, source_target_pairs={{0,8},{1,9},{2,10},{3,11},{4,12},{5,13},{6,14},{7,15},{8,0},{9,1},... | collective-permute-start | bytes 1572872 | tf_op jit(solution)/shard_map/ppermute | solution.py:240
  80.5 23.6 %collective-permute-start.1 = (bf16[128,2048]{1,0:T(8,128)(2,1)S(1)}, bf16[128,2048]{1,0:T(8,128)(2,1)S(1)}, u32[]{:S(2)}, u32[]{:S(2)}) collective-permute-start(bf16[128,2048]{1,0:T(8,128)(2,1)S(1)} %get-tuple-element.15), channel_id=1, source_target_pairs={{0,12},{1,13},{2,14},{3,15},{4,8},{5,9},{6,10},{7,11},{8,4},{9,5},... | collective-permute-start | bytes 1572872 | tf_op jit(solution)/shard_map/ppermute | solution.py:240
  83.2 20.9 %collective-permute-start.2 = (bf16[128,2048]{1,0:T(8,128)(2,1)S(1)}, bf16[128,2048]{1,0:T(8,128)(2,1)S(1)}, u32[]{:S(2)}, u32[]{:S(2)}) collective-permute-start(bf16[128,2048]{1,0:T(8,128)(2,1)S(1)} %get-tuple-element.16.refs_3_), channel_id=1, source_target_pairs={{0,4},{1,5},{2,6},{3,7},{4,0},{5,1},{6,2},{7,3},{8,12},{9,13},{10,... | collective-permute-start | bytes 1572872 | tf_op jit(solution)/shard_map/ppermute | solution.py:240
  128.2 42.2 %copy-start.3 = (s32[16,4]{0,1:T(4,128)S(1)}, s32[16,4]{0,1:T(4,128)}, u32[]{:S(2)}) copy-start(s32[16,4]{0,1:T(4,128)} %param.10) | copy-start | bytes 772

commit v10 on v9

--- a/solution.py
+++ b/solution.py
@@ -115,24 +115,35 @@
 def grad_kernel(*refs):
     n = 4
     rows_in, mains, rests, last, out = refs[:n], refs[n : n + 3], refs[n + 3 : n + 6], refs[n + 6 : n + 8], refs[n + 8]
-    x, y, tails = refs[n + 9], refs[n + 10], refs[n + 11 :]
+    x, y, tails, sem = refs[n + 9], refs[n + 10], refs[n + 11 : n + 14], refs[n + 14]
+    copies = []
+    for m in range(3):
+        at = rests[m].shape[0]
+        for piece in last:
+            size = piece.shape[0] // 3
+            copies.append(
+                pltpu.make_async_copy(
+                    piece.at[pl.ds(m * size, size)], tails[m].at[pl.ds(at, size)], sem.at[len(copies)]
+                )
+            )
+            at += size
+    for cp in copies:
+        cp.start()
     half = rows_in[0].shape[0] // 2
     me = lax.axis_index("hid") // n
     for i, d in enumerate((2, 3, 1, 0)):
         at = pl.ds(pl.multiple_of(jnp.bitwise_xor(me, d) * half, half), half)
         x[at, :] = rows_in[i][0:half, :]
         y[at, :] = rows_in[i][half : 2 * half, :]
-    for m in range(3):
-        at = rests[m].shape[0]
-        tails[m][0:at, :] = rests[m][...]
-        for piece in last:
-            size = piece.shape[0] // 3
-            tails[m][at : at + size, :] = piece[m * size : (m + 1) * size, :]
-            at += size
     dims = (((1,), (1,)), ((), ()))
     dot = lambda a, w: lax.dot_general(a[...], w[...], dims, preferred_element_type=F32)
     inner = []
     for w in (mains, tails):
+        if w is tails:
+            for m in range(3):
+                tails[m][0 : rests[m].shape[0], :] = rests[m][...]
+            for cp in copies:
+                cp.wait()
         gv, uv, hv = dot(x, w[0]), dot(x, w[1]), dot(y, w[2])
         sig = jax.nn.sigmoid(gv)
         d_up = (hv * gv * sig).astype(BF)
@@ -259,7 +270,10 @@
         "grad",
         (10 * rows * hid * width, 6 * hid * width),
         vmem=36,
-        scratch_shapes=[pltpu.VMEM((rows, width), BF)] * 2 + [pltpu.VMEM((rest + unit, width), BF)] * 3,
+        in_specs=[pl.BlockSpec(memory_space=pltpu.VMEM)] * 10 + [pl.BlockSpec(memory_space=pl.ANY)] * 2,
+        scratch_shapes=[pltpu.VMEM((rows, width), BF)] * 2
+        + [pltpu.VMEM((rest + unit, width), BF)] * 3
+        + [pltpu.SemaphoreType.DMA((6,))],
     )(*rows_all, *staged, *last)
     merged = _call(merge_kernel, _shape(8 * n_ex, width // 2), "merge", small)(over_y(parts))
     landed = lax.all_to_all(merged, "ex", split_axis=0, concat_axis=0, tiled=True)

time: 172 us -> 173 us (level)
  no operation moved by 1% of the time
where the time goes in v10:
time: 173 us; the launch traced here: 172 us
  blocking collectives  59.8 us (35%)
  waiting for transfers between devices  51.3 us (30%)
  starting transfers between devices  44.6 us (26%)
  Pallas kernels  16 us (9%)
    all_to_all x1, blocking collectives, per_device(): lax.all_to_all(merged, 'ex', split_axis=0, concat_axis=0, tiled=True)  41.7 us
    ppermute x6, waiting for transfers between devices, shift(): lax.ppermute(v, 'hid', [(y * side + x, y * side + (x + d) % side) for y i...  30 us
    ppermute x6, starting transfers between devices, shift(): lax.ppermute(v, 'hid', [(y * side + x, y * side + (x + d) % side) for y i...  18.3 us
    all_to_all x1, blocking collectives, over_y(): lax.all_to_all(v, 'hid', split_axis=0, concat_axis=0, tiled=True, axis_in...  18.1 us
    all_to_all x1, starting transfers between devices, per_device(): lax.all_to_all(packed, 'ex', split_axis=0, concat_axis=0, tiled=True)  16.9 us
    all_to_all x1, waiting for transfers between devices, per_device(): lax.all_to_all(packed, 'ex', split_axis=0, concat_axis=0, tiled=True)  16.1 us
    ppermute x3, starting transfers between devices, per_device(): lax.ppermute(v, 'hid', [(y * side + x, (y ^ d) * side + x) for y in range...  9.42 us
    pallas_call x1, Pallas kernels, per_device(): _call(grad_kernel, _shape(rows, width), 'grad', (10 * rows * hid * width,...  6.47 us
  transfers between devices with their start and end apart: 10, of which 5 were waited for; matrix products, arithmetic and copies ran while one was open for 0% of the time, Pallas kernels for 3%

profile of v10, /device:TPU:1, one launch (start us, length us, event | category | flops | bytes accessed | tf_op | source)
XLA Modules:
  0.0 172.0 jit_solution(11664930886084660969)
XLA Ops:
  0.0 2.6 %pack.1 = bf16[256,2048]{1,0:T(8,128)(2,1)} custom-call(bf16[16,2048]{1,0:T(8,128)(2,1)} %tok_in.1, bf16[16,2048]{1,0:T(8,128)(2,1)} %cot_in.1, f32[4,16]{1,0:T(4,128)} %bitcast.16, s32[4,16]{1,0:T(4,128)} %bitcast.13), custom_call_target="tpu_custom_call" | custom-call | flops 67108864 | bytes 2097152 | tf_op jit(solution)/shard_map/pack/pallas_call | solution.py:236
  2.6 16.9 %all-to-all-start = ((bf16[32,8,2048]{2,1,0:T(8,128)(2,1)}), bf16[32,8,2048]{2,1,0:T(8,128)(2,1)S(1)}, u32[]{:S(2)}, u32[]{:S(2)}) async-start(bf16[32,8,2048]{2,1,0:T(8,128)(2,1)} %bitcast.15), calls=%async_computation | async-start | bytes 2097152 | tf_op jit(solution)/shard_map/all_to_all | solution.py:246
  19.5 2.3 %split.1 = (bf16[288,2048]{1,0:T(8,128)(2,1)}, bf16[240,2048]{1,0:T(8,128)(2,1)}) custom-call(bf16[1,176,2048]{2,1,0:T(8,128)(2,1)S(1)} %copy-done, bf16[1,176,2048]{2,1,0:T(8,128)(2,1)S(1)} %copy-done.1, bf16[1,176,2048]{2,1,0:T(8,128)(2,1)S(1)} %copy-done.2), custom_call_target="tpu_custom_call" | custom-call | bytes 4325376 | tf_op jit(solution)/shard_map/split/pallas_call | solution.py:222
  21.9 3.1 %collective-permute-start.3 = (bf16[288,2048]{1,0:T(8,128)(2,1)}, bf16[288,2048]{1,0:T(8,128)(2,1)}, u32[]{:S(2)}, u32[]{:S(2)}) collective-permute-start(bf16[288,2048]{1,0:T(8,128)(2,1)} %get-tuple-element.17), channel_id=1, source_target_pairs={{0,1},{1,2},{2,3},{3,0},{4,5},{5,6},{6,7},{7,4},{8,9},{9,10},{10,1... | collective-permute-start | bytes 3538952 | tf_op jit(solution)/shard_map/ppermute | solution.py:217
  25.0 3.4 %collective-permute-start.6 = (bf16[240,2048]{1,0:T(8,128)(2,1)}, bf16[240,2048]{1,0:T(8,128)(2,1)}, u32[]{:S(2)}, u32[]{:S(2)}) collective-permute-start(bf16[240,2048]{1,0:T(8,128)(2,1)} %get-tuple-element.18), channel_id=1, source_target_pairs={{0,3},{1,0},{2,1},{3,2},{4,7},{5,4},{6,5},{7,6},{8,11},{9,8},{10,9... | collective-permute-start | bytes 2949128 | tf_op jit(solution)/shard_map/ppermute | solution.py:217
  28.4 3.2 %collective-permute-start.5 = (bf16[288,2048]{1,0:T(8,128)(2,1)}, bf16[288,2048]{1,0:T(8,128)(2,1)}, u32[]{:S(2)}, u32[]{:S(2)}) collective-permute-start(bf16[288,2048]{1,0:T(8,128)(2,1)} %get-tuple-element.17), channel_id=1, source_target_pairs={{0,3},{1,0},{2,1},{3,2},{4,7},{5,4},{6,5},{7,6},{8,11},{9,8},{10,9... | collective-permute-start | bytes 3538952 | tf_op jit(solution)/shard_map/ppermute | solution.py:217
  31.6 2.1 %collective-permute-start.4 = (bf16[240,2048]{1,0:T(8,128)(2,1)}, bf16[240,2048]{1,0:T(8,128)(2,1)}, u32[]{:S(2)}, u32[]{:S(2)}) collective-permute-start(bf16[240,2048]{1,0:T(8,128)(2,1)} %get-tuple-element.18), channel_id=1, source_target_pairs={{0,1},{1,2},{2,3},{3,0},{4,5},{5,6},{6,7},{7,4},{8,9},{9,10},{10,1... | collective-permute-start | bytes 2949128 | tf_op jit(solution)/shard_map/ppermute | solution.py:217
  33.7 18.9 %collective-permute-done.3.refs_3_ = bf16[288,2048]{1,0:T(8,128)(2,1)} collective-permute-done((bf16[288,2048]{1,0:T(8,128)(2,1)}, bf16[288,2048]{1,0:T(8,128)(2,1)}, u32[]{:S(2)}, u32[]{:S(2)}) %collective-permute-start.3) | collective-permute-done | bytes 1179680 | tf_op jit(solution)/shard_map/ppermute | solution.py:217
  52.6 1.9 %collective-permute-start.7 = (bf16[288,2048]{1,0:T(8,128)(2,1)}, bf16[288,2048]{1,0:T(8,128)(2,1)}, u32[]{:S(2)}, u32[]{:S(2)}) collective-permute-start(bf16[288,2048]{1,0:T(8,128)(2,1)} %collective-permute-done.3.refs_3_), channel_id=1, source_target_pairs={{0,1},{1,2},{2,3},{3,0},{4,5},{5,6},{6,7},{7,4},{8,9},{9,10},{10,1... | collective-permute-start | bytes 3538952 | tf_op jit(solution)/shard_map/ppermute | solution.py:217
  54.5 4.6 %collective-permute-start.8 = (bf16[240,2048]{1,0:T(8,128)(2,1)}, bf16[240,2048]{1,0:T(8,128)(2,1)}, u32[]{:S(2)}, u32[]{:S(2)}) collective-permute-start(bf16[240,2048]{1,0:T(8,128)(2,1)} %collective-permute-done.6.refs_6_), channel_id=1, source_target_pairs={{0,3},{1,0},{2,1},{3,2},{4,7},{5,4},{6,5},{7,6},{8,11},{9,8},{10,9... | collective-permute-start | bytes 2949128 | tf_op jit(solution)/shard_map/ppermute | solution.py:217
  59.1 16.1 %all-to-all-done = bf16[32,8,2048]{2,1,0:T(8,128)(2,1)S(1)} async-done(((bf16[32,8,2048]{2,1,0:T(8,128)(2,1)}), bf16[32,8,2048]{2,1,0:T(8,128)(2,1)S(1)}, u32[]{:S(2)}, u32[]{:S(2)}) %all-to-all-start) | async-done | bytes 1048608 | tf_op jit(solution)/shard_map/all_to_all | solution.py:246
  75.2 0.5 unpack.1
  75.7 4.8 %collective-permute-start = (bf16[128,2048]{1,0:T(8,128)(2,1)S(1)}, bf16[128,2048]{1,0:T(8,128)(2,1)S(1)}, u32[]{:S(2)}, u32[]{:S(2)}) collective-permute-start(bf16[128,2048]{1,0:T(8,128)(2,1)S(1)} %get-tuple-element.15), channel_id=1, source_target_pairs={{0,8},{1,9},{2,10},{3,11},{4,12},{5,13},{6,14},{7,15},{8,0},{9,1},... | collective-permute-start | bytes 1572872 | tf_op jit(solution)/shard_map/ppermute | solution.py:251
  80.5 2.7 %collective-permute-start.1 = (bf16[128,2048]{1,0:T(8,128)(2,1)S(1)}, bf16[128,2048]{1,0:T(8,128)(2,1)S(1)}, u32[]{:S(2)}, u32[]{:S(2)}) collective-permute-start(bf16[128,2048]{1,0:T(8,128)(2,1)S(1)} %get-tuple-element.15), channel_id=1, source_target_pairs={{0,12},{1,13},{2,14},{3,15},{4,8},{5,9},{6,10},{7,11},{8,4},{9,5},... | collective-permute-start | bytes 1572872 | tf_op jit(solution)/shard_map/ppermute | solution.py:251
  83.2 1.9 %collective-permute-start.2 = (bf16[128,2048]{1,0:T(8,128)(2,1)S(1)}, bf16[128,2048]{1,0:T(8,128)(2,1)S(1)}, u32[]{:S(2)}, u32[]{:S(2)}) collective-permute-start(bf16[128,2048]{1,0:T(8,128)(2,1)S(1)} %get-tuple-element.16.refs_3_), channel_id=1, source_target_pairs={{0,4},{1,5},{2,6},{3,7},{4,0},{5,1},{6,2},{7,3},{8,12},{9,13},{10,... | collective-permute-start | bytes 1572872 | tf_op jit(solution)/shard_map/ppermute | solution.py:251
  85.2 2.7 %stage.1 = (bf16[512,2048]{1,0:T(8,128)(2,1)S(1)}, bf16[512,2048]{1,0:T(8,128)(2,1)S(1)}, bf16[512,2048]{1,0:T(8,128)(2,1)S(1)}, bf16[16,2048]{1,0:T(8,128)(2,1)...) custom-call(bf16[1,176,2048]{2,1,0:T(8,128)(2,1)S(1)} %copy-done, bf16[1,176,2048]{2,1,0:T(8,128)(2,1)S(1)} %copy-done.1, ...), custom_call_target="tpu_custom_call" | custom-call | bytes 25952256 | tf_op jit(solution)/shard_map/stage/pallas_call | solution.py:258
  87.9 8.5 %collective-permute-done.8.refs_11_ = bf16[240,2048]{1,0:T(8,128)(2,1)} collective-permute-done((bf16[240,2048]{1,0:T(8,128)(2,1)}, bf16[240,2048]{1,0:T(8,128)(2,1)}, u32[]{:S(2)}, u32[]{:S(2)}) %collective-permute-start.8) | collective-permute-done | bytes 983072 | tf_op jit(solution)/shard_map/ppermute | solution.py:217
  96.4 2.6 %collective-permute-done.7.refs_10_ = bf16[288,2048]{1,0:T(8,128)(2,1)} collective-permute-done((bf16[288,2048]{1,0:T(8,128)(2,1)}, bf16[288,2048]{1,0:T(8,128)(2,1)}, u32[]{:S(2)}, u32[]{:S(2)}) %collective-permute-start.7) | collective-permute-done | bytes 1179680 | tf_op jit(solution)/shard_map/ppermute | solution.py:217
  99.0 5.2 %collective-permute-done.1.refs_1_ = bf16[128,2048]{1,0:T(8,128)(2,1)S(1)} collective-permute-done((bf16[128,2048]{1,0:T(8,128)(2,1)S(1)}, bf16[128,2048]{1,0:T(8,128)(2,1)S(1)}, u32[]{:S(2)}, u32[]{:S(2)}) %collective-permute-start.1) | collective-permute-done | bytes 524320 | tf_op jit(solution)/shard_map/ppermute | solution.py:251
  104.2 6.5 %grad.1 = bf16[256,2048]{1,0:T(8,128)(2,1)S(1)} custom-call(bf16[128,2048]{1,0:T(8,128)(2,1)S(1)} %collective-permute-done.refs_0_, bf16[128,2048]{1,0:T(8,128)(2,1)S(1)} %collective-permute-done.1.refs_1_, bf16[128,2048]{1,0:T(8,128)(2,1)S(1)} %collective-permute-done.2.refs_2_, bf16[128,2048]{1,0:T(8,128)(2,1)S(1)} %get-tuple-element.16.refs_3_, ...), custom_call_target="tpu_custom_call" | custom-call | flops 3690987520 | bytes 8650752 | tf_op jit(solution)/shard_map/grad/pallas_call | solution.py:267
  110.6 18.1 %all_to_all.33 = bf16[4,64,2048]{2,1,0:T(8,128)(2,1)S(1)} all-to-all(bf16[4,64,2048]{2,1,0:T(8,128)(2,1)S(1)} %bitcast.12), channel_id=1, replica_groups={{0,4,8,12},{1,5,9,13},{2,6,10,14},{3,7,11,15},{16,20,24,28},{17,21,25,2..., dimensions={0} | all-to-all | bytes 2097152 | tf_op jit(solution)/shard_map/all_to_all | solution.py:231
  128.8 0.4 merge.1
  129.2 41.7 %all_to_all.34 = bf16[32,8,1024]{2,1,0:T(8,128)(2,1)S(1)} all-to-all(bf16[32,8,1024]{2,1,0:T(8,128)(2,1)S(1)} %bitcast.10), channel_id=1, replica_groups=mesh['ex'=32,'hid'=16] {'ex'}, dimensions={0} | all-to-all | bytes 1048576 | tf_op jit(solution)/shard_map/all_to_all | solution.py:279
  170.9 1.1 final.1
  (13 shorter events, 0.0 us)
Async XLA Ops:
  0.0 19.5 %copy-start.2 = (bf16[1,176,2048]{2,1,0:T(8,128)(2,1)S(1)}, bf16[1,176,2048]{2,1,0:T(8,128)(2,1)}, u32[]{:S(2)}) copy-start(bf16[1,176,2048]{2,1,0:T(8,128)(2,1)} %refs_2_.3) | copy-start | bytes 2162692
  2.6 16.9 %copy-start = (bf16[1,176,2048]{2,1,0:T(8,128)(2,1)S(1)}, bf16[1,176,2048]{2,1,0:T(8,128)(2,1)}, u32[]{:S(2)}) copy-start(bf16[1,176,2048]{2,1,0:T(8,128)(2,1)} %refs_0_.3) | copy-start | bytes 2162692
  2.6 16.9 %copy-start.1 = (bf16[1,176,2048]{2,1,0:T(8,128)(2,1)S(1)}, bf16[1,176,2048]{2,1,0:T(8,128)(2,1)}, u32[]{:S(2)}) copy-start(bf16[1,176,2048]{2,1,0:T(8,128)(2,1)} %refs_1_.3) | copy-start | bytes 2162692
  2.6 72.6 %all-to-all-start = ((bf16[32,8,2048]{2,1,0:T(8,128)(2,1)}), bf16[32,8,2048]{2,1,0:T(8,128)(2,1)S(1)}, u32[]{:S(2)}, u32[]{:S(2)}) async-start(bf16[32,8,2048]{2,1,0:T(8,128)(2,1)} %bitcast.15), calls=%async_computation | async-start | bytes 2097152 | tf_op jit(solution)/shard_map/all_to_all | solution.py:246
  21.9 30.8 %collective-permute-start.3 = (bf16[288,2048]{1,0:T(8,128)(2,1)}, bf16[288,2048]{1,0:T(8,128)(2,1)}, u32[]{:S(2)}, u32[]{:S(2)}) collective-permute-start(bf16[288,2048]{1,0:T(8,128)(2,1)} %get-tuple-element.17), channel_id=1, source_target_pairs={{0,1},{1,2},{2,3},{3,0},{4,5},{5,6},{6,7},{7,4},{8,9},{9,10},{10,1... | collective-permute-start | bytes 3538952 | tf_op jit(solution)/shard_map/ppermute | solution.py:217
  25.0 29.5 %collective-permute-start.6 = (bf16[240,2048]{1,0:T(8,128)(2,1)}, bf16[240,2048]{1,0:T(8,128)(2,1)}, u32[]{:S(2)}, u32[]{:S(2)}) collective-permute-start(bf16[240,2048]{1,0:T(8,128)(2,1)} %get-tuple-element.18), channel_id=1, source_target_pairs={{0,3},{1,0},{2,1},{3,2},{4,7},{5,4},{6,5},{7,6},{8,11},{9,8},{10,9... | collective-permute-start | bytes 2949128 | tf_op jit(solution)/shard_map/ppermute | solution.py:217
  28.4 54.8 %collective-permute-start.5 = (bf16[288,2048]{1,0:T(8,128)(2,1)}, bf16[288,2048]{1,0:T(8,128)(2,1)}, u32[]{:S(2)}, u32[]{:S(2)}) collective-permute-start(bf16[288,2048]{1,0:T(8,128)(2,1)} %get-tuple-element.17), channel_id=1, source_target_pairs={{0,3},{1,0},{2,1},{3,2},{4,7},{5,4},{6,5},{7,6},{8,11},{9,8},{10,9... | collective-permute-start | bytes 3538952 | tf_op jit(solution)/shard_map/ppermute | solution.py:217
  31.6 49.0 %collective-permute-start.4 = (bf16[240,2048]{1,0:T(8,128)(2,1)}, bf16[240,2048]{1,0:T(8,128)(2,1)}, u32[]{:S(2)}, u32[]{:S(2)}) collective-permute-start(bf16[240,2048]{1,0:T(8,128)(2,1)} %get-tuple-element.18), channel_id=1, source_target_pairs={{0,1},{1,2},{2,3},{3,0},{4,5},{5,6},{6,7},{7,4},{8,9},{9,10},{10,1... | collective-permute-start | bytes 2949128 | tf_op jit(solution)/shard_map/ppermute | solution.py:217
  52.6 46.3 %collective-permute-start.7 = (bf16[288,2048]{1,0:T(8,128)(2,1)}, bf16[288,2048]{1,0:T(8,128)(2,1)}, u32[]{:S(2)}, u32[]{:S(2)}) collective-permute-start(bf16[288,2048]{1,0:T(8,128)(2,1)} %collective-permute-done.3.refs_3_), channel_id=1, source_target_pairs={{0,1},{1,2},{2,3},{3,0},{4,5},{5,6},{6,7},{7,4},{8,9},{9,10},{10,1... | collective-permute-start | bytes 3538952 | tf_op jit(solution)/shard_map/ppermute | solution.py:217
  54.5 41.8 %collective-permute-start.8 = (bf16[240,2048]{1,0:T(8,128)(2,1)}, bf16[240,2048]{1,0:T(8,128)(2,1)}, u32[]{:S(2)}, u32[]{:S(2)}) collective-permute-start(bf16[240,2048]{1,0:T(8,128)(2,1)} %collective-permute-done.6.refs_6_), channel_id=1, source_target_pairs={{0,3},{1,0},{2,1},{3,2},{4,7},{5,4},{6,5},{7,6},{8,11},{9,8},{10,9... | collective-permute-start | bytes 2949128 | tf_op jit(solution)/shard_map/ppermute | solution.py:217
  75.7 23.3 %collective-permute-start = (bf16[128,2048]{1,0:T(8,128)(2,1)S(1)}, bf16[128,2048]{1,0:T(8,128)(2,1)S(1)}, u32[]{:S(2)}, u32[]{:S(2)}) collective-permute-start(bf16[128,2048]{1,0:T(8,128)(2,1)S(1)} %get-tuple-element.15), channel_id=1, source_target_pairs={{0,8},{1,9},{2,10},{3,11},{4,12},{5,13},{6,14},{7,15},{8,0},{9,1},... | collective-permute-start | bytes 1572872 | tf_op jit(solution)/shard_map/ppermute | solution.py:251
  80.5 23.6 %collective-permute-start.1 = (bf16[128,2048]{1,0:T(8,128)(2,1)S(1)}, bf16[128,2048]{1,0:T(8,128)(2,1)S(1)}, u32[]{:S(2)}, u32[]{:S(2)}) collective-permute-start(bf16[128,2048]{1,0:T(8,128)(2,1)S(1)} %get-tuple-element.15), channel_id=1, source_target_pairs={{0,12},{1,13},{2,14},{3,15},{4,8},{5,9},{6,10},{7,11},{8,4},{9,5},... | collective-permute-start | bytes 1572872 | tf_op jit(solution)/shard_map/ppermute | solution.py:251
  83.2 20.9 %collective-permute-start.2 = (bf16[128,2048]{1,0:T(8,128)(2,1)S(1)}, bf16[128,2048]{1,0:T(8,128)(2,1)S(1)}, u32[]{:S(2)}, u32[]{:S(2)}) collective-permute-start(bf16[128,2048]{1,0:T(8,128)(2,1)S(1)} %get-tuple-element.16.refs_3_), channel_id=1, source_target_pairs={{0,4},{1,5},{2,6},{3,7},{4,0},{5,1},{6,2},{7,3},{8,12},{9,13},{10,... | collective-permute-start | bytes 1572872 | tf_op jit(solution)/shard_map/ppermute | solution.py:251
  128.8 42.1 %copy-start.3 = (s32[16,4]{0,1:T(4,128)S(1)}, s32[16,4]{0,1:T(4,128)}, u32[]{:S(2)}) copy-start(s32[16,4]{0,1:T(4,128)} %param.10) | copy-start | bytes 772

commit v11 on v9

--- a/solution.py
+++ b/solution.py
@@ -112,23 +112,33 @@
         cp.wait()
 
 
+def tail_kernel(*refs):
+    rests, last, tails, sem = refs[:3], refs[3:5], refs[5:8], refs[8]
+    copies = []
+    for m in range(3):
+        at = rests[m].shape[0]
+        copies.append((rests[m], tails[m].at[pl.ds(0, at)]))
+        for piece in last:
+            size = piece.shape[0] // 3
+            copies.append((piece.at[pl.ds(m * size, size)], tails[m].at[pl.ds(at, size)]))
+            at += size
+    copies = [pltpu.make_async_copy(src, dst, sem.at[i]) for i, (src, dst) in enumerate(copies)]
+    for cp in copies:
+        cp.start()
+    for cp in copies:
+        cp.wait()
+
+
 def grad_kernel(*refs):
     n = 4
-    rows_in, mains, rests, last, out = refs[:n], refs[n : n + 3], refs[n + 3 : n + 6], refs[n + 6 : n + 8], refs[n + 8]
-    x, y, tails = refs[n + 9], refs[n + 10], refs[n + 11 :]
+    rows_in, mains, tails, out = refs[:n], refs[n : n + 3], refs[n + 3 : n + 6], refs[n + 6]
+    x, y = refs[n + 7 :]
     half = rows_in[0].shape[0] // 2
     me = lax.axis_index("hid") // n
     for i, d in enumerate((2, 3, 1, 0)):
         at = pl.ds(pl.multiple_of(jnp.bitwise_xor(me, d) * half, half), half)
         x[at, :] = rows_in[i][0:half, :]
         y[at, :] = rows_in[i][half : 2 * half, :]
-    for m in range(3):
-        at = rests[m].shape[0]
-        tails[m][0:at, :] = rests[m][...]
-        for piece in last:
-            size = piece.shape[0] // 3
-            tails[m][at : at + size, :] = piece[m * size : (m + 1) * size, :]
-            at += size
     dims = (((1,), (1,)), ((), ()))
     dot = lambda a, w: lax.dot_general(a[...], w[...], dims, preferred_element_type=F32)
     inner = []
@@ -252,6 +262,14 @@
         in_specs=[pl.BlockSpec(memory_space=pl.ANY)] * 7,
         scratch_shapes=[pltpu.SemaphoreType.DMA((18,))],
     )(w_gate, w_up, w_down, left_early, left_late, right_early, right_late)
+    tails = _call(
+        tail_kernel,
+        (_shape(rest + unit, width),) * 3,
+        "tail",
+        (0, 12 * (rest + unit) * width),
+        in_specs=[pl.BlockSpec(memory_space=pl.ANY)] * 5,
+        scratch_shapes=[pltpu.SemaphoreType.DMA((9,))],
+    )(*staged[3:], *last)
     rows = 8 * n_ex
     parts = _call(
         grad_kernel,
@@ -259,8 +277,8 @@
         "grad",
         (10 * rows * hid * width, 6 * hid * width),
         vmem=36,
-        scratch_shapes=[pltpu.VMEM((rows, width), BF)] * 2 + [pltpu.VMEM((rest + unit, width), BF)] * 3,
-    )(*rows_all, *staged, *last)
+        scratch_shapes=[pltpu.VMEM((rows, width), BF)] * 2,
+    )(*rows_all, *staged[:3], *tails)
     merged = _call(merge_kernel, _shape(8 * n_ex, width // 2), "merge", small)(over_y(parts))
     landed = lax.all_to_all(merged, "ex", split_axis=0, concat_axis=0, tiled=True)
     return _call(final_kernel, _shape(tok, width), "final", small)(landed, routes.T)

time: 172 us -> 172 us (level)
  transfers between devices with their start and end apart: 10 -> 10, of which waited for: 5 -> 5; matrix products, arithmetic and copies ran while one was open for 0% -> 0% of each run, Pallas kernels for 3% -> 4%
where the time goes in v11:
time: 172 us
  blocking collectives  61.5 us (36%)
  waiting for transfers between devices  49.6 us (29%)
  starting transfers between devices  44.6 us (26%)
  Pallas kernels  15.7 us (9%)
    all_to_all x1, blocking collectives, per_device(): lax.all_to_all(merged, 'ex', split_axis=0, concat_axis=0, tiled=True)  43.5 us
    ppermute x6, waiting for transfers between devices, shift(): lax.ppermute(v, 'hid', [(y * side + x, y * side + (x + d) % side) for y i...  30 us
    ppermute x6, starting transfers between devices, shift(): lax.ppermute(v, 'hid', [(y * side + x, y * side + (x + d) % side) for y i...  18.3 us
    all_to_all x1, blocking collectives, over_y(): lax.all_to_all(v, 'hid', split_axis=0, concat_axis=0, tiled=True, axis_in...  18.1 us
    all_to_all x1, starting transfers between devices, per_device(): lax.all_to_all(packed, 'ex', split_axis=0, concat_axis=0, tiled=True)  16.9 us
    all_to_all x1, waiting for transfers between devices, per_device(): lax.all_to_all(packed, 'ex', split_axis=0, concat_axis=0, tiled=True)  16.1 us
    ppermute x3, starting transfers between devices, per_device(): lax.ppermute(v, 'hid', [(y * side + x, (y ^ d) * side + x) for y in range...  9.43 us
    pallas_call x1, Pallas kernels, per_device(): _call(grad_kernel, _shape(rows, width), 'grad', (10 * rows * hid * width,...  4.43 us
  transfers between devices with their start and end apart: 10, of which 5 were waited for; matrix products, arithmetic and copies ran while one was open for 0% of the time, Pallas kernels for 4%

profile of v11, /device:TPU:1, one launch (start us, length us, event | category | flops | bytes accessed | tf_op | source)
XLA Modules:
  0.0 171.7 jit_solution(15488674407578407889)
XLA Ops:
  0.0 2.6 %pack.1 = bf16[256,2048]{1,0:T(8,128)(2,1)} custom-call(bf16[16,2048]{1,0:T(8,128)(2,1)} %tok_in.1, bf16[16,2048]{1,0:T(8,128)(2,1)} %cot_in.1, f32[4,16]{1,0:T(4,128)} %bitcast.16, s32[4,16]{1,0:T(4,128)} %bitcast.13), custom_call_target="tpu_custom_call" | custom-call | flops 67108864 | bytes 2097152 | tf_op jit(solution)/shard_map/pack/pallas_call | solution.py:235
  2.6 16.9 %all-to-all-start = ((bf16[32,8,2048]{2,1,0:T(8,128)(2,1)}), bf16[32,8,2048]{2,1,0:T(8,128)(2,1)S(1)}, u32[]{:S(2)}, u32[]{:S(2)}) async-start(bf16[32,8,2048]{2,1,0:T(8,128)(2,1)} %bitcast.15), calls=%async_computation | async-start | bytes 2097152 | tf_op jit(solution)/shard_map/all_to_all | solution.py:245
  19.5 2.3 %split.1 = (bf16[288,2048]{1,0:T(8,128)(2,1)}, bf16[240,2048]{1,0:T(8,128)(2,1)}) custom-call(bf16[1,176,2048]{2,1,0:T(8,128)(2,1)S(1)} %copy-done, bf16[1,176,2048]{2,1,0:T(8,128)(2,1)S(1)} %copy-done.1, bf16[1,176,2048]{2,1,0:T(8,128)(2,1)S(1)} %copy-done.2), custom_call_target="tpu_custom_call" | custom-call | bytes 4325376 | tf_op jit(solution)/shard_map/split/pallas_call | solution.py:221
  21.9 3.1 %collective-permute-start.3 = (bf16[288,2048]{1,0:T(8,128)(2,1)}, bf16[288,2048]{1,0:T(8,128)(2,1)}, u32[]{:S(2)}, u32[]{:S(2)}) collective-permute-start(bf16[288,2048]{1,0:T(8,128)(2,1)} %get-tuple-element.20), channel_id=1, source_target_pairs={{0,1},{1,2},{2,3},{3,0},{4,5},{5,6},{6,7},{7,4},{8,9},{9,10},{10,1... | collective-permute-start | bytes 3538952 | tf_op jit(solution)/shard_map/ppermute | solution.py:216
  25.0 3.4 %collective-permute-start.6 = (bf16[240,2048]{1,0:T(8,128)(2,1)}, bf16[240,2048]{1,0:T(8,128)(2,1)}, u32[]{:S(2)}, u32[]{:S(2)}) collective-permute-start(bf16[240,2048]{1,0:T(8,128)(2,1)} %get-tuple-element.21), channel_id=1, source_target_pairs={{0,3},{1,0},{2,1},{3,2},{4,7},{5,4},{6,5},{7,6},{8,11},{9,8},{10,9... | collective-permute-start | bytes 2949128 | tf_op jit(solution)/shard_map/ppermute | solution.py:216
  28.4 3.2 %collective-permute-start.5 = (bf16[288,2048]{1,0:T(8,128)(2,1)}, bf16[288,2048]{1,0:T(8,128)(2,1)}, u32[]{:S(2)}, u32[]{:S(2)}) collective-permute-start(bf16[288,2048]{1,0:T(8,128)(2,1)} %get-tuple-element.20), channel_id=1, source_target_pairs={{0,3},{1,0},{2,1},{3,2},{4,7},{5,4},{6,5},{7,6},{8,11},{9,8},{10,9... | collective-permute-start | bytes 3538952 | tf_op jit(solution)/shard_map/ppermute | solution.py:216
  31.5 2.1 %collective-permute-start.4 = (bf16[240,2048]{1,0:T(8,128)(2,1)}, bf16[240,2048]{1,0:T(8,128)(2,1)}, u32[]{:S(2)}, u32[]{:S(2)}) collective-permute-start(bf16[240,2048]{1,0:T(8,128)(2,1)} %get-tuple-element.21), channel_id=1, source_target_pairs={{0,1},{1,2},{2,3},{3,0},{4,5},{5,6},{6,7},{7,4},{8,9},{9,10},{10,1... | collective-permute-start | bytes 2949128 | tf_op jit(solution)/shard_map/ppermute | solution.py:216
  33.7 18.9 %collective-permute-done.3.refs_3_ = bf16[288,2048]{1,0:T(8,128)(2,1)} collective-permute-done((bf16[288,2048]{1,0:T(8,128)(2,1)}, bf16[288,2048]{1,0:T(8,128)(2,1)}, u32[]{:S(2)}, u32[]{:S(2)}) %collective-permute-start.3) | collective-permute-done | bytes 1179680 | tf_op jit(solution)/shard_map/ppermute | solution.py:216
  52.6 1.9 %collective-permute-start.7 = (bf16[288,2048]{1,0:T(8,128)(2,1)}, bf16[288,2048]{1,0:T(8,128)(2,1)}, u32[]{:S(2)}, u32[]{:S(2)}) collective-permute-start(bf16[288,2048]{1,0:T(8,128)(2,1)} %collective-permute-done.3.refs_3_), channel_id=1, source_target_pairs={{0,1},{1,2},{2,3},{3,0},{4,5},{5,6},{6,7},{7,4},{8,9},{9,10},{10,1... | collective-permute-start | bytes 3538952 | tf_op jit(solution)/shard_map/ppermute | solution.py:216
  54.5 4.6 %collective-permute-start.8 = (bf16[240,2048]{1,0:T(8,128)(2,1)}, bf16[240,2048]{1,0:T(8,128)(2,1)}, u32[]{:S(2)}, u32[]{:S(2)}) collective-permute-start(bf16[240,2048]{1,0:T(8,128)(2,1)} %collective-permute-done.6.refs_6_), channel_id=1, source_target_pairs={{0,3},{1,0},{2,1},{3,2},{4,7},{5,4},{6,5},{7,6},{8,11},{9,8},{10,9... | collective-permute-start | bytes 2949128 | tf_op jit(solution)/shard_map/ppermute | solution.py:216
  59.1 16.1 %all-to-all-done = bf16[32,8,2048]{2,1,0:T(8,128)(2,1)S(1)} async-done(((bf16[32,8,2048]{2,1,0:T(8,128)(2,1)}), bf16[32,8,2048]{2,1,0:T(8,128)(2,1)S(1)}, u32[]{:S(2)}, u32[]{:S(2)}) %all-to-all-start) | async-done | bytes 1048608 | tf_op jit(solution)/shard_map/all_to_all | solution.py:245
  75.2 0.4 unpack.1
  75.7 4.8 %collective-permute-start = (bf16[128,2048]{1,0:T(8,128)(2,1)S(1)}, bf16[128,2048]{1,0:T(8,128)(2,1)S(1)}, u32[]{:S(2)}, u32[]{:S(2)}) collective-permute-start(bf16[128,2048]{1,0:T(8,128)(2,1)S(1)} %get-tuple-element.18), channel_id=1, source_target_pairs={{0,8},{1,9},{2,10},{3,11},{4,12},{5,13},{6,14},{7,15},{8,0},{9,1},... | collective-permute-start | bytes 1572872 | tf_op jit(solution)/shard_map/ppermute | solution.py:250
  80.5 2.7 %collective-permute-start.1 = (bf16[128,2048]{1,0:T(8,128)(2,1)S(1)}, bf16[128,2048]{1,0:T(8,128)(2,1)S(1)}, u32[]{:S(2)}, u32[]{:S(2)}) collective-permute-start(bf16[128,2048]{1,0:T(8,128)(2,1)S(1)} %get-tuple-element.18), channel_id=1, source_target_pairs={{0,12},{1,13},{2,14},{3,15},{4,8},{5,9},{6,10},{7,11},{8,4},{9,5},... | collective-permute-start | bytes 1572872 | tf_op jit(solution)/shard_map/ppermute | solution.py:250
  83.2 1.9 %collective-permute-start.2 = (bf16[128,2048]{1,0:T(8,128)(2,1)S(1)}, bf16[128,2048]{1,0:T(8,128)(2,1)S(1)}, u32[]{:S(2)}, u32[]{:S(2)}) collective-permute-start(bf16[128,2048]{1,0:T(8,128)(2,1)S(1)} %get-tuple-element.19.refs_3_), channel_id=1, source_target_pairs={{0,4},{1,5},{2,6},{3,7},{4,0},{5,1},{6,2},{7,3},{8,12},{9,13},{10,... | collective-permute-start | bytes 1572872 | tf_op jit(solution)/shard_map/ppermute | solution.py:250
  85.2 2.7 %stage.1 = (bf16[512,2048]{1,0:T(8,128)(2,1)S(1)}, bf16[512,2048]{1,0:T(8,128)(2,1)S(1)}, bf16[512,2048]{1,0:T(8,128)(2,1)S(1)}, bf16[16,2048]{1,0:T(8,128)(2,1)...) custom-call(bf16[1,176,2048]{2,1,0:T(8,128)(2,1)S(1)} %copy-done, bf16[1,176,2048]{2,1,0:T(8,128)(2,1)S(1)} %copy-done.1, ...), custom_call_target="tpu_custom_call" | custom-call | bytes 25952256 | tf_op jit(solution)/shard_map/stage/pallas_call | solution.py:257
  87.9 8.5 %collective-permute-done.8.refs_4_ = bf16[240,2048]{1,0:T(8,128)(2,1)} collective-permute-done((bf16[240,2048]{1,0:T(8,128)(2,1)}, bf16[240,2048]{1,0:T(8,128)(2,1)}, u32[]{:S(2)}, u32[]{:S(2)}) %collective-permute-start.8) | collective-permute-done | bytes 983072 | tf_op jit(solution)/shard_map/ppermute | solution.py:216
  96.3 2.6 %collective-permute-done.7.refs_3_ = bf16[288,2048]{1,0:T(8,128)(2,1)} collective-permute-done((bf16[288,2048]{1,0:T(8,128)(2,1)}, bf16[288,2048]{1,0:T(8,128)(2,1)}, u32[]{:S(2)}, u32[]{:S(2)}) %collective-permute-start.7) | collective-permute-done | bytes 1179680 | tf_op jit(solution)/shard_map/ppermute | solution.py:216
  99.0 1.7 tail.1
  100.7 3.5 %collective-permute-done.1.refs_1_ = bf16[128,2048]{1,0:T(8,128)(2,1)S(1)} collective-permute-done((bf16[128,2048]{1,0:T(8,128)(2,1)S(1)}, bf16[128,2048]{1,0:T(8,128)(2,1)S(1)}, u32[]{:S(2)}, u32[]{:S(2)}) %collective-permute-start.1) | collective-permute-done | bytes 524320 | tf_op jit(solution)/shard_map/ppermute | solution.py:250
  104.2 4.4 %grad.1 = bf16[256,2048]{1,0:T(8,128)(2,1)S(1)} custom-call(bf16[128,2048]{1,0:T(8,128)(2,1)S(1)} %collective-permute-done.refs_0_, bf16[128,2048]{1,0:T(8,128)(2,1)S(1)} %collective-permute-done.1.refs_1_, bf16[128,2048]{1,0:T(8,128)(2,1)S(1)} %collective-permute-done.2.refs_2_, bf16[128,2048]{1,0:T(8,128)(2,1)S(1)} %get-tuple-element.19.refs_3_, ...), custom_call_target="tpu_custom_call" | custom-call | flops 3690987520 | bytes 8650752 | tf_op jit(solution)/shard_map/grad/pallas_call | solution.py:274
  108.6 18.1 %all_to_all.33 = bf16[4,64,2048]{2,1,0:T(8,128)(2,1)S(1)} all-to-all(bf16[4,64,2048]{2,1,0:T(8,128)(2,1)S(1)} %bitcast.12), channel_id=1, replica_groups={{0,4,8,12},{1,5,9,13},{2,6,10,14},{3,7,11,15},{16,20,24,28},{17,21,25,2..., dimensions={0} | all-to-all | bytes 2097152 | tf_op jit(solution)/shard_map/all_to_all | solution.py:230
  127.1 43.5 %all_to_all.34 = bf16[32,8,1024]{2,1,0:T(8,128)(2,1)S(1)} all-to-all(bf16[32,8,1024]{2,1,0:T(8,128)(2,1)S(1)} %bitcast.10), channel_id=1, replica_groups=mesh['ex'=32,'hid'=16] {'ex'}, dimensions={0} | all-to-all | bytes 1048576 | tf_op jit(solution)/shard_map/all_to_all | solution.py:283
  170.6 1.1 final.1
  (14 shorter events, 0.4 us)
Async XLA Ops:
  0.0 19.5 %copy-start.2 = (bf16[1,176,2048]{2,1,0:T(8,128)(2,1)S(1)}, bf16[1,176,2048]{2,1,0:T(8,128)(2,1)}, u32[]{:S(2)}) copy-start(bf16[1,176,2048]{2,1,0:T(8,128)(2,1)} %refs_2_.3) | copy-start | bytes 2162692
  2.6 16.9 %copy-start = (bf16[1,176,2048]{2,1,0:T(8,128)(2,1)S(1)}, bf16[1,176,2048]{2,1,0:T(8,128)(2,1)}, u32[]{:S(2)}) copy-start(bf16[1,176,2048]{2,1,0:T(8,128)(2,1)} %refs_0_.3) | copy-start | bytes 2162692
  2.6 16.9 %copy-start.1 = (bf16[1,176,2048]{2,1,0:T(8,128)(2,1)S(1)}, bf16[1,176,2048]{2,1,0:T(8,128)(2,1)}, u32[]{:S(2)}) copy-start(bf16[1,176,2048]{2,1,0:T(8,128)(2,1)} %refs_1_.3) | copy-start | bytes 2162692
  2.6 72.6 %all-to-all-start = ((bf16[32,8,2048]{2,1,0:T(8,128)(2,1)}), bf16[32,8,2048]{2,1,0:T(8,128)(2,1)S(1)}, u32[]{:S(2)}, u32[]{:S(2)}) async-start(bf16[32,8,2048]{2,1,0:T(8,128)(2,1)} %bitcast.15), calls=%async_computation | async-start | bytes 2097152 | tf_op jit(solution)/shard_map/all_to_all | solution.py:245
  21.9 30.8 %collective-permute-start.3 = (bf16[288,2048]{1,0:T(8,128)(2,1)}, bf16[288,2048]{1,0:T(8,128)(2,1)}, u32[]{:S(2)}, u32[]{:S(2)}) collective-permute-start(bf16[288,2048]{1,0:T(8,128)(2,1)} %get-tuple-element.20), channel_id=1, source_target_pairs={{0,1},{1,2},{2,3},{3,0},{4,5},{5,6},{6,7},{7,4},{8,9},{9,10},{10,1... | collective-permute-start | bytes 3538952 | tf_op jit(solution)/shard_map/ppermute | solution.py:216
  25.0 29.5 %collective-permute-start.6 = (bf16[240,2048]{1,0:T(8,128)(2,1)}, bf16[240,2048]{1,0:T(8,128)(2,1)}, u32[]{:S(2)}, u32[]{:S(2)}) collective-permute-start(bf16[240,2048]{1,0:T(8,128)(2,1)} %get-tuple-element.21), channel_id=1, source_target_pairs={{0,3},{1,0},{2,1},{3,2},{4,7},{5,4},{6,5},{7,6},{8,11},{9,8},{10,9... | collective-permute-start | bytes 2949128 | tf_op jit(solution)/shard_map/ppermute | solution.py:216
  28.4 54.9 %collective-permute-start.5 = (bf16[288,2048]{1,0:T(8,128)(2,1)}, bf16[288,2048]{1,0:T(8,128)(2,1)}, u32[]{:S(2)}, u32[]{:S(2)}) collective-permute-start(bf16[288,2048]{1,0:T(8,128)(2,1)} %get-tuple-element.20), channel_id=1, source_target_pairs={{0,3},{1,0},{2,1},{3,2},{4,7},{5,4},{6,5},{7,6},{8,11},{9,8},{10,9... | collective-permute-start | bytes 3538952 | tf_op jit(solution)/shard_map/ppermute | solution.py:216
  31.5 49.0 %collective-permute-start.4 = (bf16[240,2048]{1,0:T(8,128)(2,1)}, bf16[240,2048]{1,0:T(8,128)(2,1)}, u32[]{:S(2)}, u32[]{:S(2)}) collective-permute-start(bf16[240,2048]{1,0:T(8,128)(2,1)} %get-tuple-element.21), channel_id=1, source_target_pairs={{0,1},{1,2},{2,3},{3,0},{4,5},{5,6},{6,7},{7,4},{8,9},{9,10},{10,1... | collective-permute-start | bytes 2949128 | tf_op jit(solution)/shard_map/ppermute | solution.py:216
  52.6 46.3 %collective-permute-start.7 = (bf16[288,2048]{1,0:T(8,128)(2,1)}, bf16[288,2048]{1,0:T(8,128)(2,1)}, u32[]{:S(2)}, u32[]{:S(2)}) collective-permute-start(bf16[288,2048]{1,0:T(8,128)(2,1)} %collective-permute-done.3.refs_3_), channel_id=1, source_target_pairs={{0,1},{1,2},{2,3},{3,0},{4,5},{5,6},{6,7},{7,4},{8,9},{9,10},{10,1... | collective-permute-start | bytes 3538952 | tf_op jit(solution)/shard_map/ppermute | solution.py:216
  54.5 41.8 %collective-permute-start.8 = (bf16[240,2048]{1,0:T(8,128)(2,1)}, bf16[240,2048]{1,0:T(8,128)(2,1)}, u32[]{:S(2)}, u32[]{:S(2)}) collective-permute-start(bf16[240,2048]{1,0:T(8,128)(2,1)} %collective-permute-done.6.refs_6_), channel_id=1, source_target_pairs={{0,3},{1,0},{2,1},{3,2},{4,7},{5,4},{6,5},{7,6},{8,11},{9,8},{10,9... | collective-permute-start | bytes 2949128 | tf_op jit(solution)/shard_map/ppermute | solution.py:216
  75.7 25.0 %collective-permute-start = (bf16[128,2048]{1,0:T(8,128)(2,1)S(1)}, bf16[128,2048]{1,0:T(8,128)(2,1)S(1)}, u32[]{:S(2)}, u32[]{:S(2)}) collective-permute-start(bf16[128,2048]{1,0:T(8,128)(2,1)S(1)} %get-tuple-element.18), channel_id=1, source_target_pairs={{0,8},{1,9},{2,10},{3,11},{4,12},{5,13},{6,14},{7,15},{8,0},{9,1},... | collective-permute-start | bytes 1572872 | tf_op jit(solution)/shard_map/ppermute | solution.py:250
  80.5 23.6 %collective-permute-start.1 = (bf16[128,2048]{1,0:T(8,128)(2,1)S(1)}, bf16[128,2048]{1,0:T(8,128)(2,1)S(1)}, u32[]{:S(2)}, u32[]{:S(2)}) collective-permute-start(bf16[128,2048]{1,0:T(8,128)(2,1)S(1)} %get-tuple-element.18), channel_id=1, source_target_pairs={{0,12},{1,13},{2,14},{3,15},{4,8},{5,9},{6,10},{7,11},{8,4},{9,5},... | collective-permute-start | bytes 1572872 | tf_op jit(solution)/shard_map/ppermute | solution.py:250
  83.2 20.9 %collective-permute-start.2 = (bf16[128,2048]{1,0:T(8,128)(2,1)S(1)}, bf16[128,2048]{1,0:T(8,128)(2,1)S(1)}, u32[]{:S(2)}, u32[]{:S(2)}) collective-permute-start(bf16[128,2048]{1,0:T(8,128)(2,1)S(1)} %get-tuple-element.19.refs_3_), channel_id=1, source_target_pairs={{0,4},{1,5},{2,6},{3,7},{4,0},{5,1},{6,2},{7,3},{8,12},{9,13},{10,... | collective-permute-start | bytes 1572872 | tf_op jit(solution)/shard_map/ppermute | solution.py:250
  126.7 43.9 %copy-start.3 = (s32[16,4]{0,1:T(4,128)S(1)}, s32[16,4]{0,1:T(4,128)}, u32[]{:S(2)}) copy-start(s32[16,4]{0,1:T(4,128)} %param.10) | copy-start | bytes 772

commit v12 on v11

--- a/solution.py
+++ b/solution.py
@@ -57,17 +57,12 @@
     out_ref[...] = (weight * jnp.dot(pick, data, preferred_element_type=F32)).astype(BF)
 
 
-def split_kernel(*refs):
-    w_in, outs, sem = refs[:3], refs[3:5], refs[5]
-    cut = outs[0].shape[0] // 3
-    copies = []
-    for m, w in enumerate(w_in):
-        for i, (at, size) in enumerate(((0, cut), (cut, w.shape[1] - cut))):
-            copies.append(
-                pltpu.make_async_copy(
-                    w.at[0, pl.ds(at, size)], outs[i].at[pl.ds(m * size, size)], sem.at[2 * m + i]
-                )
-            )
+def split_kernel(at, g_in, u_in, d_in, out, sem):
+    size = out.shape[0] // 3
+    copies = [
+        pltpu.make_async_copy(w.at[0, pl.ds(at, size)], out.at[pl.ds(m * size, size)], sem.at[m])
+        for m, w in enumerate((g_in, u_in, d_in))
+    ]
     for cp in copies:
         cp.start()
     for cp in copies:
@@ -218,14 +213,19 @@
         )
 
     cut = (unit // 2 + 15) // 16 * 16
-    early, late = _call(
-        split_kernel,
-        (_shape(3 * cut, width), _shape(3 * (unit - cut), width)),
-        "split",
-        (0, 12 * unit * width),
-        in_specs=[pl.BlockSpec(memory_space=pltpu.HBM)] * 3,
-        scratch_shapes=[pltpu.SemaphoreType.DMA((6,))],
-    )(w_gate, w_up, w_down)
+    early, late = [
+        _call(
+            functools.partial(split_kernel, at),
+            _shape(3 * size, width),
+            name,
+            (0, 12 * size * width),
+            in_specs=[pl.BlockSpec(memory_space=pltpu.HBM)] * 3,
+            out_specs=pl.BlockSpec(memory_space=pl.ANY),
+            scratch_shapes=[pltpu.SemaphoreType.DMA((3,))],
+        )(w_gate, w_up, w_down)
+        for name, at, size in (("early", 0, cut), ("late", cut, unit - cut))
+    ]
+
     def over_y(v):
         return lax.all_to_all(
             v, "hid", split_axis=0, concat_axis=0, tiled=True, axis_index_groups=along_y

time: 172 us -> 171 us (level)
    ppermute x6, waiting for transfers between devices: 30 us -> 27.7 us  [shift(): lax.ppermute(v, 'hid', [(y * side + x, y * side + (x + d) % side) for y i...]
where the time goes in v12:
time: 171 us; the launch traced here: 170 us
  blocking collectives  60.3 us (35%)
  waiting for transfers between devices  49.8 us (29%)
  starting transfers between devices  44.6 us (26%)
  Pallas kernels  15.5 us (9%)
    all_to_all x1, blocking collectives, per_device(): lax.all_to_all(merged, 'ex', split_axis=0, concat_axis=0, tiled=True)  42.2 us
    ppermute x6, waiting for transfers between devices, shift(): lax.ppermute(v, 'hid', [(y * side + x, y * side + (x + d) % side) for y i...  27.7 us
    ppermute x6, starting transfers between devices, shift(): lax.ppermute(v, 'hid', [(y * side + x, y * side + (x + d) % side) for y i...  18.3 us
    all_to_all x1, blocking collectives, over_y(): lax.all_to_all(v, 'hid', split_axis=0, concat_axis=0, tiled=True, axis_in...  18.1 us
    all_to_all x1, waiting for transfers between devices, per_device(): lax.all_to_all(packed, 'ex', split_axis=0, concat_axis=0, tiled=True)  17.4 us
    all_to_all x1, starting transfers between devices, per_device(): lax.all_to_all(packed, 'ex', split_axis=0, concat_axis=0, tiled=True)  16.9 us
    ppermute x3, starting transfers between devices, per_device(): lax.ppermute(v, 'hid', [(y * side + x, (y ^ d) * side + x) for y in range...  9.42 us
    ppermute x3, waiting for transfers between devices, per_device(): lax.ppermute(v, 'hid', [(y * side + x, (y ^ d) * side + x) for y in range...  4.76 us
  transfers between devices with their start and end apart: 10, of which 5 were waited for; matrix products, arithmetic and copies ran while one was open for 0% of the time, Pallas kernels for 4%

profile of v12, /device:TPU:1, one launch (start us, length us, event | category | flops | bytes accessed | tf_op | source)
XLA Modules:
  0.0 170.4 jit_solution(16171425709709968899)
XLA Ops:
  0.0 2.6 %pack.1 = bf16[256,2048]{1,0:T(8,128)(2,1)} custom-call(bf16[16,2048]{1,0:T(8,128)(2,1)} %tok_in.1, bf16[16,2048]{1,0:T(8,128)(2,1)} %cot_in.1, f32[4,16]{1,0:T(4,128)} %bitcast.16, s32[4,16]{1,0:T(4,128)} %bitcast.13), custom_call_target="tpu_custom_call" | custom-call | flops 67108864 | bytes 2097152 | tf_op jit(solution)/shard_map/pack/pallas_call | solution.py:235
  2.6 16.9 %all-to-all-start = ((bf16[32,8,2048]{2,1,0:T(8,128)(2,1)}), bf16[32,8,2048]{2,1,0:T(8,128)(2,1)S(1)}, u32[]{:S(2)}, u32[]{:S(2)}) async-start(bf16[32,8,2048]{2,1,0:T(8,128)(2,1)} %bitcast.15), calls=%async_computation | async-start | bytes 2097152 | tf_op jit(solution)/shard_map/all_to_all | solution.py:245
  19.5 1.0 early.1
  20.6 3.1 %collective-permute-start.3 = (bf16[288,2048]{1,0:T(8,128)(2,1)}, bf16[288,2048]{1,0:T(8,128)(2,1)}, u32[]{:S(2)}, u32[]{:S(2)}) collective-permute-start(bf16[288,2048]{1,0:T(8,128)(2,1)} %early.1), channel_id=1, source_target_pairs={{0,1},{1,2},{2,3},{3,0},{4,5},{5,6},{6,7},{7,4},{8,9},{9,10},{10,1... | collective-permute-start | bytes 3538952 | tf_op jit(solution)/shard_map/ppermute | solution.py:211
  23.7 1.1 late.1
  24.8 3.4 %collective-permute-start.6 = (bf16[240,2048]{1,0:T(8,128)(2,1)}, bf16[240,2048]{1,0:T(8,128)(2,1)}, u32[]{:S(2)}, u32[]{:S(2)}) collective-permute-start(bf16[240,2048]{1,0:T(8,128)(2,1)} %late.1), channel_id=1, source_target_pairs={{0,3},{1,0},{2,1},{3,2},{4,7},{5,4},{6,5},{7,6},{8,11},{9,8},{10,9... | collective-permute-start | bytes 2949128 | tf_op jit(solution)/shard_map/ppermute | solution.py:211
  28.2 3.2 %collective-permute-start.5 = (bf16[288,2048]{1,0:T(8,128)(2,1)}, bf16[288,2048]{1,0:T(8,128)(2,1)}, u32[]{:S(2)}, u32[]{:S(2)}) collective-permute-start(bf16[288,2048]{1,0:T(8,128)(2,1)} %early.1), channel_id=1, source_target_pairs={{0,3},{1,0},{2,1},{3,2},{4,7},{5,4},{6,5},{7,6},{8,11},{9,8},{10,9... | collective-permute-start | bytes 3538952 | tf_op jit(solution)/shard_map/ppermute | solution.py:211
  31.4 2.1 %collective-permute-start.4 = (bf16[240,2048]{1,0:T(8,128)(2,1)}, bf16[240,2048]{1,0:T(8,128)(2,1)}, u32[]{:S(2)}, u32[]{:S(2)}) collective-permute-start(bf16[240,2048]{1,0:T(8,128)(2,1)} %late.1), channel_id=1, source_target_pairs={{0,1},{1,2},{2,3},{3,0},{4,5},{5,6},{6,7},{7,4},{8,9},{9,10},{10,1... | collective-permute-start | bytes 2949128 | tf_op jit(solution)/shard_map/ppermute | solution.py:211
  33.5 17.9 %collective-permute-done.3.refs_3_ = bf16[288,2048]{1,0:T(8,128)(2,1)} collective-permute-done((bf16[288,2048]{1,0:T(8,128)(2,1)}, bf16[288,2048]{1,0:T(8,128)(2,1)}, u32[]{:S(2)}, u32[]{:S(2)}) %collective-permute-start.3) | collective-permute-done | bytes 1179680 | tf_op jit(solution)/shard_map/ppermute | solution.py:211
  51.3 1.9 %collective-permute-start.7 = (bf16[288,2048]{1,0:T(8,128)(2,1)}, bf16[288,2048]{1,0:T(8,128)(2,1)}, u32[]{:S(2)}, u32[]{:S(2)}) collective-permute-start(bf16[288,2048]{1,0:T(8,128)(2,1)} %collective-permute-done.3.refs_3_), channel_id=1, source_target_pairs={{0,1},{1,2},{2,3},{3,0},{4,5},{5,6},{6,7},{7,4},{8,9},{9,10},{10,1... | collective-permute-start | bytes 3538952 | tf_op jit(solution)/shard_map/ppermute | solution.py:211
  53.3 4.6 %collective-permute-start.8 = (bf16[240,2048]{1,0:T(8,128)(2,1)}, bf16[240,2048]{1,0:T(8,128)(2,1)}, u32[]{:S(2)}, u32[]{:S(2)}) collective-permute-start(bf16[240,2048]{1,0:T(8,128)(2,1)} %collective-permute-done.6.refs_6_), channel_id=1, source_target_pairs={{0,3},{1,0},{2,1},{3,2},{4,7},{5,4},{6,5},{7,6},{8,11},{9,8},{10,9... | collective-permute-start | bytes 2949128 | tf_op jit(solution)/shard_map/ppermute | solution.py:211
  57.9 17.4 %all-to-all-done = bf16[32,8,2048]{2,1,0:T(8,128)(2,1)S(1)} async-done(((bf16[32,8,2048]{2,1,0:T(8,128)(2,1)}), bf16[32,8,2048]{2,1,0:T(8,128)(2,1)S(1)}, u32[]{:S(2)}, u32[]{:S(2)}) %all-to-all-start) | async-done | bytes 1048608 | tf_op jit(solution)/shard_map/all_to_all | solution.py:245
  75.7 4.8 %collective-permute-start = (bf16[128,2048]{1,0:T(8,128)(2,1)S(1)}, bf16[128,2048]{1,0:T(8,128)(2,1)S(1)}, u32[]{:S(2)}, u32[]{:S(2)}) collective-permute-start(bf16[128,2048]{1,0:T(8,128)(2,1)S(1)} %get-tuple-element.16), channel_id=1, source_target_pairs={{0,8},{1,9},{2,10},{3,11},{4,12},{5,13},{6,14},{7,15},{8,0},{9,1},... | collective-permute-start | bytes 1572872 | tf_op jit(solution)/shard_map/ppermute | solution.py:250
  80.5 2.7 %collective-permute-start.1 = (bf16[128,2048]{1,0:T(8,128)(2,1)S(1)}, bf16[128,2048]{1,0:T(8,128)(2,1)S(1)}, u32[]{:S(2)}, u32[]{:S(2)}) collective-permute-start(bf16[128,2048]{1,0:T(8,128)(2,1)S(1)} %get-tuple-element.16), channel_id=1, source_target_pairs={{0,12},{1,13},{2,14},{3,15},{4,8},{5,9},{6,10},{7,11},{8,4},{9,5},... | collective-permute-start | bytes 1572872 | tf_op jit(solution)/shard_map/ppermute | solution.py:250
  83.2 1.9 %collective-permute-start.2 = (bf16[128,2048]{1,0:T(8,128)(2,1)S(1)}, bf16[128,2048]{1,0:T(8,128)(2,1)S(1)}, u32[]{:S(2)}, u32[]{:S(2)}) collective-permute-start(bf16[128,2048]{1,0:T(8,128)(2,1)S(1)} %get-tuple-element.17.refs_3_), channel_id=1, source_target_pairs={{0,4},{1,5},{2,6},{3,7},{4,0},{5,1},{6,2},{7,3},{8,12},{9,13},{10,... | collective-permute-start | bytes 1572872 | tf_op jit(solution)/shard_map/ppermute | solution.py:250
  85.2 2.7 %stage.1 = (bf16[512,2048]{1,0:T(8,128)(2,1)S(1)}, bf16[512,2048]{1,0:T(8,128)(2,1)S(1)}, bf16[512,2048]{1,0:T(8,128)(2,1)S(1)}, bf16[16,2048]{1,0:T(8,128)(2,1)...) custom-call(bf16[1,176,2048]{2,1,0:T(8,128)(2,1)S(1)} %copy-done, bf16[1,176,2048]{2,1,0:T(8,128)(2,1)S(1)} %copy-done.1, ...), custom_call_target="tpu_custom_call" | custom-call | bytes 25952256 | tf_op jit(solution)/shard_map/stage/pallas_call | solution.py:257
  87.9 8.3 %collective-permute-done.8.refs_4_ = bf16[240,2048]{1,0:T(8,128)(2,1)} collective-permute-done((bf16[240,2048]{1,0:T(8,128)(2,1)}, bf16[240,2048]{1,0:T(8,128)(2,1)}, u32[]{:S(2)}, u32[]{:S(2)}) %collective-permute-start.8) | collective-permute-done | bytes 983072 | tf_op jit(solution)/shard_map/ppermute | solution.py:211
  96.2 1.5 collective-permute-done.7.refs_3_
  97.7 1.7 tail.1
  99.4 4.8 %collective-permute-done.1.refs_1_ = bf16[128,2048]{1,0:T(8,128)(2,1)S(1)} collective-permute-done((bf16[128,2048]{1,0:T(8,128)(2,1)S(1)}, bf16[128,2048]{1,0:T(8,128)(2,1)S(1)}, u32[]{:S(2)}, u32[]{:S(2)}) %collective-permute-start.1) | collective-permute-done | bytes 524320 | tf_op jit(solution)/shard_map/ppermute | solution.py:250
  104.2 4.4 %grad.1 = bf16[256,2048]{1,0:T(8,128)(2,1)S(1)} custom-call(bf16[128,2048]{1,0:T(8,128)(2,1)S(1)} %collective-permute-done.refs_0_, bf16[128,2048]{1,0:T(8,128)(2,1)S(1)} %collective-permute-done.1.refs_1_, bf16[128,2048]{1,0:T(8,128)(2,1)S(1)} %collective-permute-done.2.refs_2_, bf16[128,2048]{1,0:T(8,128)(2,1)S(1)} %get-tuple-element.17.refs_3_, ...), custom_call_target="tpu_custom_call" | custom-call | flops 3690987520 | bytes 8650752 | tf_op jit(solution)/shard_map/grad/pallas_call | solution.py:274
  108.6 18.1 %all_to_all.33 = bf16[4,64,2048]{2,1,0:T(8,128)(2,1)S(1)} all-to-all(bf16[4,64,2048]{2,1,0:T(8,128)(2,1)S(1)} %bitcast.12), channel_id=1, replica_groups={{0,4,8,12},{1,5,9,13},{2,6,10,14},{3,7,11,15},{16,20,24,28},{17,21,25,2..., dimensions={0} | all-to-all | bytes 2097152 | tf_op jit(solution)/shard_map/all_to_all | solution.py:230
  127.1 42.2 %all_to_all.34 = bf16[32,8,1024]{2,1,0:T(8,128)(2,1)S(1)} all-to-all(bf16[32,8,1024]{2,1,0:T(8,128)(2,1)S(1)} %bitcast.10), channel_id=1, replica_groups=mesh['ex'=32,'hid'=16] {'ex'}, dimensions={0} | all-to-all | bytes 1048576 | tf_op jit(solution)/shard_map/all_to_all | solution.py:283
  169.3 1.1 final.1
  (15 shorter events, 0.9 us)
Async XLA Ops:
  0.0 19.5 %copy-start.2 = (bf16[1,176,2048]{2,1,0:T(8,128)(2,1)S(1)}, bf16[1,176,2048]{2,1,0:T(8,128)(2,1)}, u32[]{:S(2)}) copy-start(bf16[1,176,2048]{2,1,0:T(8,128)(2,1)} %refs_2_.1) | copy-start | bytes 2162692
  2.6 16.9 %copy-start = (bf16[1,176,2048]{2,1,0:T(8,128)(2,1)S(1)}, bf16[1,176,2048]{2,1,0:T(8,128)(2,1)}, u32[]{:S(2)}) copy-start(bf16[1,176,2048]{2,1,0:T(8,128)(2,1)} %refs_0_.1) | copy-start | bytes 2162692
  2.6 16.9 %copy-start.1 = (bf16[1,176,2048]{2,1,0:T(8,128)(2,1)S(1)}, bf16[1,176,2048]{2,1,0:T(8,128)(2,1)}, u32[]{:S(2)}) copy-start(bf16[1,176,2048]{2,1,0:T(8,128)(2,1)} %refs_1_.1) | copy-start | bytes 2162692
  2.6 72.6 %all-to-all-start = ((bf16[32,8,2048]{2,1,0:T(8,128)(2,1)}), bf16[32,8,2048]{2,1,0:T(8,128)(2,1)S(1)}, u32[]{:S(2)}, u32[]{:S(2)}) async-start(bf16[32,8,2048]{2,1,0:T(8,128)(2,1)} %bitcast.15), calls=%async_computation | async-start | bytes 2097152 | tf_op jit(solution)/shard_map/all_to_all | solution.py:245
  20.6 30.8 %collective-permute-start.3 = (bf16[288,2048]{1,0:T(8,128)(2,1)}, bf16[288,2048]{1,0:T(8,128)(2,1)}, u32[]{:S(2)}, u32[]{:S(2)}) collective-permute-start(bf16[288,2048]{1,0:T(8,128)(2,1)} %early.1), channel_id=1, source_target_pairs={{0,1},{1,2},{2,3},{3,0},{4,5},{5,6},{6,7},{7,4},{8,9},{9,10},{10,1... | collective-permute-start | bytes 3538952 | tf_op jit(solution)/shard_map/ppermute | solution.py:211
  24.8 28.5 %collective-permute-start.6 = (bf16[240,2048]{1,0:T(8,128)(2,1)}, bf16[240,2048]{1,0:T(8,128)(2,1)}, u32[]{:S(2)}, u32[]{:S(2)}) collective-permute-start(bf16[240,2048]{1,0:T(8,128)(2,1)} %late.1), channel_id=1, source_target_pairs={{0,3},{1,0},{2,1},{3,2},{4,7},{5,4},{6,5},{7,6},{8,11},{9,8},{10,9... | collective-permute-start | bytes 2949128 | tf_op jit(solution)/shard_map/ppermute | solution.py:211
  28.2 55.0 %collective-permute-start.5 = (bf16[288,2048]{1,0:T(8,128)(2,1)}, bf16[288,2048]{1,0:T(8,128)(2,1)}, u32[]{:S(2)}, u32[]{:S(2)}) collective-permute-start(bf16[288,2048]{1,0:T(8,128)(2,1)} %early.1), channel_id=1, source_target_pairs={{0,3},{1,0},{2,1},{3,2},{4,7},{5,4},{6,5},{7,6},{8,11},{9,8},{10,9... | collective-permute-start | bytes 3538952 | tf_op jit(solution)/shard_map/ppermute | solution.py:211
  31.4 49.1 %collective-permute-start.4 = (bf16[240,2048]{1,0:T(8,128)(2,1)}, bf16[240,2048]{1,0:T(8,128)(2,1)}, u32[]{:S(2)}, u32[]{:S(2)}) collective-permute-start(bf16[240,2048]{1,0:T(8,128)(2,1)} %late.1), channel_id=1, source_target_pairs={{0,1},{1,2},{2,3},{3,0},{4,5},{5,6},{6,7},{7,4},{8,9},{9,10},{10,1... | collective-permute-start | bytes 2949128 | tf_op jit(solution)/shard_map/ppermute | solution.py:211
  51.3 46.3 %collective-permute-start.7 = (bf16[288,2048]{1,0:T(8,128)(2,1)}, bf16[288,2048]{1,0:T(8,128)(2,1)}, u32[]{:S(2)}, u32[]{:S(2)}) collective-permute-start(bf16[288,2048]{1,0:T(8,128)(2,1)} %collective-permute-done.3.refs_3_), channel_id=1, source_target_pairs={{0,1},{1,2},{2,3},{3,0},{4,5},{5,6},{6,7},{7,4},{8,9},{9,10},{10,1... | collective-permute-start | bytes 3538952 | tf_op jit(solution)/shard_map/ppermute | solution.py:211
  53.3 42.9 %collective-permute-start.8 = (bf16[240,2048]{1,0:T(8,128)(2,1)}, bf16[240,2048]{1,0:T(8,128)(2,1)}, u32[]{:S(2)}, u32[]{:S(2)}) collective-permute-start(bf16[240,2048]{1,0:T(8,128)(2,1)} %collective-permute-done.6.refs_6_), channel_id=1, source_target_pairs={{0,3},{1,0},{2,1},{3,2},{4,7},{5,4},{6,5},{7,6},{8,11},{9,8},{10,9... | collective-permute-start | bytes 2949128 | tf_op jit(solution)/shard_map/ppermute | solution.py:211
  75.7 23.7 %collective-permute-start = (bf16[128,2048]{1,0:T(8,128)(2,1)S(1)}, bf16[128,2048]{1,0:T(8,128)(2,1)S(1)}, u32[]{:S(2)}, u32[]{:S(2)}) collective-permute-start(bf16[128,2048]{1,0:T(8,128)(2,1)S(1)} %get-tuple-element.16), channel_id=1, source_target_pairs={{0,8},{1,9},{2,10},{3,11},{4,12},{5,13},{6,14},{7,15},{8,0},{9,1},... | collective-permute-start | bytes 1572872 | tf_op jit(solution)/shard_map/ppermute | solution.py:250
  80.5 23.6 %collective-permute-start.1 = (bf16[128,2048]{1,0:T(8,128)(2,1)S(1)}, bf16[128,2048]{1,0:T(8,128)(2,1)S(1)}, u32[]{:S(2)}, u32[]{:S(2)}) collective-permute-start(bf16[128,2048]{1,0:T(8,128)(2,1)S(1)} %get-tuple-element.16), channel_id=1, source_target_pairs={{0,12},{1,13},{2,14},{3,15},{4,8},{5,9},{6,10},{7,11},{8,4},{9,5},... | collective-permute-start | bytes 1572872 | tf_op jit(solution)/shard_map/ppermute | solution.py:250
  83.2 20.9 %collective-permute-start.2 = (bf16[128,2048]{1,0:T(8,128)(2,1)S(1)}, bf16[128,2048]{1,0:T(8,128)(2,1)S(1)}, u32[]{:S(2)}, u32[]{:S(2)}) collective-permute-start(bf16[128,2048]{1,0:T(8,128)(2,1)S(1)} %get-tuple-element.17.refs_3_), channel_id=1, source_target_pairs={{0,4},{1,5},{2,6},{3,7},{4,0},{5,1},{6,2},{7,3},{8,12},{9,13},{10,... | collective-permute-start | bytes 1572872 | tf_op jit(solution)/shard_map/ppermute | solution.py:250
  126.7 42.6 %copy-start.3 = (s32[16,4]{0,1:T(4,128)S(1)}, s32[16,4]{0,1:T(4,128)}, u32[]{:S(2)}) copy-start(s32[16,4]{0,1:T(4,128)} %param.10) | copy-start | bytes 772
